TPU v7x, 32 devices: a whole 2x2x4 slice. The times are simulated.
32 devices in a mesh: seq: 8 (over z, x), kv: 4 (over y, core).
Axes of the slice: x: 2, y: 2, z: 4, core: 2. Of those that a mesh axis runs over, the one named last changes fastest.
Arguments:
- inputs: bfloat16 [4, 1024, 2048], P(None, 'seq'), may hold values from -6 to 6
- cotangent: bfloat16 [4, 1024, 2048], P(None, 'seq'), may hold values from -6 to 6
- bucket_sizes: int32 [4, 4], replicated, may hold values from 32 to 928, as said below
- true_lengths: int32 [4, 4], replicated, may hold values from 1 to 928, as said below
- attention_gain: bfloat16 [2048], P('seq'), may hold values from 0.099609375 to 1.8984375
- feedforward_gain: bfloat16 [2048], P('seq'), may hold values from 0.099609375 to 1.8984375
- query_gain: bfloat16 [128], replicated, may hold values from 0.099609375 to 1.8984375
- key_gain: bfloat16 [128], replicated, may hold values from 0.099609375 to 1.8984375
- query_weight: bfloat16 [2048, 2048], P('seq', 'kv'), may hold values from -0.125 to 0.125
- key_matrix: bfloat16 [2048, 1024], P('seq', 'kv'), may hold values from -0.125 to 0.125
- value_matrix: bfloat16 [2048, 1024], P('seq', 'kv'), may hold values from -0.125 to 0.125
- headgate_weight: bfloat16 [2048, 16], P('seq', 'kv'), may hold values from -0.125 to 0.125
- output_weight: bfloat16 [2048, 2048], P('kv', 'seq'), may hold values from -1 to 1
- gate_weight: bfloat16 [2048, 6144], P('seq', 'kv'), may hold values from -0.125 to 0.125
- up_weight: bfloat16 [2048, 6144], P('seq', 'kv'), may hold values from -0.125 to 0.125
- down_weight: bfloat16 [6144, 2048], P('kv', 'seq'), may hold values from -0.078125 to 0.078125
Outputs:
- block_output: bfloat16 [4, 1024, 2048], P(None, 'seq')
- input_grad: bfloat16 [4, 1024, 2048], P(None, 'seq')
- attention_gain_grad: float32 [2048], P('seq')
- feedforward_gain_grad: float32 [2048], P('seq')
- query_gain_grad: float32 [128], replicated
- key_gain_grad: float32 [128], replicated
- query_weight_grad: float32 [2048, 2048], P('seq', 'kv')
- key_weight_grad: float32 [2048, 1024], P('seq', 'kv')
- value_weight_grad: float32 [2048, 1024], P('seq', 'kv')
- headgate_weight_grad: float32 [2048, 16], P('seq', 'kv')
- output_weight_grad: float32 [2048, 2048], P('kv', 'seq')
- gate_weight_grad: float32 [2048, 6144], P('seq', 'kv')
- up_weight_grad: float32 [2048, 6144], P('seq', 'kv')
- down_weight_grad: float32 [6144, 2048], P('kv', 'seq')
Inputs may be any that keep to these rules, and one draw needn't show every extreme that they name: `bucket_sizes`: each micro-batch's 4 buckets are positive multiples of 32 tokens laid end to end that fill its 1024 tokens; the second bucket starts among the first 128 tokens and ends among the last 128. `true_lengths`: each true length is at least its bucket's size minus 128 / 4 plus 1, and at most the bucket's size.
All inputs are finite; a program needn't handle non-finite values.
Results may differ from a plain program's by a relative error of at most 0.024.
Values may be sent and summed in bfloat16 or wider, within the bound.
A program may use at most 256 MiB of HBM per device.

v0:
```python
import math

import jax
import jax.numpy as jnp
from jax import lax
from jax.sharding import PartitionSpec as P

HEAD_SIZE = 128


EPS = 1e-06
ROPE_BASE = 1000000.0
MASKED = -1e30


def rms_scale(values):
    return lax.rsqrt(jnp.mean(values * values, axis=-1, keepdims=True) + EPS)


def norm_backward(grad, normal, factor):
    return factor * (grad - normal * jnp.mean(grad * normal, axis=-1, keepdims=True))


def rope_tables(positions, width):
    half = width // 2
    steps = jnp.arange(half, dtype=jnp.float32) * (2.0 / width)
    inverse = jnp.exp(-steps * math.log(ROPE_BASE))
    angles = positions.astype(jnp.float32)[:, None] * inverse[None, :]
    cosine = jnp.cos(angles)
    sine = jnp.sin(angles)
    return (jnp.concatenate([cosine, cosine], axis=-1), jnp.concatenate([sine, sine], axis=-1))


def rotate_forward(values, cosine, sine):
    half = values.shape[-1] // 2
    turned = jnp.concatenate([-values[..., half:], values[..., :half]], axis=-1)
    return values * cosine[:, None, :] + turned * sine[:, None, :]


def rotate_backward(grad, cosine, sine):
    half = grad.shape[-1] // 2
    moved = grad * sine[:, None, :]
    return grad * cosine[:, None, :] + jnp.concatenate(
        [moved[..., half:], -moved[..., :half]], axis=-1
    )


def token_layout(index, buckets, lengths):
    ends = jnp.cumsum(buckets)
    starts = ends - buckets
    member = (index[:, None] >= starts[None, :]) & (index[:, None] < ends[None, :])
    labels = jnp.arange(buckets.shape[0], dtype=jnp.int32)
    segment = jnp.sum(jnp.where(member, labels[None, :], 0), axis=1)
    position = index - jnp.sum(jnp.where(member, starts[None, :], 0), axis=1)
    limit = jnp.sum(jnp.where(member, lengths[None, :], 0), axis=1)
    return (segment, position, position < limit)


def outer_sum(left, right):
    return lax.dot_general(
        left, right, (((0,), (0,)), ((), ())), preferred_element_type=jnp.float32
    )


def times_transpose(left, weight):
    return lax.dot_general(
        left, weight, (((1,), (1,)), ((), ())), preferred_element_type=jnp.float32
    )


def block_scores(query_kg, key_block, start, row_index, row_segment, buckets, lengths, scale):
    key_index = start + jnp.arange(key_block.shape[0], dtype=jnp.int32)
    key_segment, key_position, key_valid = token_layout(key_index, buckets, lengths)
    allowed = (
        (row_segment[:, None] == key_segment[None, :])
        & (key_index[None, :] <= row_index[:, None])
        & key_valid[None, :]
    )
    raw = (
        jnp.einsum("kgtd,skd->kgts", query_kg, key_block, preferred_element_type=jnp.float32)
        * scale
    )
    return (jnp.where(allowed, raw, MASKED), allowed)


def split_blocks(keys, values, block):
    blocks = keys.shape[0] // block
    key_blocks = keys.reshape(blocks, block, keys.shape[1], keys.shape[2])
    value_blocks = values.reshape(blocks, block, values.shape[1], values.shape[2])
    starts = jnp.arange(blocks) * block
    return (key_blocks, value_blocks, starts)


def attention_forward(
    query_kg, keys, values, row_index, row_segment, buckets, lengths, block, scale
):
    key_blocks, value_blocks, starts = split_blocks(keys, values, block)

    def first_pass(carry, item):
        running_max, total = carry
        key_block, start = item
        masked, allowed = block_scores(
            query_kg, key_block, start, row_index, row_segment, buckets, lengths, scale
        )
        new_max = jnp.maximum(running_max, jnp.max(masked, axis=-1))
        total = total * jnp.exp(running_max - new_max) + jnp.sum(
            jnp.where(allowed, jnp.exp(masked - new_max[..., None]), 0.0), axis=-1
        )
        return ((new_max, total), None)

    begin = (
        jnp.full(query_kg.shape[:3], MASKED, jnp.float32),
        jnp.zeros(query_kg.shape[:3], jnp.float32),
    )
    (running_max, total), unused = lax.scan(first_pass, begin, (key_blocks, starts))
    log_total = running_max + jnp.log(total)

    def second_pass(accumulated, item):
        key_block, value_block, start = item
        masked, allowed = block_scores(
            query_kg, key_block, start, row_index, row_segment, buckets, lengths, scale
        )
        weights = jnp.where(allowed, jnp.exp(masked - log_total[..., None]), 0.0).astype(
            jnp.bfloat16
        )
        return (
            accumulated
            + jnp.einsum(
                "kgts,skd->kgtd", weights, value_block, preferred_element_type=jnp.float32
            ),
            None,
        )

    attended, unused = lax.scan(
        second_pass, jnp.zeros(query_kg.shape, jnp.float32), (key_blocks, value_blocks, starts)
    )
    return (attended, log_total)


def attention_backward(
    query_kg,
    grad_kg,
    log_total,
    delta,
    keys,
    values,
    row_index,
    row_segment,
    buckets,
    lengths,
    block,
    scale,
):
    key_blocks, value_blocks, starts = split_blocks(keys, values, block)

    def step(grad_query, item):
        key_block, value_block, start = item
        masked, allowed = block_scores(
            query_kg, key_block, start, row_index, row_segment, buckets, lengths, scale
        )
        weights = jnp.where(allowed, jnp.exp(masked - log_total[..., None]), 0.0)
        grad_weights = jnp.einsum(
            "kgtd,skd->kgts", grad_kg, value_block, preferred_element_type=jnp.float32
        )
        grad_scores = (weights * (grad_weights - delta[..., None])).astype(jnp.bfloat16)
        grad_query = grad_query + scale * jnp.einsum(
            "kgts,skd->kgtd", grad_scores, key_block, preferred_element_type=jnp.float32
        )
        grad_key = scale * jnp.einsum(
            "kgts,kgtd->skd", grad_scores, query_kg, preferred_element_type=jnp.float32
        )
        grad_value = jnp.einsum(
            "kgts,kgtd->skd",
            weights.astype(jnp.bfloat16),
            grad_kg,
            preferred_element_type=jnp.float32,
        )
        return (grad_query, (grad_key, grad_value))

    grad_query, (grad_keys, grad_values) = lax.scan(
        step, jnp.zeros(query_kg.shape, jnp.float32), (key_blocks, value_blocks, starts)
    )
    return (grad_query, grad_keys.reshape(keys.shape), grad_values.reshape(values.shape))


def local(
    inputs,
    cotangent,
    bucket_sizes,
    true_lengths,
    attention_gain,
    feedforward_gain,
    query_gain,
    key_gain,
    query_weight,
    key_matrix,
    value_matrix,
    headgate_weight,
    output_weight,
    gate_weight,
    up_weight,
    down_weight,
):
    batches, rows, width = inputs.shape
    seq_count = lax.axis_size("seq")
    block = math.gcd(rows * seq_count, 512)
    local_heads = query_weight.shape[1] // HEAD_SIZE
    local_groups = key_matrix.shape[1] // HEAD_SIZE
    group = local_heads // local_groups
    scale = HEAD_SIZE ** (-0.5)
    row_index = lax.axis_index("seq") * rows + jnp.arange(rows, dtype=jnp.int32)
    gain_query = query_gain.astype(jnp.float32)
    gain_key = key_gain.astype(jnp.float32)
    sum_attention_gain = jnp.zeros((width,), jnp.float32)
    sum_feedforward_gain = jnp.zeros((width,), jnp.float32)
    sum_query = jnp.zeros((width, query_weight.shape[1]), jnp.float32)
    sum_key = jnp.zeros((width, key_matrix.shape[1]), jnp.float32)
    sum_value = jnp.zeros((width, value_matrix.shape[1]), jnp.float32)
    sum_headgate = jnp.zeros((width, headgate_weight.shape[1]), jnp.float32)
    sum_output = jnp.zeros((output_weight.shape[0], width), jnp.float32)
    sum_gate = jnp.zeros((width, gate_weight.shape[1]), jnp.float32)
    sum_upward = jnp.zeros((width, up_weight.shape[1]), jnp.float32)
    sum_down = jnp.zeros((down_weight.shape[0], width), jnp.float32)
    sum_query_gain = jnp.zeros((HEAD_SIZE,), jnp.float32)
    sum_key_gain = jnp.zeros((HEAD_SIZE,), jnp.float32)
    results = []
    input_grads = []
    for batch in range(batches):
        gathered = (
            lax.all_gather(attention_gain, "seq", axis=0, tiled=True),
            lax.all_gather(feedforward_gain, "seq", axis=0, tiled=True),
            lax.all_gather(query_weight, "seq", axis=0, tiled=True),
            lax.all_gather(key_matrix, "seq", axis=0, tiled=True),
            lax.all_gather(value_matrix, "seq", axis=0, tiled=True),
            lax.all_gather(headgate_weight, "seq", axis=0, tiled=True),
            lax.all_gather(output_weight, "seq", axis=1, tiled=True),
            lax.all_gather(gate_weight, "seq", axis=0, tiled=True),
            lax.all_gather(up_weight, "seq", axis=0, tiled=True),
            lax.all_gather(down_weight, "seq", axis=1, tiled=True),
        )
        (
            gain_a,
            gain_f,
            w_query,
            key_projection_weight,
            value_projection_weight,
            w_head,
            w_output,
            w_gate,
            w_up,
            w_down,
        ) = gathered
        gain_a = gain_a.astype(jnp.float32)
        gain_f = gain_f.astype(jnp.float32)
        buckets = bucket_sizes[batch]
        lengths = true_lengths[batch]
        row_segment, row_position, row_valid = token_layout(row_index, buckets, lengths)
        cosine, sine = rope_tables(row_position, HEAD_SIZE)
        current = inputs[batch].astype(jnp.float32)
        scale_a = rms_scale(current)
        normal_a = current * scale_a
        normed_input = (normal_a * gain_a).astype(jnp.bfloat16)
        query_proj = jnp.dot(normed_input, w_query, preferred_element_type=jnp.float32).reshape(
            rows, local_heads, HEAD_SIZE
        )
        key_proj = jnp.dot(
            normed_input, key_projection_weight, preferred_element_type=jnp.float32
        ).reshape(rows, local_groups, HEAD_SIZE)
        value_proj = jnp.dot(
            normed_input, value_projection_weight, preferred_element_type=jnp.float32
        )
        query_scale = rms_scale(query_proj)
        query_normal = query_proj * query_scale
        key_scale = rms_scale(key_proj)
        key_normal = key_proj * key_scale
        query_rot = rotate_forward(query_normal * gain_query, cosine, sine).astype(jnp.bfloat16)
        key_rot = rotate_forward(key_normal * gain_key, cosine, sine).astype(jnp.bfloat16)
        value_low = value_proj.astype(jnp.bfloat16).reshape(rows, local_groups, HEAD_SIZE)
        logits = jnp.dot(normed_input, w_head, preferred_element_type=jnp.float32)
        gate = jax.nn.sigmoid(logits)
        all_keys, all_values = (
            lax.all_gather(key_rot, "seq", axis=0, tiled=True),
            lax.all_gather(value_low, "seq", axis=0, tiled=True),
        )
        query_kg = query_rot.reshape(rows, local_groups, group, HEAD_SIZE).transpose(1, 2, 0, 3)
        attended_kg, log_total = attention_forward(
            query_kg, all_keys, all_values, row_index, row_segment, buckets, lengths, block, scale
        )
        attended = attended_kg.transpose(2, 0, 1, 3).reshape(rows, local_heads, HEAD_SIZE)
        mixed = (
            (attended * gate[:, :, None])
            .astype(jnp.bfloat16)
            .reshape(rows, local_heads * HEAD_SIZE)
        )
        hidden = current + lax.psum(
            jnp.dot(mixed, w_output, preferred_element_type=jnp.float32).astype(jnp.bfloat16), "kv"
        ).astype(jnp.float32)
        scale_f = rms_scale(hidden)
        normal_f = hidden * scale_f
        inner = (normal_f * gain_f).astype(jnp.bfloat16)
        gated = jnp.dot(inner, w_gate, preferred_element_type=jnp.float32)
        upward = jnp.dot(inner, w_up, preferred_element_type=jnp.float32)
        sigma = jax.nn.sigmoid(gated)
        swish = gated * sigma
        product = (swish * upward).astype(jnp.bfloat16)
        output = hidden + lax.psum(
            jnp.dot(product, w_down, preferred_element_type=jnp.float32).astype(jnp.bfloat16), "kv"
        ).astype(jnp.float32)
        results.append(output.astype(jnp.bfloat16))
        grad_out = cotangent[batch].astype(jnp.float32)
        grad_low = grad_out.astype(jnp.bfloat16)
        sum_down = sum_down + outer_sum(product, grad_low)
        grad_product = times_transpose(grad_low, w_down)
        grad_gated = (grad_product * upward * sigma * (1.0 + gated * (1.0 - sigma))).astype(
            jnp.bfloat16
        )
        grad_upward = (grad_product * swish).astype(jnp.bfloat16)
        sum_gate = sum_gate + outer_sum(inner, grad_gated)
        sum_upward = sum_upward + outer_sum(inner, grad_upward)
        grad_inner = lax.psum(
            (times_transpose(grad_gated, w_gate) + times_transpose(grad_upward, w_up)).astype(
                jnp.bfloat16
            ),
            "kv",
        ).astype(jnp.float32)
        sum_feedforward_gain = sum_feedforward_gain + jnp.sum(grad_inner * normal_f, axis=0)
        grad_hidden = grad_out + norm_backward(grad_inner * gain_f, normal_f, scale_f)
        grad_branch = grad_hidden.astype(jnp.bfloat16)
        sum_output = sum_output + outer_sum(mixed, grad_branch)
        grad_mixed = times_transpose(grad_branch, w_output).reshape(rows, local_heads, HEAD_SIZE)
        grad_heads = (grad_mixed * gate[:, :, None]).astype(jnp.bfloat16)
        grad_logits = (jnp.sum(grad_mixed * attended, axis=-1) * gate * (1.0 - gate)).astype(
            jnp.bfloat16
        )
        back_keys = lax.all_gather(key_rot, "seq", axis=0, tiled=True)
        back_values = lax.all_gather(value_low, "seq", axis=0, tiled=True)
        grad_kg = grad_heads.reshape(rows, local_groups, group, HEAD_SIZE).transpose(1, 2, 0, 3)
        delta = jnp.sum(grad_kg.astype(jnp.float32) * attended_kg, axis=-1)
        grad_query_kg, grad_keys, grad_values = attention_backward(
            query_kg,
            grad_kg,
            log_total,
            delta,
            back_keys,
            back_values,
            row_index,
            row_segment,
            buckets,
            lengths,
            block,
            scale,
        )
        local_keys, local_values = (
            lax.psum_scatter(
                grad_keys.astype(jnp.bfloat16), "seq", scatter_dimension=0, tiled=True
            ).astype(jnp.float32),
            lax.psum_scatter(
                grad_values.astype(jnp.bfloat16), "seq", scatter_dimension=0, tiled=True
            ).astype(jnp.float32),
        )
        grad_query_rot = grad_query_kg.transpose(2, 0, 1, 3).reshape(rows, local_heads, HEAD_SIZE)
        grad_query_norm = rotate_backward(grad_query_rot, cosine, sine)
        sum_query_gain = sum_query_gain + jnp.sum(grad_query_norm * query_normal, axis=(0, 1))
        grad_query = (
            norm_backward(grad_query_norm * gain_query, query_normal, query_scale)
            .astype(jnp.bfloat16)
            .reshape(rows, local_heads * HEAD_SIZE)
        )
        grad_key_norm = rotate_backward(local_keys, cosine, sine)
        sum_key_gain = sum_key_gain + jnp.sum(grad_key_norm * key_normal, axis=(0, 1))
        grad_key = (
            norm_backward(grad_key_norm * gain_key, key_normal, key_scale)
            .astype(jnp.bfloat16)
            .reshape(rows, local_groups * HEAD_SIZE)
        )
        grad_value = local_values.astype(jnp.bfloat16).reshape(rows, local_groups * HEAD_SIZE)
        sum_query = sum_query + outer_sum(normed_input, grad_query)
        sum_key = sum_key + outer_sum(normed_input, grad_key)
        sum_value = sum_value + outer_sum(normed_input, grad_value)
        sum_headgate = sum_headgate + outer_sum(normed_input, grad_logits)
        grad_partial = (
            times_transpose(grad_query, w_query)
            + times_transpose(grad_key, key_projection_weight)
            + times_transpose(grad_value, value_projection_weight)
            + times_transpose(grad_logits, w_head)
        )
        grad_normed = lax.psum(grad_partial.astype(jnp.bfloat16), "kv").astype(jnp.float32)
        sum_attention_gain = sum_attention_gain + jnp.sum(grad_normed * normal_a, axis=0)
        grad_input = grad_hidden + norm_backward(grad_normed * gain_a, normal_a, scale_a)
        input_grads.append(grad_input.astype(jnp.bfloat16))
    (
        attention_total,
        feedforward_total,
        query_total,
        key_total,
        value_total,
        headgate_total,
        output_total,
        gate_total,
        upward_total,
        down_total,
    ) = (
        lax.psum_scatter(
            sum_attention_gain.astype(jnp.bfloat16), "seq", scatter_dimension=0, tiled=True
        ).astype(jnp.float32),
        lax.psum_scatter(
            sum_feedforward_gain.astype(jnp.bfloat16), "seq", scatter_dimension=0, tiled=True
        ).astype(jnp.float32),
        lax.psum_scatter(
            sum_query.astype(jnp.bfloat16), "seq", scatter_dimension=0, tiled=True
        ).astype(jnp.float32),
        lax.psum_scatter(
            sum_key.astype(jnp.bfloat16), "seq", scatter_dimension=0, tiled=True
        ).astype(jnp.float32),
        lax.psum_scatter(
            sum_value.astype(jnp.bfloat16), "seq", scatter_dimension=0, tiled=True
        ).astype(jnp.float32),
        lax.psum_scatter(
            sum_headgate.astype(jnp.bfloat16), "seq", scatter_dimension=0, tiled=True
        ).astype(jnp.float32),
        lax.psum_scatter(
            sum_output.astype(jnp.bfloat16), "seq", scatter_dimension=1, tiled=True
        ).astype(jnp.float32),
        lax.psum_scatter(
            sum_gate.astype(jnp.bfloat16), "seq", scatter_dimension=0, tiled=True
        ).astype(jnp.float32),
        lax.psum_scatter(
            sum_upward.astype(jnp.bfloat16), "seq", scatter_dimension=0, tiled=True
        ).astype(jnp.float32),
        lax.psum_scatter(
            sum_down.astype(jnp.bfloat16), "seq", scatter_dimension=1, tiled=True
        ).astype(jnp.float32),
    )
    query_gain_total, key_gain_total = lax.psum((sum_query_gain, sum_key_gain), ("seq", "kv"))
    return (
        jnp.stack(results, axis=0),
        jnp.stack(input_grads, axis=0),
        attention_total,
        feedforward_total,
        query_gain_total,
        key_gain_total,
        query_total,
        key_total,
        value_total,
        headgate_total,
        output_total,
        gate_total,
        upward_total,
        down_total,
    )


def solution(mesh):
    in_specs = (
        P(None, "seq", None),
        P(None, "seq", None),
        P(),
        P(),
        P("seq"),
        P("seq"),
        P(),
        P(),
        P("seq", "kv"),
        P("seq", "kv"),
        P("seq", "kv"),
        P("seq", "kv"),
        P("kv", "seq"),
        P("seq", "kv"),
        P("seq", "kv"),
        P("kv", "seq"),
    )
    out_specs = (
        P(None, "seq", None),
        P(None, "seq", None),
        P("seq"),
        P("seq"),
        P(),
        P(),
        P("seq", "kv"),
        P("seq", "kv"),
        P("seq", "kv"),
        P("seq", "kv"),
        P("kv", "seq"),
        P("seq", "kv"),
        P("seq", "kv"),
        P("kv", "seq"),
    )
    return jax.shard_map(local, mesh=mesh, in_specs=in_specs, out_specs=out_specs, check_vma=False)
```

profile of v0, /device:TPU:0, one launch (start us, length us, event | category | flops | bytes accessed | tf_op | source)
XLA Modules:
  0.0 2090.8 jit_solution(5918234405296866905)
XLA Ops:
  45.5 26.2 %all_gather.42 = bf16[2048,4]{0,1:T(4,128)(2,1)S(1)} all-gather(bf16[256,4]{0,1:T(4,128)(2,1)} %param.51), channel_id=1, replica_groups=mesh['seq'=8,'kv'=4] {'seq'}, dimensions={0}, use_global_device_ids=true | all-gather | bytes 18432 | tf_op jit(solution)/shard_map/all_gather | solution.py:235
  78.4 28.5 %all_gather.50 = bf16[1024,2,128]{0,2,1:T(8,128)(2,1)S(1)} all-gather(bf16[128,2,128]{0,2,1:T(8,128)(2,1)S(1)} %fusion.483), channel_id=1, replica_groups=mesh['seq'=8,'kv'=4] {'seq'}, dimensions={0}, use_global_device_ids=true | all-gather | bytes 589824 | tf_op jit(solution)/shard_map/all_gather | solution.py:282
  110.0 32.4 %all_gather.51 = bf16[1024,2,128]{2,0,1:T(8,128)(2,1)S(1)} all-gather(bf16[128,2,128]{2,0,1:T(8,128)(2,1)S(1)} %bitcast.1495), channel_id=1, replica_groups=mesh['seq'=8,'kv'=4] {'seq'}, dimensions={0}, use_global_device_ids=true | all-gather | bytes 589824 | tf_op jit(solution)/shard_map/all_gather | solution.py:283
  247.6 35.7 %all_gather.52 = bf16[1024,2,128]{0,2,1:T(8,128)(2,1)} all-gather(bf16[128,2,128]{0,2,1:T(8,128)(2,1)S(1)} %fusion.485), channel_id=1, replica_groups=mesh['seq'=8,'kv'=4] {'seq'}, dimensions={0}, use_global_device_ids=true | all-gather | bytes 589824 | tf_op jit(solution)/shard_map/all_gather | solution.py:282
  310.2 32.9 %all_gather.53 = bf16[1024,2,128]{2,0,1:T(8,128)(2,1)S(1)} all-gather(bf16[128,2,128]{2,0,1:T(8,128)(2,1)S(1)} %bitcast.1496), channel_id=1, replica_groups=mesh['seq'=8,'kv'=4] {'seq'}, dimensions={0}, use_global_device_ids=true | all-gather | bytes 589824 | tf_op jit(solution)/shard_map/all_gather | solution.py:283
  355.3 29.6 %all_gather.38 = bf16[1024,2,128]{0,2,1:T(8,128)(2,1)} all-gather(bf16[128,2,128]{0,2,1:T(8,128)(2,1)S(1)} %fusion.479), channel_id=1, replica_groups=mesh['seq'=8,'kv'=4] {'seq'}, dimensions={0}, use_global_device_ids=true | all-gather | bytes 589824 | tf_op jit(solution)/shard_map/all_gather | solution.py:282
  412.8 37.3 %all_gather.41 = bf16[1024,2,128]{2,0,1:T(8,128)(2,1)S(1)} all-gather(bf16[128,2,128]{2,0,1:T(8,128)(2,1)S(1)} %bitcast.1497), channel_id=1, replica_groups=mesh['seq'=8,'kv'=4] {'seq'}, dimensions={0}, use_global_device_ids=true | all-gather | bytes 589824 | tf_op jit(solution)/shard_map/all_gather | solution.py:283
  464.3 30.4 %all_gather.48 = bf16[1024,2,128]{0,2,1:T(8,128)(2,1)} all-gather(bf16[128,2,128]{0,2,1:T(8,128)(2,1)S(1)} %fusion.481), channel_id=1, replica_groups=mesh['seq'=8,'kv'=4] {'seq'}, dimensions={0}, use_global_device_ids=true | all-gather | bytes 589824 | tf_op jit(solution)/shard_map/all_gather | solution.py:282
  503.7 32.9 %all_gather.49 = bf16[1024,2,128]{2,0,1:T(8,128)(2,1)S(1)} all-gather(bf16[128,2,128]{2,0,1:T(8,128)(2,1)S(1)} %bitcast.1498), channel_id=1, replica_groups=mesh['seq'=8,'kv'=4] {'seq'}, dimensions={0}, use_global_device_ids=true | all-gather | bytes 589824 | tf_op jit(solution)/shard_map/all_gather | solution.py:283
  602.0 47.9 %all-reduce.18.cloned.1.call-done = (bf16[128,2048]{1,0:T(8,128)(2,1)}, bf16[128,2048]{1,0:T(8,128)(2,1)}, bf16[128,2048]{1,0:T(8,128)(2,1)}, bf16[128,2048]{1,0:T(8,128)(2,1)}) async-done(((bf16[128,2048]{1,0:T(8,128)(2,1)}, bf16[128,2048]{1,0:T(8,128)(2,1)}, bf16[128,2048]{1,0:T(8,128)(2,1)}, bf16[128,2048]{1,0:T(8,128)(2,1)}), (bf16[128,2048]{1,0:T(8,128)(2,1)}, bf16[128,2048]{1,0:T(8,128)(2,1)}, ...) | async-done | bytes 2097168 | tf_op jit(solution)/shard_map/psum | solution.py:295
  695.7 38.6 %all-reduce.16.cloned.1.call-done = (bf16[128,2048]{1,0:T(8,128)(2,1)}, bf16[128,2048]{1,0:T(8,128)(2,1)}, bf16[128,2048]{1,0:T(8,128)(2,1)}) async-done(((bf16[128,2048]{1,0:T(8,128)(2,1)}, bf16[128,2048]{1,0:T(8,128)(2,1)}, bf16[128,2048]{1,0:T(8,128)(2,1)}), (bf16[128,2048]{1,0:T(8,128)(2,1)}, bf16[128,2048]{1,0:T(8,128)(2,1)}, bf16[128,2048]{1,0:T(8,128)(2,1)})) %all-reduce.16.cloned.1.call-update) | async-done | bytes 1572880 | tf_op jit(solution)/shard_map/psum | solution.py:320
  921.2 44.2 %reduce-scatter.55.cloned.1.call-done = bf16[128,256]{1,0:T(8,128)(2,1)} async-done(((bf16[1024,256]{1,0:T(8,128)(2,1)}), bf16[128,256]{1,0:T(8,128)(2,1)}) %reduce-scatter.55.cloned.1.call-update) | async-done | bytes 65552
  967.1 63.1 %reduce-scatter.49.cloned.1.call-done = bf16[128,256]{1,0:T(8,128)(2,1)} async-done(((bf16[1024,256]{1,0:T(8,128)(2,1)}), bf16[128,256]{1,0:T(8,128)(2,1)}) %reduce-scatter.49.cloned.1.call-update) | async-done | bytes 65552
  1042.5 52.3 %reduce-scatter.33.cloned.1.call-done = bf16[128,2,128]{2,0,1:T(8,128)(2,1)} async-done(((bf16[1024,2,128]{2,0,1:T(8,128)(2,1)}), bf16[128,2,128]{2,0,1:T(8,128)(2,1)}) %reduce-scatter.33.cloned.1.call-update) | async-done | bytes 65552 | tf_op jit(solution)/shard_map/reduce_scatter | solution.py:357
  1095.7 63.2 %reduce-scatter.29.cloned.1.call-done = bf16[128,2,128]{2,0,1:T(8,128)(2,1)} async-done(((bf16[1024,2,128]{2,0,1:T(8,128)(2,1)}), bf16[128,2,128]{2,0,1:T(8,128)(2,1)}) %reduce-scatter.29.cloned.1.call-update) | async-done | bytes 65552 | tf_op jit(solution)/shard_map/reduce_scatter | solution.py:357
  1159.9 63.6 %reduce-scatter.27.cloned.1.call-done = bf16[128,2,128]{2,0,1:T(8,128)(2,1)} async-done(((bf16[1024,2,128]{2,0,1:T(8,128)(2,1)}), bf16[128,2,128]{2,0,1:T(8,128)(2,1)}) %reduce-scatter.27.cloned.1.call-update) | async-done | bytes 65552 | tf_op jit(solution)/shard_map/reduce_scatter | solution.py:357
  1224.4 63.1 %reduce-scatter.31.cloned.1.call-done = bf16[128,2,128]{2,0,1:T(8,128)(2,1)} async-done(((bf16[1024,2,128]{2,0,1:T(8,128)(2,1)}), bf16[128,2,128]{2,0,1:T(8,128)(2,1)}) %reduce-scatter.31.cloned.1.call-update) | async-done | bytes 65552 | tf_op jit(solution)/shard_map/reduce_scatter | solution.py:357
  1434.3 40.3 %all-reduce.2 = (f32[128]{0:T(128)}, f32[128]{0:T(128)}) all-reduce(f32[128]{0:T(128)S(1)} %add_add_fusion.1, f32[128]{0:T(128)S(1)} %add_add_fusion), channel_id=1, replica_groups=mesh['seq'=8,'kv'=4] {'seq','kv'}, use_global_device_ids=true, to_apply=%region_158.159 | all-reduce | flops 256 | bytes 2048 | tf_op jit(solution)/shard_map/psum | solution.py:434
  1486.5 88.2 %all-reduce.14.cloned.1.call-done = (bf16[128,2048]{1,0:T(8,128)(2,1)}, bf16[128,2048]{1,0:T(8,128)(2,1)}, bf16[128,2048]{1,0:T(8,128)(2,1)}, bf16[128,2048]{1,0...) async-done(((bf16[128,2048]{1,0:T(8,128)(2,1)}, bf16[128,2048]{1,0:T(8,128)(2,1)}, ...) | async-done | bytes 4194320 | tf_op jit(solution)/shard_map/psum | solution.py:306
  1609.1 38.0 %reduce-scatter.35.cloned.1.call-done = bf16[256,512]{1,0:T(8,128)(2,1)} async-done(((bf16[2048,512]{1,0:T(8,128)(2,1)}), bf16[256,512]{1,0:T(8,128)(2,1)}) %reduce-scatter.35.cloned.1.call-update) | async-done | bytes 262160 | tf_op jit(solution)/shard_map/reduce_scatter | solution.py:409
  1648.9 69.1 %reduce-scatter.41.cloned.1.call-done = bf16[512,256]{1,0:T(8,128)(2,1)} async-done(((bf16[512,2048]{1,0:T(8,128)(2,1)}), bf16[512,256]{1,0:T(8,128)(2,1)}) %reduce-scatter.41.cloned.1.call-update) | async-done | bytes 262160 | tf_op jit(solution)/shard_map/reduce_scatter | solution.py:421
  1719.7 119.2 %reduce-scatter.43.cloned.1.call-done = bf16[256,1536]{1,0:T(8,128)(2,1)} async-done(((bf16[2048,1536]{1,0:T(8,128)(2,1)}), bf16[256,1536]{1,0:T(8,128)(2,1)}) %reduce-scatter.43.cloned.1.call-update) | async-done | bytes 786448 | tf_op jit(solution)/shard_map/reduce_scatter | solution.py:424
  1841.4 118.5 %reduce-scatter.45.cloned.1.call-done = bf16[256,1536]{1,0:T(8,128)(2,1)} async-done(((bf16[2048,1536]{1,0:T(8,128)(2,1)}), bf16[256,1536]{1,0:T(8,128)(2,1)}) %reduce-scatter.45.cloned.1.call-update) | async-done | bytes 786448 | tf_op jit(solution)/shard_map/reduce_scatter | solution.py:427
  1962.4 119.0 %reduce-scatter.47.cloned.1.call-done = bf16[1536,256]{1,0:T(8,128)(2,1)} async-done(((bf16[1536,2048]{1,0:T(8,128)(2,1)}), bf16[1536,256]{1,0:T(8,128)(2,1)}) %reduce-scatter.47.cloned.1.call-update) | async-done | bytes 786448 | tf_op jit(solution)/shard_map/reduce_scatter | solution.py:430
  (1280 shorter events, 957.5 us)
Async XLA Ops:
  8.7 141.6 %all-gather.12.cloned.1.call-start = ((), (), s32[]{:S(2)}) async-start(), calls=%async_computation.17 | async-start | bytes 2359296 | tf_op jit(solution)/shard_map/all_gather | solution.py:232
  9.4 193.4 %all-gather.16.cloned.1.call-start = ((), (), s32[]{:S(2)}) async-start(), calls=%async_computation.19 | async-start | bytes 2359296 | tf_op jit(solution)/shard_map/all_gather | solution.py:236
  10.0 227.2 %all-reduce.12.cloned.1.call-start = ((), (), s32[]{:S(2)}) async-start(), calls=%async_computation.23 | async-start | bytes 1048576 | tf_op jit(solution)/shard_map/psum | solution.py:295
  205.7 373.7 %all-gather.18.cloned.1.call-start = ((), (), s32[]{:S(2)}) async-start(), calls=%async_computation.20 | async-start | bytes 7077888 | tf_op jit(solution)/shard_map/all_gather | solution.py:237
  206.3 377.1 %all-gather.22.cloned.1.call-start = ((), (), s32[]{:S(2)}) async-start(), calls=%async_computation.22 | async-start | bytes 7077888 | tf_op jit(solution)/shard_map/all_gather | solution.py:239
  207.0 381.5 %all-gather.20.cloned.1.call-start = ((), (), s32[]{:S(2)}) async-start(), calls=%async_computation.21 | async-start | bytes 7077888 | tf_op jit(solution)/shard_map/all_gather | solution.py:238
  207.8 442.2 %all-reduce.18.cloned.1.call-start = ((), (), s32[]{:S(2)}) async-start(), calls=%async_computation.42 | async-start | bytes 4194304 | tf_op jit(solution)/shard_map/psum | solution.py:295
  690.8 226.1 %reduce-scatter.53.cloned.1.call-start = ((), (), s32[]{:S(2)}) async-start(), calls=%async_computation.37 | async-start | bytes 589824
  774.4 143.6 %reduce-scatter.51.cloned.1.call-start = ((), (), s32[]{:S(2)}) async-start(), calls=%async_computation.36 | async-start | bytes 589824
  811.9 153.5 %reduce-scatter.55.cloned.1.call-start = ((), (), s32[]{:S(2)}) async-start(), calls=%async_computation.38 | async-start | bytes 589824
  839.6 190.6 %reduce-scatter.49.cloned.1.call-start = ((), (), s32[]{:S(2)}) async-start(), calls=%async_computation.35 | async-start | bytes 589824
  865.1 229.6 %reduce-scatter.33.cloned.1.call-start = ((), (), s32[]{:S(2)}) async-start(), calls=%async_computation.27 | async-start | bytes 589824 | tf_op jit(solution)/shard_map/reduce_scatter | solution.py:357
  886.8 272.1 %reduce-scatter.29.cloned.1.call-start = ((), (), s32[]{:S(2)}) async-start(), calls=%async_computation.25 | async-start | bytes 589824 | tf_op jit(solution)/shard_map/reduce_scatter | solution.py:357
  894.1 329.4 %reduce-scatter.27.cloned.1.call-start = ((), (), s32[]{:S(2)}) async-start(), calls=%async_computation.24 | async-start | bytes 589824 | tf_op jit(solution)/shard_map/reduce_scatter | solution.py:357
  897.0 390.5 %reduce-scatter.31.cloned.1.call-start = ((), (), s32[]{:S(2)}) async-start(), calls=%async_computation.26 | async-start | bytes 589824 | tf_op jit(solution)/shard_map/reduce_scatter | solution.py:357
  907.1 525.7 %reduce-scatter.57.cloned.1.call-start = ((), (), s32[]{:S(2)}) async-start(), calls=%async_computation.39 | async-start | bytes 589824
  914.5 560.1 %reduce-scatter.37.cloned.1.call-start = ((), (), s32[]{:S(2)}) async-start(), calls=%async_computation.29 | async-start | bytes 1179648 | tf_op jit(solution)/shard_map/reduce_scatter | solution.py:412
  1039.6 445.2 %reduce-scatter.39.cloned.1.call-start = ((), (), s32[]{:S(2)}) async-start(), calls=%async_computation.30 | async-start | bytes 1179648 | tf_op jit(solution)/shard_map/reduce_scatter | solution.py:415
  1296.9 277.8 %all-reduce.14.cloned.1.call-start = ((), (), s32[]{:S(2)}) async-start(), calls=%async_computation.40 | async-start | bytes 8388608 | tf_op jit(solution)/shard_map/psum | solution.py:306
  1307.9 339.1 %reduce-scatter.35.cloned.1.call-start = ((), (), s32[]{:S(2)}) async-start(), calls=%async_computation.28 | async-start | bytes 2359296 | tf_op jit(solution)/shard_map/reduce_scatter | solution.py:409
  1312.7 405.2 %reduce-scatter.41.cloned.1.call-start = ((), (), s32[]{:S(2)}) async-start(), calls=%async_computation.31 | async-start | bytes 2359296 | tf_op jit(solution)/shard_map/reduce_scatter | solution.py:421
  1320.2 518.7 %reduce-scatter.43.cloned.1.call-start = ((), (), s32[]{:S(2)}) async-start(), calls=%async_computation.32 | async-start | bytes 7077888 | tf_op jit(solution)/shard_map/reduce_scatter | solution.py:424
  1356.5 603.4 %reduce-scatter.45.cloned.1.call-start = ((), (), s32[]{:S(2)}) async-start(), calls=%async_computation.33 | async-start | bytes 7077888 | tf_op jit(solution)/shard_map/reduce_scatter | solution.py:427
  1393.6 687.8 %reduce-scatter.47.cloned.1.call-start = ((), (), s32[]{:S(2)}) async-start(), calls=%async_computation.34 | async-start | bytes 7077888 | tf_op jit(solution)/shard_map/reduce_scatter | solution.py:430
  (317 other events, 4497.2 us)
Sparse Core Ops, SparseCore 0:
  99.1 51.1 all-gather.11
  152.2 50.5 all-gather.15
  239.2 117.5 all-gather.17
  358.9 111.9 all-gather.21
  473.0 107.6 all-gather.19
  601.7 48.1 all-reduce.17
  690.9 43.3 all-reduce.15
  774.5 61.9 reduce-scatter.52
  839.7 60.9 reduce-scatter.50
  904.4 60.9 reduce-scatter.54
  969.2 60.8 reduce-scatter.48
  1033.7 61.0 reduce-scatter.32
  1098.0 60.9 reduce-scatter.28
  1162.5 60.9 reduce-scatter.26
  1226.7 60.8 reduce-scatter.30
  1291.3 61.0 reduce-scatter.56
  1355.6 62.4 reduce-scatter.36
  1422.4 62.3 reduce-scatter.38
  1488.8 85.8 all-reduce.13
  1578.6 68.3 reduce-scatter.34
  1650.9 67.0 reduce-scatter.40
  1722.0 116.9 reduce-scatter.42
  1842.8 117.0 reduce-scatter.44
  1963.8 117.5 reduce-scatter.46
  (3 shorter events, 115.8 us)
where the time goes:
time: 2100 us; the launch traced here: 2090 us
  waiting for transfers between devices  1030 us (49%)
  blocking collectives  389 us (19%)
  matrix products  323 us (15%)
  other arithmetic  184 us (9%)
  local copies, waits for them, and re-layouts  138 us (7%)
    reduce_scatter x4, waiting for transfers between devices, local(): lax.psum_scatter(grad_values.astype(jnp.bfloat16), 'seq', scatter_dimensi...  242 us
    all_gather x4, blocking collectives, local(): lax.all_gather(value_low, 'seq', axis=0, tiled=True)  136 us
    dot_general x32, matrix products, outer_sum(): lax.dot_general(left, right, (((0,), (0,)), ((), ())), preferred_element_...  128 us
    all_gather x4, blocking collectives, local(): lax.all_gather(key_rot, 'seq', axis=0, tiled=True)  124 us
    reduce_scatter x1, waiting for transfers between devices, local(): lax.psum_scatter(sum_gate.astype(jnp.bfloat16), 'seq', scatter_dimension=...  119 us
    reduce_scatter x1, waiting for transfers between devices, local(): lax.psum_scatter(sum_down.astype(jnp.bfloat16), 'seq', scatter_dimension=...  119 us
    reduce_scatter x1, waiting for transfers between devices, local(): lax.psum_scatter(sum_upward.astype(jnp.bfloat16), 'seq', scatter_dimensio...  119 us
    unnamed x32, waiting for transfers between devices  112 us
  transfers between devices with their start and end apart: 27, of which 18 were waited for; matrix products, arithmetic and copies ran while one was open for 25% of the time, Pallas kernels for 0%

commit v1 on v0

--- a/solution.py
+++ b/solution.py
@@ -1,8 +1,11 @@
+import functools
 import math
 
 import jax
 import jax.numpy as jnp
 from jax import lax
+from jax.experimental import pallas as pl
+from jax.experimental.pallas import tpu as pltpu
 from jax.sharding import PartitionSpec as P
 
 HEAD_SIZE = 128
@@ -450,7 +453,1002 @@
     )
 
 
+BF = jnp.bfloat16
+F32 = jnp.float32
+ANY = pl.BlockSpec(memory_space=pl.ANY)
+VM = pl.BlockSpec(memory_space=pltpu.VMEM)
+DMA = pltpu.SemaphoreType.DMA
+
+
+def place():
+    s = lax.axis_index("seq")
+    k = lax.axis_index("kv")
+    return (lax.div(s, 2), lax.rem(s, 2), lax.div(k, 2), lax.rem(k, 2))
+
+
+def device(l, x, y, c):
+    return (l * 2 + x, y * 2 + c)
+
+
+def remote(src, dst, send, recv, target):
+    return pltpu.make_async_remote_copy(
+        src_ref=src,
+        dst_ref=dst,
+        send_sem=send,
+        recv_sem=recv,
+        device_id=target,
+        device_id_type=pl.DeviceIdType.MESH,
+    )
+
+
+def greet(partners):
+    barrier = pltpu.get_barrier_semaphore()
+    count = 0
+    for target, there in partners:
+
+        def call(target=target):
+            pl.semaphore_signal(
+                barrier, inc=1, device_id=target, device_id_type=pl.DeviceIdType.MESH
+            )
+
+        if there is None:
+            call()
+            count = count + 1
+        else:
+            pl.when(there)(call)
+            count = count + jnp.where(there, 1, 0)
+    pl.semaphore_wait(barrier, count)
+
+
+class Line:
+    def __init__(self, length, g, ag_send, ag_recv, land=None, rs_send=None, rs_recv=None):
+        self.n = length
+        self.g, self.ag_send, self.ag_recv = g, ag_send, ag_recv
+        self.land, self.rs_send, self.rs_recv = land, rs_send, rs_recv
+        self.l, self.x, self.y, self.c = place()
+
+    def partners(self):
+        l, x, y, c = self.l, self.x, self.y, self.c
+        return [
+            (device(l - 1, x, y, c), l >= 1),
+            (device(l + 1, x, y, c), l <= self.n - 2),
+        ]
+
+    def block(self, item, b):
+        return self.g.at[item, pl.ds(2 * b, 2)]
+
+    def _ag(self, item, way, b):
+        step = -1 if way == 0 else 1
+        return remote(
+            self.block(item, b),
+            self.block(item, b),
+            self.ag_send.at[item, way, b],
+            self.ag_recv.at[item, b],
+            device(self.l + step, self.x, self.y, self.c),
+        )
+
+    def ag_start(self, item):
+        l = self.l
+        pl.when(l >= 1)(lambda: self._ag(item, 0, l).start())
+        pl.when(l <= self.n - 2)(lambda: self._ag(item, 1, l).start())
+
+    def ag_step(self, item, t):
+        l, n = self.l, self.n
+
+        @pl.when(l + t <= n - 1)
+        def _():
+            self._ag(item, 0, l + t).wait_recv()
+            pl.when(l >= 1)(lambda: self._ag(item, 0, l + t).start())
+
+        @pl.when(l - t >= 0)
+        def _():
+            self._ag(item, 1, l - t).wait_recv()
+            pl.when(l <= n - 2)(lambda: self._ag(item, 1, l - t).start())
+
+    def ag_end(self, item):
+        l, n = self.l, self.n
+        for b in range(n):
+            pl.when((l >= 1) & (l <= b))(lambda b=b: self._ag(item, 0, b).wait_send())
+            pl.when((l <= n - 2) & (l >= b))(lambda b=b: self._ag(item, 1, b).wait_send())
+
+    def _slot(self, item, slot):
+        return self.land.at[item, pl.ds(2 * slot, 2)]
+
+    def _rs(self, item, way, o):
+        if way == 0:
+            target = self.l - 1
+            slot = jnp.where(target == o, self.n, o)
+        else:
+            target = self.l + 1
+            slot = o
+        return remote(
+            self.block(item, o),
+            self._slot(item, slot),
+            self.rs_send.at[item, way, o],
+            self.rs_recv.at[item, slot],
+            device(target, self.x, self.y, self.c),
+        )
+
+    def _take(self, item, o, slot):
+        here = self._slot(item, slot)
+        pltpu.make_async_copy(here, here, self.rs_recv.at[item, slot]).wait()
+        for h in range(2):
+            total = self.g[item, 2 * o + h].astype(F32) + self.land[item, 2 * slot + h].astype(F32)
+            self.g[item, 2 * o + h] = total.astype(BF)
+
+    def rs_step(self, item, q):
+        l, n = self.l, self.n
+        right, left = n - q, q - 1
+
+        @pl.when(l < right)
+        def _():
+            pl.when(l >= 1)(lambda: self._take(item, right, right))
+            self._rs(item, 1, right).start()
+
+        @pl.when(l > left)
+        def _():
+            pl.when(l <= n - 2)(lambda: self._take(item, left, left))
+            self._rs(item, 0, left).start()
+
+    def rs_final(self, item):
+        l, n = self.l, self.n
+        pl.when(l >= 1)(lambda: self._take(item, l, l))
+        pl.when(l <= n - 2)(lambda: self._take(item, l, n))
+
+    def rs_end(self, item):
+        l, n = self.l, self.n
+        for o in range(n):
+            pl.when(l < o)(lambda o=o: self._rs(item, 1, o).wait_send())
+            pl.when(l > o)(lambda o=o: self._rs(item, 0, o).wait_send())
+
+
+def each(count, body):
+    def step(i, unused):
+        body(i)
+        return 0
+
+    lax.fori_loop(0, count, step, 0)
+
+
+class Pair:
+    def __init__(self, line, refs, send, recv, local, half):
+        self.line, self.refs = line, refs
+        self.send, self.recv, self.local, self.half = send, recv, local, half
+
+    def partner(self):
+        line = self.line
+        return (device(line.l, 1 - line.x, line.y, line.c), None)
+
+    def _part(self, ref, kind, j, x):
+        at = pl.multiple_of(x * self.half + j * 256, 256)
+        return ref.at[pl.ds(at, 256), :] if kind == 2 else ref.at[:, pl.ds(at, 256)]
+
+    def _copies(self, item, kind, j):
+        line = self.line
+        mine = line.g.at[item, 2 * line.l + line.x]
+        out = remote(
+            self._part(self.refs[kind], kind, j, 1 - line.x),
+            mine,
+            self.send.at[item],
+            self.recv.at[item],
+            self.partner()[0],
+        )
+        here = pltpu.make_async_copy(
+            self._part(self.refs[kind], kind, j, line.x), mine, self.local.at[item]
+        )
+        return out, here
+
+    def start(self, item, kind, j):
+        for copy in self._copies(item, kind, j):
+            copy.start()
+
+    def end(self, item, kind, j):
+        out, here = self._copies(item, kind, j)
+        here.wait()
+        out.wait_send()
+        out.wait_recv()
+
+
+class Back(Pair):
+    def _copies(self, item, kind, j):
+        line = self.line
+        home = self._part(self.refs[kind], kind, j, line.x)
+        out = remote(
+            line.g.at[item, 2 * line.l + 1 - line.x],
+            home,
+            self.send.at[item],
+            self.recv.at[item],
+            self.partner()[0],
+        )
+        here = pltpu.make_async_copy(
+            line.g.at[item, 2 * line.l + line.x], home, self.local.at[item]
+        )
+        return out, here
+
+
+def back_wait(back, item, kind, j):
+    line = back.line
+    out, here = back._copies(item, kind, j)
+    here.wait()
+    out.wait_send()
+    there = back._part(back.refs[kind], kind, j, 1 - line.x)
+    pltpu.make_async_copy(there, there, back.recv.at[item]).wait()
+
+
+def dot(a, b):
+    return lax.dot_general(a, b, (((1,), (0,)), ((), ())), preferred_element_type=F32)
+
+
+def dot_t(a, b):
+    return lax.dot_general(a, b, (((1,), (1,)), ((), ())), preferred_element_type=F32)
+
+
+def front_kernel(
+    n, x_ref, z_ref, wq, wkv, wo, x_all, z_all, g, p_send, p_recv, p_loc, ag_send, ag_recv, t_send, t_recv, t_loc
+):
+    line = Line(n, g, ag_send, ag_recv)
+    pair = Pair(line, (wq, wkv, wo), p_send, p_recv, p_loc, 256)
+    l, x, y, c = line.l, line.x, line.y, line.c
+    across, mate = device(l, 1 - x, y, c), device(l, x, y, 1 - c)
+    greet(line.partners() + [(across, None), (mate, None)])
+    for item in range(3):
+        pair.start(item, item, 0)
+
+    def token(i, src, dst):
+        own = pltpu.make_async_copy(src, dst.at[:, x], t_loc.at[i])
+        out = remote(
+            src.at[pl.ds(2 * c, 2)], dst.at[pl.ds(2 * c, 2), x], t_send.at[i, 0], t_recv.at[i, 0], across
+        )
+        part = dst.at[pl.ds(2 * c, 2), 1 - x]
+        on = remote(part, part, t_send.at[i, 1], t_recv.at[i, 1], mate)
+        return own, out, on
+
+    tokens = [token(0, x_ref, x_all), token(1, z_ref, z_all)]
+    for own, out, on in tokens:
+        own.start()
+        out.start()
+    for item in range(3):
+        pair.end(item, item, 0)
+        line.ag_start(item)
+    for i, (own, out, on) in enumerate(tokens):
+        out.wait_recv()
+        on.start()
+    for t in range(1, n):
+        for item in range(3):
+            line.ag_step(item, t)
+    for own, out, on in tokens:
+        own.wait()
+        out.wait_send()
+        on.wait()
+    for item in range(3):
+        line.ag_end(item)
+
+
+def front(n, x_in, z_in, wq, wkv, wo):
+    b, r, d = x_in.shape
+    whole = jax.ShapeDtypeStruct((b, 2, r, d), BF)
+    return pl.pallas_call(
+        functools.partial(front_kernel, n),
+        out_shape=(whole, whole, jax.ShapeDtypeStruct((3, 2 * n, 256, 256), BF)),
+        in_specs=[ANY] * 5,
+        out_specs=(ANY, ANY, ANY),
+        scratch_shapes=[
+            DMA((3,)),
+            DMA((3,)),
+            DMA((3,)),
+            DMA((3, 2, n)),
+            DMA((3, n)),
+            DMA((2, 2)),
+            DMA((2, 2)),
+            DMA((2,)),
+        ],
+        compiler_params=pltpu.CompilerParams(collective_id=0, has_side_effects=True),
+        name="front",
+    )(x_in, z_in, wq, wkv, wo)
+
+
+def keys_kernel(n, own_ref, out_ref, send, recv, local):
+    l, x, y, c = place()
+    left, right = device(l - 1, x, y, c), device(l + 1, x, y, c)
+    greet([(left, l >= 1), (right, l <= n - 2)])
+    own = pltpu.make_async_copy(own_ref, out_ref.at[l], local)
+    own.start()
+
+    def copy(b, src):
+        return remote(src, out_ref.at[b], send.at[b], recv.at[b], right)
+
+    pl.when(l <= n - 2)(lambda: copy(l, own_ref).start())
+    for t in range(1, n):
+
+        @pl.when(l - t >= 0)
+        def _():
+            b = l - t
+            copy(b, out_ref.at[b]).wait_recv()
+            pl.when(l <= n - 2)(lambda: copy(b, out_ref.at[b]).start())
+
+    for b in range(n):
+        pl.when((l >= b) & (l <= n - 2))(lambda b=b: copy(b, out_ref.at[b]).wait_send())
+    own.wait()
+
+
+def keys_forward(n, own):
+    return pl.pallas_call(
+        functools.partial(keys_kernel, n),
+        out_shape=jax.ShapeDtypeStruct((n,) + own.shape, BF),
+        in_specs=[VM],
+        out_specs=ANY,
+        scratch_shapes=[DMA((n,)), DMA((n,)), DMA],
+        compiler_params=pltpu.CompilerParams(collective_id=1, has_side_effects=True),
+        name="keys",
+    )(own)
+
+
+def keys_back_kernel(n, part_ref, out_ref, work, land, send, recv, local):
+    l, x, y, c = place()
+    left, right = device(l - 1, x, y, c), device(l + 1, x, y, c)
+    greet([(left, l >= 1), (right, l <= n - 2)])
+    load = pltpu.make_async_copy(part_ref, work, local)
+    load.start()
+    load.wait()
+
+    def copy(o):
+        return remote(work.at[o], land.at[o], send.at[o], recv.at[o], left)
+
+    def take(o):
+        copy(o).wait_recv()
+
+        def add(i, unused):
+            at = pl.ds(pl.multiple_of(i * 128, 128), 128)
+            work[o, at] = (work[o, at].astype(F32) + land[o, at].astype(F32)).astype(BF)
+            return 0
+
+        lax.fori_loop(0, work.shape[1] // 128, add, 0)
+
+    for o in range(n - 1):
+
+        @pl.when(l > o)
+        def _(o=o):
+            pl.when(l <= n - 2)(lambda: take(o))
+            copy(o).start()
+
+    pl.when(l <= n - 2)(lambda: take(l))
+    out_ref[...] = work[l]
+    for o in range(n - 1):
+        pl.when(l > o)(lambda o=o: copy(o).wait_send())
+
+
+def keys_back(n, parts):
+    return pl.pallas_call(
+        functools.partial(keys_back_kernel, n),
+        out_shape=jax.ShapeDtypeStruct(parts.shape[1:], BF),
+        in_specs=[ANY],
+        out_specs=VM,
+        scratch_shapes=[
+            pltpu.VMEM(parts.shape, BF),
+            pltpu.VMEM(parts.shape, BF),
+            DMA((n,)),
+            DMA((n,)),
+            DMA,
+        ],
+        compiler_params=pltpu.CompilerParams(
+            collective_id=2, has_side_effects=True, vmem_limit_bytes=40 * 2**20
+        ),
+        name="keys_back",
+    )(parts)
+
+
+class Group:
+    def __init__(self):
+        self.l, self.x, self.y, self.c = place()
+        self.mate = device(self.l, self.x, self.y, 1 - self.c)
+
+    def other(self, i):
+        x = 1 - self.x if i & 1 else self.x
+        y = 1 - self.y if i & 2 else self.y
+        return x, y
+
+    def chip(self, i):
+        x, y = self.other(i)
+        return device(self.l, x, y, self.c)
+
+    def partners(self):
+        return [(self.mate, None)] + [(self.chip(i), None) for i in (1, 2, 3)]
+
+
+def sum_kernel(m, part_ref, out_ref, core_land, low, chip_land, c_send, c_recv, s_send, s_recv):
+    group = Group()
+    x, y, c = group.x, group.y, group.c
+    greet(group.partners())
+    pairs = [(i, b) for b in range(4) for i in range(m)]
+
+    def to_mate(i, b):
+        return remote(
+            part_ref.at[i, b, :, :, 1 - c],
+            core_land.at[i, b],
+            c_send.at[i, b],
+            c_recv.at[i, b],
+            group.mate,
+        )
+
+    def to_chip(i, b, o):
+        ox, oy = group.other(o)
+        return remote(
+            low.at[i, b, ox, oy],
+            chip_land.at[i, o - 1, b],
+            s_send.at[i, b, o - 1],
+            s_recv.at[i, b, o - 1],
+            group.chip(o),
+        )
+
+    for i, b in pairs:
+        to_mate(i, b).start()
+    for i, b in pairs:
+        to_mate(i, b).wait_recv()
+        for u in range(2):
+            for v in range(2):
+                low[i, b, u, v] = (
+                    part_ref[i, b, u, v, c].astype(F32) + core_land[i, b, u, v].astype(F32)
+                ).astype(BF)
+        for o in (3, 1, 2):
+            to_chip(i, b, o).start()
+    for i, b in pairs:
+        total = low[i, b, x, y].astype(F32)
+        for o in (1, 2, 3):
+            to_chip(i, b, o).wait_recv()
+            total = total + chip_land[i, o - 1, b].astype(F32)
+        out_ref[i, b] = total
+    for i, b in pairs:
+        to_mate(i, b).wait_send()
+        for o in (1, 2, 3):
+            to_chip(i, b, o).wait_send()
+
+
+def group_sum(part, collective):
+    m, d = part.shape[0], part.shape[-1]
+    return pl.pallas_call(
+        functools.partial(sum_kernel, m),
+        out_shape=jax.ShapeDtypeStruct((m, 4, 32, d), F32),
+        in_specs=[VM],
+        out_specs=VM,
+        scratch_shapes=[
+            pltpu.VMEM((m, 4, 2, 2, 32, d), BF),
+            pltpu.VMEM((m, 4, 2, 2, 32, d), BF),
+            pltpu.VMEM((m, 3, 4, 32, d), BF),
+            DMA((m, 4)),
+            DMA((m, 4)),
+            DMA((m, 4, 3)),
+            DMA((m, 4, 3)),
+        ],
+        compiler_params=pltpu.CompilerParams(
+            collective_id=collective, has_side_effects=True, vmem_limit_bytes=56 * 2**20
+        ),
+        name=f"group_sum{m}",
+    )(part)
+
+
+def spread_kernel(own_ref, out_ref, s_send, s_recv, c_send, c_recv, local):
+    group = Group()
+    x, y, c = group.x, group.y, group.c
+    greet(group.partners())
+    mine = out_ref.at[:, x, y, c]
+    keep = pltpu.make_async_copy(own_ref, mine, local)
+    keep.start()
+
+    def to_chip(o):
+        return remote(own_ref, mine, s_send.at[o - 1], s_recv.at[o - 1], group.chip(o))
+
+    def to_mate(o):
+        ox, oy = group.other(o)
+        part = out_ref.at[:, ox, oy, c]
+        src = own_ref if o == 0 else part
+        return remote(src, part, c_send.at[o], c_recv.at[o], group.mate)
+
+    for o in (3, 1, 2):
+        to_chip(o).start()
+    to_mate(0).start()
+    for o in (1, 2, 3):
+        to_chip(o).wait_recv()
+        to_mate(o).start()
+    keep.wait()
+    for o in (1, 2, 3):
+        to_chip(o).wait_send()
+    for o in range(4):
+        to_mate(o).wait()
+
+
+def group_spread(own, collective):
+    b, r, d = own.shape
+    return pl.pallas_call(
+        spread_kernel,
+        out_shape=jax.ShapeDtypeStruct((b, 2, 2, 2, r, d), own.dtype),
+        in_specs=[VM],
+        out_specs=ANY,
+        scratch_shapes=[DMA((3,)), DMA((3,)), DMA((4,)), DMA((4,)), DMA],
+        compiler_params=pltpu.CompilerParams(collective_id=collective, has_side_effects=True),
+        name="group_spread",
+    )(own)
+
+
+def home_kernel(own_ref, out_ref, s_send, s_recv, local):
+    group = Group()
+    l, x, y, c = group.l, group.x, group.y, group.c
+    others = [device(l, x, y, 1 - c), device(l, x, 1 - y, c), device(l, x, 1 - y, 1 - c)]
+    greet([(o, None) for o in others])
+    mine = out_ref.at[:, :, y, c]
+    keep = pltpu.make_async_copy(own_ref, mine, local)
+    keep.start()
+    copies = [
+        remote(own_ref, mine, s_send.at[i], s_recv.at[i], o) for i, o in enumerate(others)
+    ]
+    for copy in copies:
+        copy.start()
+    keep.wait()
+    for copy in copies:
+        copy.wait()
+
+
+def home(own):
+    m, b, r, d = own.shape
+    return pl.pallas_call(
+        home_kernel,
+        out_shape=jax.ShapeDtypeStruct((m, b, 2, 2, r, d), own.dtype),
+        in_specs=[VM],
+        out_specs=ANY,
+        scratch_shapes=[DMA((3,)), DMA((3,)), DMA],
+        compiler_params=pltpu.CompilerParams(collective_id=7, has_side_effects=True),
+        name="home",
+    )(own)
+
+
+def rows_kernel(n, part_ref, dq, dkv, do, g, land, rs_send, rs_recv, b_send, b_recv, b_loc, local):
+    line = Line(n, g, None, None, land, rs_send, rs_recv)
+    back = Back(line, (dq, dkv, do), b_send, b_recv, b_loc, 256)
+    greet(line.partners() + [back.partner()])
+    load = pltpu.make_async_copy(part_ref, g, local)
+    load.start()
+    load.wait()
+    for q in range(1, n):
+        each(3, lambda item, q=q: line.rs_step(item, q))
+    each(3, line.rs_final)
+    for item in range(3):
+        back.start(item, item, 0)
+    for item in range(3):
+        back_wait(back, item, item, 0)
+    each(3, line.rs_end)
+
+
+def rows_sum(n, parts):
+    return pl.pallas_call(
+        functools.partial(rows_kernel, n),
+        out_shape=(
+            jax.ShapeDtypeStruct((256, 512), BF),
+            jax.ShapeDtypeStruct((256, 512), BF),
+            jax.ShapeDtypeStruct((512, 256), BF),
+        ),
+        in_specs=[ANY],
+        out_specs=(ANY, ANY, ANY),
+        scratch_shapes=[
+            pltpu.VMEM((3, 2 * n, 256, 256), BF),
+            pltpu.VMEM((3, 2 * n + 2, 256, 256), BF),
+            DMA((3, 2, n)),
+            DMA((3, n + 1)),
+            DMA((3,)),
+            DMA((3,)),
+            DMA((3,)),
+            DMA,
+        ],
+        compiler_params=pltpu.CompilerParams(
+            collective_id=8, has_side_effects=True, vmem_limit_bytes=40 * 2**20
+        ),
+        name="rows_sum",
+    )(parts)
+
+
+def ffn_kernel(
+    n,
+    chunks,
+    inner_ref,
+    dz_ref,
+    wg,
+    wu,
+    wd,
+    out_ref,
+    din_ref,
+    dgw,
+    duw,
+    ddw,
+    inner_t,
+    out_acc,
+    din_acc,
+    g,
+    land,
+    low,
+    prod_t,
+    p_send,
+    p_recv,
+    p_loc,
+    ag_send,
+    ag_recv,
+    rs_send,
+    rs_recv,
+    b_send,
+    b_recv,
+    b_loc,
+    o_loc,
+):
+    line = Line(n, g, ag_send, ag_recv, land, rs_send, rs_recv)
+    half = chunks * 256
+    pair = Pair(line, (wg, wu, wd), p_send, p_recv, p_loc, half)
+    back = Back(line, (dgw, duw, ddw), b_send, b_recv, b_loc, half)
+    greet(line.partners() + [pair.partner()])
+    blocks = 2 * n
+    for j in range(chunks):
+        for kind in range(3):
+            pair.start(3 * j + kind, kind, j)
+
+    def turn(i, unused):
+        m, s = lax.div(i, blocks), lax.rem(i, blocks)
+        tile = inner_ref[m, :, pl.ds(pl.multiple_of(s * 256, 256), 256)]
+        inner_t[s, :, pl.ds(pl.multiple_of(m * 256, 256), 256)] = tile.T
+        return 0
+
+    for j in range(chunks):
+        for kind in range(3):
+            pair.end(3 * j + kind, kind, j)
+            line.ag_start(3 * j + kind)
+    lax.fori_loop(0, 4 * blocks, turn, 0)
+
+    def compute(j):
+        base = 3 * j
+
+        def rows(m, unused):
+            a = inner_ref[m]
+            d = dz_ref[m]
+            gated = dot(a, g[base].reshape(blocks * 256, 256))
+            upward = dot(a, g[base + 1].reshape(blocks * 256, 256))
+            grad = dot_t(d[:, :256], g[base + 2, 0])
+            for s in range(1, blocks):
+                grad = grad + dot_t(d[:, s * 256 : (s + 1) * 256], g[base + 2, s])
+            sigma = jax.nn.sigmoid(gated)
+            swish = gated * sigma
+            product = (swish * upward).astype(BF)
+            d_gated = (grad * upward * sigma * (1.0 + gated * (1.0 - sigma))).astype(BF)
+            d_upward = (grad * swish).astype(BF)
+            at = pl.ds(pl.multiple_of(m * 256, 256), 256)
+            low[0, at] = d_gated
+            low[1, at] = d_upward
+            prod_t[:, at] = product.T
+            for s in range(blocks):
+                cols = slice(s * 256, (s + 1) * 256)
+                o = dot(product, g[base + 2, s])
+                i = dot_t(d_gated, g[base, s]) + dot_t(d_upward, g[base + 1, s])
+                if j == 0:
+                    out_acc[m, :, cols] = o
+                    din_acc[m, :, cols] = i
+                else:
+                    out_acc[m, :, cols] += o
+                    din_acc[m, :, cols] += i
+            return 0
+
+        lax.fori_loop(0, 4, rows, 0)
+
+        def weights(s, unused):
+            t = inner_t[s]
+            g[base, s] = dot(t, low[0]).astype(BF)
+            g[base + 1, s] = dot(t, low[1]).astype(BF)
+            z = dz_ref[:, :, pl.ds(pl.multiple_of(s * 256, 256), 256)].reshape(1024, 256)
+            g[base + 2, s] = dot(prod_t[...], z).astype(BF)
+            return 0
+
+        lax.fori_loop(0, blocks, weights, 0)
+
+    def items(j, body):
+        each(3, lambda i: body(3 * j + i))
+
+    for j in range(chunks):
+        for t in range(1, n):
+            items(j, lambda item, t=t: line.ag_step(item, t))
+            if j > 0:
+                items(j - 1, lambda item, t=t: line.rs_step(item, t))
+        items(j, line.ag_end)
+        compute(j)
+        if j > 0:
+            items(j - 1, line.rs_final)
+            for kind in range(3):
+                back.start(3 * j - 3 + kind, kind, j - 1)
+    last = chunks - 1
+
+    def flush(m, unused):
+        inner_ref[m] = out_acc[m].astype(BF)
+        dz_ref[m] = din_acc[m].astype(BF)
+        return 0
+
+    for t in range(1, n):
+        items(last, lambda item, t=t: line.rs_step(item, t))
+    lax.fori_loop(0, 4, flush, 0)
+    outs = [
+        pltpu.make_async_copy(inner_ref, out_ref, o_loc.at[0]),
+        pltpu.make_async_copy(dz_ref, din_ref, o_loc.at[1]),
+    ]
+    for copy in outs:
+        copy.start()
+    items(last, line.rs_final)
+    for kind in range(3):
+        back.start(3 * last + kind, kind, last)
+    for j in range(chunks):
+        for kind in range(3):
+            back_wait(back, 3 * j + kind, kind, j)
+    for j in range(chunks):
+        items(j, line.rs_end)
+    for copy in outs:
+        copy.wait()
+
+
+def ffn(n, inner, dz, wg, wu, wd):
+    d, hid = wg.shape[0] * 2 * n, wg.shape[1]
+    chunks = hid // 512
+    items = 3 * chunks
+    tokens = jax.ShapeDtypeStruct((4, 256, d), BF)
+    return pl.pallas_call(
+        lambda inner_any, dz_any, *rest: ffn_load(n, chunks, inner_any, dz_any, *rest),
+        out_shape=(
+            tokens,
+            tokens,
+            jax.ShapeDtypeStruct(wg.shape, BF),
+            jax.ShapeDtypeStruct(wu.shape, BF),
+            jax.ShapeDtypeStruct(wd.shape, BF),
+        ),
+        in_specs=[ANY] * 5,
+        out_specs=(ANY,) * 5,
+        scratch_shapes=[
+            pltpu.VMEM((4, 256, d), BF),
+            pltpu.VMEM((4, 256, d), BF),
+            DMA((2,)),
+            pltpu.VMEM((2 * n, 256, 1024), BF),
+            pltpu.VMEM((4, 256, d), F32),
+            pltpu.VMEM((4, 256, d), F32),
+            pltpu.VMEM((items, 2 * n, 256, 256), BF),
+            pltpu.VMEM((items, 2 * n + 2, 256, 256), BF),
+            pltpu.VMEM((2, 1024, 256), BF),
+            pltpu.VMEM((256, 1024), BF),
+            DMA((items,)),
+            DMA((items,)),
+            DMA((items,)),
+            DMA((items, 2, n)),
+            DMA((items, n)),
+            DMA((items, 2, n)),
+            DMA((items, n + 1)),
+            DMA((items,)),
+            DMA((items,)),
+            DMA((items,)),
+            DMA((2,)),
+        ],
+        compiler_params=pltpu.CompilerParams(
+            collective_id=9, has_side_effects=True, vmem_limit_bytes=62 * 2**20
+        ),
+        name="ffn",
+    )(inner, dz, wg, wu, wd)
+
+
+def ffn_load(n, chunks, inner_any, dz_any, wg, wu, wd, out, din, dgw, duw, ddw, inner_v, dz_v, in_loc, *rest):
+    loads = [
+        pltpu.make_async_copy(inner_any, inner_v, in_loc.at[0]),
+        pltpu.make_async_copy(dz_any, dz_v, in_loc.at[1]),
+    ]
+    for copy in loads:
+        copy.start()
+    for copy in loads:
+        copy.wait()
+    ffn_kernel(n, chunks, inner_v, dz_v, wg, wu, wd, out, din, dgw, duw, ddw, *rest)
+
+
+def fast_local(
+    inputs,
+    cotangent,
+    bucket_sizes,
+    true_lengths,
+    attention_gain,
+    feedforward_gain,
+    query_gain,
+    key_gain,
+    query_weight,
+    key_matrix,
+    value_matrix,
+    headgate_weight,
+    output_weight,
+    gate_weight,
+    up_weight,
+    down_weight,
+):
+    batches, rows, width = inputs.shape
+    n = lax.axis_size("seq") // 2
+    seq, kv = lax.axis_index("seq"), lax.axis_index("kv")
+    l, x = seq // 2, seq % 2
+    scale = HEAD_SIZE ** (-0.5)
+    span = 2 * rows
+    gain_query = query_gain.astype(F32)
+    gain_key = key_gain.astype(F32)
+
+    small = jnp.concatenate(
+        [headgate_weight.T, attention_gain[None], feedforward_gain[None]], axis=0
+    )
+    small = lax.all_gather(small, "seq", axis=1, tiled=True)
+    w_head = lax.dynamic_slice_in_dim(small, x * 2, 2, 0)
+    gain_a = small[4].astype(F32)
+    gain_f = small[5].astype(F32)
+    paired = jnp.concatenate(
+        [key_matrix[:, :128], value_matrix[:, :128], key_matrix[:, 128:], value_matrix[:, 128:]],
+        axis=1,
+    )
+    x_all, z_all, g = front(n, inputs, cotangent, query_weight, paired, output_weight)
+    w_query = g[0].reshape(width, 256)
+    w_keys = g[1].reshape(width, 256)
+    w_output = g[2]
+
+    def own_rows(values):
+        return lax.dynamic_slice_in_dim(values, kv * 32, 32, 1)
+
+    row_index = l * span + jnp.arange(span, dtype=jnp.int32)
+    key_index = jnp.arange(n * span, dtype=jnp.int32)
+    layouts = [token_layout(row_index, bucket_sizes[b], true_lengths[b]) for b in range(batches)]
+    key_layouts = [
+        token_layout(key_index, bucket_sizes[b], true_lengths[b]) for b in range(batches)
+    ]
+    positions = jnp.concatenate([item[1] for item in layouts])
+    allowed = jnp.stack(
+        [
+            (mine[0][:, None] == theirs[0][None, :])
+            & (key_index[None, :] <= row_index[:, None])
+            & theirs[2][None, :]
+            for mine, theirs in zip(layouts, key_layouts)
+        ]
+    )[:, None]
+    cosine, sine = rope_tables(positions, HEAD_SIZE)
+
+    current = x_all.reshape(batches * span, width).astype(F32)
+    normed = (current * rms_scale(current) * gain_a).astype(BF)
+    query_proj = jnp.dot(normed, w_query, preferred_element_type=F32).reshape(-1, 2, HEAD_SIZE)
+    keys_proj = jnp.dot(normed, w_keys, preferred_element_type=F32)
+    key_proj = keys_proj[:, :HEAD_SIZE].reshape(-1, 1, HEAD_SIZE)
+    value_low = keys_proj[:, HEAD_SIZE:].astype(BF)
+    query_scale = rms_scale(query_proj)
+    query_normal = query_proj * query_scale
+    key_scale = rms_scale(key_proj)
+    key_normal = key_proj * key_scale
+    query_rot = rotate_forward(query_normal * gain_query, cosine, sine).astype(BF)
+    key_rot = rotate_forward(key_normal * gain_key, cosine, sine).astype(BF)
+    gate = jax.nn.sigmoid(times_transpose(normed, w_head))
+    own_keys = jnp.concatenate([key_rot.reshape(-1, HEAD_SIZE), value_low], axis=1)
+    all_keys = keys_forward(n, own_keys).reshape(n, batches, span, 256)
+    seen = (jnp.arange(n) <= l)[:, None, None, None]
+    all_keys = jnp.where(seen, all_keys, 0).transpose(1, 0, 2, 3).reshape(batches, n * span, 256)
+    keys, values = all_keys[..., :HEAD_SIZE], all_keys[..., HEAD_SIZE:]
+    query = query_rot.reshape(batches, span, 2, HEAD_SIZE).transpose(0, 2, 1, 3)
+
+    def weights_of(log_total=None):
+        raw = jnp.einsum("bhtd,bsd->bhts", query, keys, preferred_element_type=F32) * scale
+        if log_total is None:
+            return jnp.where(allowed, jnp.exp(raw), 0.0)
+        return jnp.where(allowed, jnp.exp(raw - log_total), 0.0)
+
+    spread = weights_of()
+    log_total = jnp.log(jnp.sum(spread, axis=-1, keepdims=True))
+    weights = weights_of(log_total)
+    attended = jnp.einsum("bhts,bsd->bhtd", weights.astype(BF), values, preferred_element_type=F32)
+    gate_heads = gate.reshape(batches, span, 2).transpose(0, 2, 1)[..., None]
+    mixed = (attended * gate_heads).astype(BF).transpose(0, 2, 1, 3).reshape(-1, 256)
+    branch = jnp.concatenate(
+        [jnp.dot(mixed, w_output[s], preferred_element_type=F32) for s in range(2 * n)], axis=1
+    ).astype(BF)
+    split = (batches, 2, 2, 2, 32, width)
+    own_x = own_rows(inputs).astype(F32)
+    hidden = own_x + group_sum(branch.reshape((1,) + split), 3)[0]
+    scale_f = rms_scale(hidden)
+    normal_f = hidden * scale_f
+    inner = group_spread((normal_f * gain_f).astype(BF), 4)
+    out_part, din_part, d_gate, d_up, d_down = ffn(
+        n,
+        inner.reshape(batches, span, width),
+        z_all.reshape(batches, span, width),
+        gate_weight,
+        up_weight,
+        down_weight,
+    )
+    sums = group_sum(jnp.stack([out_part.reshape(split), din_part.reshape(split)]), 5)
+    own_out = (hidden + sums[0]).astype(BF)
+    grad_inner = sums[1]
+    own_dz = own_rows(cotangent).astype(F32)
+    sum_feedforward_gain = jnp.sum(grad_inner * normal_f, axis=(0, 1))
+    grad_hidden = own_dz + norm_backward(grad_inner * gain_f, normal_f, scale_f)
+    grad_branch = group_spread(grad_hidden.astype(BF), 6).reshape(-1, width)
+    d_output = jnp.stack(
+        [outer_sum(mixed, grad_branch[:, s * 256 : (s + 1) * 256]).astype(BF) for s in range(2 * n)]
+    )
+    grad_mixed = sum(
+        times_transpose(grad_branch[:, s * 256 : (s + 1) * 256], w_output[s]) for s in range(2 * n)
+    )
+    grad_mixed = grad_mixed.reshape(batches, span, 2, HEAD_SIZE).transpose(0, 2, 1, 3)
+    grad_heads = (grad_mixed * gate_heads).astype(BF)
+    grad_logits = (
+        jnp.sum(grad_mixed * attended, axis=-1, keepdims=True) * gate_heads * (1.0 - gate_heads)
+    ).astype(BF)
+    delta = jnp.sum(grad_heads.astype(F32) * attended, axis=-1, keepdims=True)
+    grad_weights = jnp.einsum("bhtd,bsd->bhts", grad_heads, values, preferred_element_type=F32)
+    grad_scores = (weights * (grad_weights - delta)).astype(BF)
+    grad_query = scale * jnp.einsum(
+        "bhts,bsd->bhtd", grad_scores, keys, preferred_element_type=F32
+    )
+    grad_keys = scale * jnp.einsum(
+        "bhts,bhtd->bsd", grad_scores, query, preferred_element_type=F32
+    )
+    grad_values = jnp.einsum(
+        "bhts,bhtd->bsd", weights.astype(BF), grad_heads, preferred_element_type=F32
+    )
+    grad_pair = jnp.concatenate([grad_keys, grad_values], axis=-1).astype(BF)
+    grad_pair = grad_pair.reshape(batches, n, span, 256).transpose(1, 0, 2, 3)
+    local_pair = keys_back(n, grad_pair.reshape(n, batches * span, 256)).astype(F32)
+
+    grad_query_rot = grad_query.transpose(0, 2, 1, 3).reshape(-1, 2, HEAD_SIZE)
+    grad_query_norm = rotate_backward(grad_query_rot, cosine, sine)
+    sum_query_gain = jnp.sum(grad_query_norm * query_normal, axis=(0, 1))
+    d_query = (
+        norm_backward(grad_query_norm * gain_query, query_normal, query_scale)
+        .astype(BF)
+        .reshape(-1, 256)
+    )
+    grad_key_norm = rotate_backward(local_pair[:, None, :HEAD_SIZE], cosine, sine)
+    sum_key_gain = jnp.sum(grad_key_norm * key_normal, axis=(0, 1))
+    d_key = norm_backward(grad_key_norm * gain_key, key_normal, key_scale).astype(BF)
+    d_pair = jnp.concatenate(
+        [d_key.reshape(-1, HEAD_SIZE), local_pair[:, HEAD_SIZE:].astype(BF)], axis=1
+    )
+    logits_low = grad_logits[..., 0].transpose(0, 2, 1).reshape(-1, 2)
+    d_head = outer_sum(logits_low, normed)
+    d_head = jnp.where(jnp.arange(2)[:, None, None] == x, d_head[None], 0.0).reshape(4, width)
+    d_query_weight = outer_sum(normed, d_query).astype(BF).reshape(2 * n, 256, 256)
+    d_pair_weight = outer_sum(normed, d_pair).astype(BF).reshape(2 * n, 256, 256)
+    grad_partial = (
+        times_transpose(d_query, w_query)
+        + times_transpose(d_pair, w_keys)
+        + jnp.dot(logits_low, w_head, preferred_element_type=F32)
+    ).astype(BF)
+    grad_normed = group_sum(grad_partial.reshape((1,) + split), 10)[0]
+    dq, dkv, do = rows_sum(n, jnp.stack([d_query_weight, d_pair_weight, d_output]))
+    scale_a = rms_scale(own_x)
+    normal_a = own_x * scale_a
+    sum_attention_gain = jnp.sum(grad_normed * normal_a, axis=(0, 1))
+    own_grad = (grad_hidden + norm_backward(grad_normed * gain_a, normal_a, scale_a)).astype(BF)
+    outs = home(jnp.stack([own_out, own_grad])).reshape(2, batches, rows, width)
+    gains = lax.psum(
+        jnp.concatenate([sum_attention_gain, sum_feedforward_gain, sum_query_gain, sum_key_gain]),
+        ("seq", "kv"),
+    )
+    head_total = lax.psum(d_head, "seq")
+    own_width = width // (2 * n)
+
+    def cut(values):
+        return lax.dynamic_slice_in_dim(values, seq * own_width, own_width, values.ndim - 1)
+
+    return (
+        outs[0],
+        outs[1],
+        cut(gains[:width]),
+        cut(gains[width : 2 * width]),
+        gains[2 * width : 2 * width + HEAD_SIZE],
+        gains[2 * width + HEAD_SIZE :],
+        dq.astype(F32),
+        jnp.concatenate([dkv[:, :128], dkv[:, 256:384]], axis=1).astype(F32),
+        jnp.concatenate([dkv[:, 128:256], dkv[:, 384:]], axis=1).astype(F32),
+        cut(head_total).T,
+        do.astype(F32),
+        d_gate.astype(F32),
+        d_up.astype(F32),
+        d_down.astype(F32),
+    )
+
+
 def solution(mesh):
+    chosen = fast_local if dict(mesh.shape) == {"seq": 8, "kv": 4} else local
     in_specs = (
         P(None, "seq", None),
         P(None, "seq", None),
@@ -485,4 +1483,4 @@
         P("seq", "kv"),
         P("kv", "seq"),
     )
-    return jax.shard_map(local, mesh=mesh, in_specs=in_specs, out_specs=out_specs, check_vma=False)
+    return jax.shard_map(chosen, mesh=mesh, in_specs=in_specs, out_specs=out_specs, check_vma=False)

time: 2100 us -> 1140 us (0.54)
  waiting for transfers between devices: 1030 us -> 0 us
  Pallas kernels: 0 us -> 849 us
  blocking collectives: 389 us -> 109 us
  matrix products: 323 us -> 71.5 us
  other arithmetic: 184 us -> 60.8 us
  local copies, waits for them, and re-layouts: 138 us -> 36.4 us
    pallas_call x0 -> x11, Pallas kernels: none -> 849 us  [the longest x1 363 us: ffn(): pl.pallas_call(lambda inner_any, dz_any, *rest: ffn_load(n, chunks, inner...]
    reduce_scatter x11 -> x0, waiting for transfers between devices: 714 us -> none  [the longest x4 242 us: local(): lax.psum_scatter(grad_values.astype(jnp.bfloat16), 'seq', scatter_dimensi...]
    all_gather x11 -> x1, blocking collectives: 326 us -> 32.2 us  [fast_local(): small = lax.all_gather(small, 'seq', axis=1, tiled=True)]
    psum x4 -> x0, waiting for transfers between devices: 184 us -> none  [the longest x1 88.2 us: local(): lax.psum(jnp.dot(product, w_down, preferred_element_type=jnp.float32).ast...]
    dot_general x32 -> x11, matrix products: 128 us -> 9.39 us  [outer_sum(): lax.dot_general(left, right, (((0,), (0,)), ((), ())), preferred_element_...]
    unnamed x32 -> x0, waiting for transfers between devices: 112 us -> none
    dot_general x88 -> x16, matrix products: 132 us -> 36.1 us  [the longest x8 9.55 us: fast_local(): jnp.dot(mixed, w_output[s], preferred_element_type=F32)]
    dot_general x32 -> x11, matrix products: 62.6 us -> 17.5 us  [times_transpose(): lax.dot_general(left, weight, (((1,), (1,)), ((), ())), preferred_element...]
  transfers between devices with their start and end apart: 27 -> 0, of which waited for: 18 -> 0; matrix products, arithmetic and copies ran while one was open for 25% -> 0% of each run, Pallas kernels for 0% -> 0%
where the time goes in v1:
time: 1140 us; the launch traced here: 1130 us
  Pallas kernels  849 us (74%)
  blocking collectives  109 us (10%)
  matrix products  71.5 us (6%)
  other arithmetic  60.8 us (5%)
  local copies, waits for them, and re-layouts  36.4 us (3%)
    pallas_call x1, Pallas kernels, ffn(): pl.pallas_call(lambda inner_any, dz_any, *rest: ffn_load(n, chunks, inner...  363 us
    pallas_call x1, Pallas kernels, front(): pl.pallas_call(functools.partial(front_kernel, n), out_shape=(whole, whol...  142 us
    pallas_call x3, Pallas kernels, group_sum(): pl.pallas_call(functools.partial(sum_kernel, m), out_shape=jax.ShapeDtype...  115 us
    pallas_call x2, Pallas kernels, group_spread(): pl.pallas_call(spread_kernel, out_shape=jax.ShapeDtypeStruct((b, 2, 2, 2,...  62.7 us
    pallas_call x1, Pallas kernels, rows_sum(): pl.pallas_call(functools.partial(rows_kernel, n), out_shape=(jax.ShapeDty...  59.7 us
    pallas_call x1, Pallas kernels, home(): pl.pallas_call(home_kernel, out_shape=jax.ShapeDtypeStruct((m, b, 2, 2, r...  49.3 us
    pallas_call x1, Pallas kernels, keys_back(): pl.pallas_call(functools.partial(keys_back_kernel, n), out_shape=jax.Shap...  45.1 us
    psum x1, blocking collectives, fast_local(): lax.psum(jnp.concatenate([sum_attention_gain, sum_feedforward_gain, sum_q...  38.9 us

profile of v1, /device:TPU:0, one launch (start us, length us, event | category | flops | bytes accessed | tf_op | source)
XLA Modules:
  0.0 1129.1 jit_solution(12680236312585136210)
XLA Ops:
  2.7 32.2 %all_gather.3 = bf16[6,2048]{1,0:T(8,128)(2,1)S(1)} all-gather(bf16[6,256]{1,0:T(8,128)(2,1)S(1)} %pad_maximum_fusion.12), channel_id=1, replica_groups=mesh['seq'=8,'kv'=4] {'seq'}, dimensions={1}, use_global_device_ids=true | all-gather | bytes 27648 | tf_op jit(solution)/shard_map/all_gather | solution.py:1275
  36.6 142.1 %front.1 = (bf16[4,2,128,2048]{3,2,1,0:T(8,128)(2,1)}, bf16[4,2,128,2048]{3,2,1,0:T(8,128)(2,1)}, bf16[3,8,256,256]{3,2,1,0:T(8,128)(2,1)}) custom-call(bf16[4,128,2048]{2,1,0:T(8,128)(2,1)} %x_ref.1, bf16[4,128,2048]{2,1,0:T(8,128)(2,1)} %z_ref.1, bf16[256,512]{1,0:T(8,128)(2,1)} %wq.1, bf16[256,512]{1,0:T(8,128)(2,1)} %pad_maximum_fusion.10.wkv, ...), custom_call_target="tpu_custom_call" | custom-call | tf_op jit(solution)/shard_map/front/pallas_call | solution.py:730
  186.1 3.5 multiply_reduce_fusion.6
  193.4 3.5 fusion.197
  201.9 12.0 %keys.1 = bf16[4,1024,256]{2,1,0:T(8,128)(2,1)} custom-call(bf16[1024,256]{1,0:T(8,128)(2,1)} %pad_maximum_fusion.6.own_ref), custom_call_target="tpu_custom_call" | custom-call | tf_op jit(solution)/shard_map/keys/pallas_call | solution.py:775
  226.0 8.5 fusion.2
  234.5 5.2 fusion.4
  239.6 3.4 fusion.58
  243.0 5.9 fusion.72
  261.2 30.5 %group_sum1.2 = f32[1,4,32,2048]{3,2,1,0:T(8,128)} custom-call(bf16[1,4,2,2,2,32,2048]{6,5,4,3,2,1,0:T(8,128)(2,1)} %copy-done.23), custom_call_target="tpu_custom_call" | custom-call | tf_op jit(solution)/shard_map/group_sum1/pallas_call | solution.py:908
  294.4 31.3 %group_spread.2 = bf16[4,2,2,2,32,2048]{5,4,3,2,1,0:T(8,128)(2,1)} custom-call(bf16[4,32,2048]{2,1,0:T(8,128)(2,1)} %multiply_convert_fusion.3.own_ref), custom_call_target="tpu_custom_call" | custom-call | tf_op jit(solution)/shard_map/group_spread/pallas_call | solution.py:961
  325.8 363.5 %ffn.1 = (bf16[4,256,2048]{2,1,0:T(8,128)(2,1)}, bf16[4,256,2048]{2,1,0:T(8,128)(2,1)}, bf16[256,1536]{1,0:T(8,128)(2,1)}, bf16[256,1536]{1,0:T(8,128)(2,1)}, bf16[1536,256]{1,0:T(8,128)(2,1)}) custom-call(bf16[4,256,2048]{2,1,0:T(8,128)(2,1)} %bitcast.411, bf16[4,256,2048]{2,1,0:T(8,128)(2,1)} %bitcast.422, bf16[256,1536]{1,0:T(8,128)(2,1)} %rest_0_.1, ...), custom_call_target="tpu_custom_call" | custom-call | tf_op jit(solution)/shard_map/ffn/pallas_call | solution.py:1192
  689.3 7.4 pad_maximum_fusion.part_ref
  696.7 53.7 %group_sum2.1 = f32[2,4,32,2048]{3,2,1,0:T(8,128)} custom-call(bf16[2,4,2,2,2,32,2048]{6,5,4,3,2,1,0:T(8,128)(2,1)} %pad_maximum_fusion.part_ref), custom_call_target="tpu_custom_call" | custom-call | tf_op jit(solution)/shard_map/group_sum2/pallas_call | solution.py:908
  755.0 31.3 %group_spread.3 = bf16[4,2,2,2,32,2048]{5,4,3,2,1,0:T(8,128)(2,1)} custom-call(bf16[4,32,2048]{2,1,0:T(8,128)(2,1)} %get-tuple-element.74.own_ref), custom_call_target="tpu_custom_call" | custom-call | tf_op jit(solution)/shard_map/group_spread/pallas_call | solution.py:961
  804.4 5.1 multiply_convert_fusion
  830.0 45.1 %keys_back.1 = bf16[1024,256]{1,0:T(8,128)(2,1)S(1)} custom-call(bf16[4,1024,256]{2,1,0:T(8,128)(2,1)S(1)} %bitcast.387), custom_call_target="tpu_custom_call" | custom-call | tf_op jit(solution)/shard_map/keys_back/pallas_call | solution.py:821
  878.0 3.3 add_convert_fusion
  881.2 30.3 %group_sum1.3 = f32[1,4,32,2048]{3,2,1,0:T(8,128)} custom-call(bf16[1,4,2,2,2,32,2048]{6,5,4,3,2,1,0:T(8,128)(2,1)} %bitcast.410), custom_call_target="tpu_custom_call" | custom-call | tf_op jit(solution)/shard_map/group_sum1/pallas_call | solution.py:908
  916.3 49.3 %home.1 = bf16[2,4,2,2,32,2048]{5,4,3,2,1,0:T(8,128)(2,1)} custom-call(bf16[2,4,32,2048]{3,2,1,0:T(8,128)(2,1)} %pad_maximum_fusion.3.own_ref), custom_call_target="tpu_custom_call" | custom-call | tf_op jit(solution)/shard_map/home/pallas_call | solution.py:992
  965.5 4.9 fusion.189
  970.4 38.9 %psum.14 = f32[4352]{0:T(1024)S(1)} all-reduce(f32[4352]{0:T(1024)S(1)} %pad_maximum_fusion.11), channel_id=1, replica_groups=mesh['seq'=8,'kv'=4] {'seq','kv'}, use_global_device_ids=true, to_apply=%region_40.41 | all-reduce | flops 4352 | bytes 34816 | tf_op jit(solution)/shard_map/psum | solution.py:1422
  1021.9 59.7 %rows_sum.1 = (bf16[256,512]{1,0:T(8,128)(2,1)S(1)}, bf16[256,512]{1,0:T(8,128)(2,1)S(1)}, bf16[512,256]{1,0:T(8,128)(2,1)S(1)}) custom-call(bf16[3,8,256,256]{3,2,1,0:T(8,128)(2,1)S(1)} %pad_maximum_fusion.1.part_ref), custom_call_target="tpu_custom_call" | custom-call | tf_op jit(solution)/shard_map/rows_sum/pallas_call | solution.py:1021
  1084.9 38.3 %psum.15 = f32[4,2048]{1,0:T(4,128)S(1)} all-reduce(f32[4,2048]{1,0:T(4,128)S(1)} %broadcast_select_fusion), channel_id=1, replica_groups=mesh['seq'=8,'kv'=4] {'seq'}, use_global_device_ids=true, to_apply=%region_41.42 | all-reduce | flops 8192 | bytes 65536 | tf_op jit(solution)/shard_map/psum | solution.py:1426
  (232 shorter events, 118.1 us)
Async XLA Ops:
  185.2 8.2 copy-start.25
  186.1 3.6 copy-start.37
  186.1 4.4 copy-start.38
  189.7 31.8 %copy-start.8 = (f32[1024,2,128]{0,2,1:T(8,128)}, f32[1024,2,128]{0,2,1:T(8,128)S(1)}, u32[]{:S(2)}) copy-start(f32[1024,2,128]{0,2,1:T(8,128)S(1)} %get-tuple-element.126) | copy-start | bytes 3145732
  193.4 5.5 copy-start.40
  196.8 4.3 copy-start.15
  215.9 27.1 %copy-start.10 = (bf16[4,4,256,256]{3,2,1,0:T(8,128)(2,1)}, bf16[4,4,256,256]{3,2,1,0:T(8,128)(2,1)S(1)}, u32[]{:S(2)}) copy-start(bf16[4,4,256,256]{3,2,1,0:T(8,128)(2,1)S(1)} %copy.147) | copy-start | bytes 6291460
  226.0 8.5 copy-start.35
  249.3 8.8 copy-start.29
  794.3 8.6 copy-start.24
  804.4 7.0 copy-start.11
  813.7 7.1 copy-start.9
  820.7 3.9 slice-start
  829.8 45.4 %copy-start.20 = (f32[1024,64]{1,0:T(8,128)S(1)}, f32[1024,64]{1,0:T(8,128)}, u32[]{:S(2)}) copy-start(f32[1024,64]{1,0:T(8,128)} %copy-done.19) | copy-start | bytes 786436
  830.0 45.6 %copy-start.16 = (f32[1024,256]{1,0:T(8,128)S(1)}, f32[1024,256]{1,0:T(8,128)}, u32[]{:S(2)}) copy-start(f32[1024,256]{1,0:T(8,128)} %copy-done.15) | copy-start | bytes 3145732
  830.0 45.6 %copy-start.22 = (f32[1024,64]{1,0:T(8,128)S(1)}, f32[1024,64]{1,0:T(8,128)}, u32[]{:S(2)}) copy-start(f32[1024,64]{1,0:T(8,128)} %copy-done.21) | copy-start | bytes 786436
  881.2 30.3 %copy-start.17 = (bf16[4,128,2048]{2,1,0:T(8,128)(2,1)S(1)}, bf16[4,128,2048]{2,1,0:T(8,128)(2,1)}, u32[]{:S(2)}) copy-start(bf16[4,128,2048]{2,1,0:T(8,128)(2,1)} %x_ref.1) | copy-start | bytes 6291460
  881.2 32.0 %copy-start.2 = (f32[2,4,32,2048]{3,2,1,0:T(8,128)S(1)}, f32[2,4,32,2048]{3,2,1,0:T(8,128)}, u32[]{:S(2)}) copy-start(f32[2,4,32,2048]{3,2,1,0:T(8,128)} %group_sum2.1) | copy-start | bytes 6291460
  911.5 3.7 copy-start.31
  965.5 45.6 %copy-start.30 = (bf16[4,256,2,128]{3,2,1,0:T(2,128)(2,1)S(1)}, bf16[4,256,2,128]{3,2,1,0:T(2,128)(2,1)}, u32[]{:S(2)}) copy-start(bf16[4,256,2,128]{3,2,1,0:T(2,128)(2,1)} %copy-done.29) | copy-start | bytes 1572868
  1009.3 6.0 copy-start.4
  1081.6 43.1 %copy-start.34 = (bf16[256,1536]{1,0:T(8,128)(2,1)S(1)}, bf16[256,1536]{1,0:T(8,128)(2,1)}, u32[]{:S(2)}) copy-start(bf16[256,1536]{1,0:T(8,128)(2,1)} %get-tuple-element.33) | copy-start | bytes 2359300
  1082.5 43.5 %copy-start.33 = (bf16[256,1536]{1,0:T(8,128)(2,1)S(1)}, bf16[256,1536]{1,0:T(8,128)(2,1)}, u32[]{:S(2)}) copy-start(bf16[256,1536]{1,0:T(8,128)(2,1)} %get-tuple-element.34) | copy-start | bytes 2359300
  1083.9 43.4 %copy-start.32 = (bf16[1536,256]{1,0:T(8,128)(2,1)S(1)}, bf16[1536,256]{1,0:T(8,128)(2,1)}, u32[]{:S(2)}) copy-start(bf16[1536,256]{1,0:T(8,128)(2,1)} %get-tuple-element.35) | copy-start | bytes 2359300
  (19 other events, 42.3 us)

commit v2 on v1

--- a/solution.py
+++ b/solution.py
@@ -545,6 +545,25 @@
             self._ag(item, 1, l - t).wait_recv()
             pl.when(l <= n - 2)(lambda: self._ag(item, 1, l - t).start())
 
+    def pump(self, item, t):
+        l, n = self.l, self.n
+
+        @pl.when((l + t <= n - 1) & (l >= 1))
+        def _():
+            self._ag(item, 0, l + t).wait_recv()
+            self._ag(item, 0, l + t).start()
+
+        @pl.when((l - t >= 0) & (l <= n - 2))
+        def _():
+            self._ag(item, 1, l - t).wait_recv()
+            self._ag(item, 1, l - t).start()
+
+    def collect(self, item):
+        l, n = self.l, self.n
+        for t in range(1, n):
+            pl.when(l == 0)(lambda t=t: self._ag(item, 0, t).wait_recv())
+            pl.when(l == n - 1)(lambda t=t: self._ag(item, 1, n - 1 - t).wait_recv())
+
     def ag_end(self, item):
         l, n = self.l, self.n
         for b in range(n):
@@ -683,104 +702,470 @@
     return lax.dot_general(a, b, (((1,), (1,)), ((), ())), preferred_element_type=F32)
 
 
-def front_kernel(
-    n, x_ref, z_ref, wq, wkv, wo, x_all, z_all, g, p_send, p_recv, p_loc, ag_send, ag_recv, t_send, t_recv, t_loc
+def head_kernel(
+    n,
+    x_any,
+    z_any,
+    wq,
+    wkv,
+    wo,
+    wg,
+    wu,
+    wd,
+    small,
+    cos_ref,
+    sin_ref,
+    row_lo,
+    row_hi,
+    g_out,
+    own_out,
+    normed_out,
+    kv_out,
+    q_out,
+    qp_out,
+    kp_out,
+    gate_out,
+    att_out,
+    lse_out,
+    hidden_out,
+    inner_out,
+    dz_out,
+    small_out,
+    x_v,
+    normed,
+    g,
+    own_g,
+    small_g,
+    gain_row,
+    heads_row,
+    kv,
+    q_v,
+    qp,
+    kp,
+    gate_v,
+    att,
+    tot,
+    part,
+    core_land,
+    low,
+    chip_land,
+    inner,
+    hidden,
+    p_send,
+    p_recv,
+    p_loc,
+    ag_send,
+    ag_recv,
+    sp_sem,
+    sa_send,
+    sa_recv,
+    t_send,
+    t_recv,
+    z_send,
+    z_recv,
+    kv_send,
+    kv_recv,
+    c_send,
+    c_recv,
+    s_send,
+    s_recv,
+    i_send,
+    i_recv,
+    j_send,
+    j_recv,
+    o_loc,
 ):
     line = Line(n, g, ag_send, ag_recv)
-    pair = Pair(line, (wq, wkv, wo), p_send, p_recv, p_loc, 256)
     l, x, y, c = line.l, line.x, line.y, line.c
-    across, mate = device(l, 1 - x, y, c), device(l, x, y, 1 - c)
-    greet(line.partners() + [(across, None), (mate, None)])
+    k = y * 2 + c
+    group = Group()
+    across, mate = device(l, 1 - x, y, c), group.mate
+    right = device(l + 1, x, y, c)
+    tiny = Line(n, small_g, sa_send, sa_recv)
+    scale = HEAD_SIZE ** (-0.5)
+    late = 9
+    first = Pair(line, (wq, wkv, wo), p_send, p_recv, p_loc, 256)
+    rest = Pair(line, (wg, wu, wd), p_send, p_recv, p_loc, 768)
+
+    def swap(item):
+        if item < 3:
+            return first, item, item, 0
+        return rest, item, item % 3, item // 3 - 1
+
+    def swap_start(item):
+        pair, item, kind, j = swap(item)
+        pair.start(item, kind, j)
+
+    def swap_end(item):
+        pair, item, kind, j = swap(item)
+        pair.end(item, kind, j)
+
+    outs = []
+
+    def put(src, dst):
+        copy = pltpu.make_async_copy(src, dst, o_loc.at[len(outs)])
+        copy.start()
+        outs.append(copy)
+
+    greet(line.partners() + [(mate, None)] + [(group.chip(i), None) for i in (1, 2, 3)])
+
+    small_here = small_g.at[0, 2 * l + x]
+    small_out_copy = remote(small, small_here, sp_sem.at[0], sp_sem.at[1], across)
+    small_own = pltpu.make_async_copy(small, small_here, sp_sem.at[2])
+    small_out_copy.start()
+    small_own.start()
+    swap_start(0)
+    swap_start(1)
+    own_x = pltpu.make_async_copy(x_any, x_v.at[:, x], t_send.at[2])
+    own_x.start()
+    halves = pl.ds(2 * c, 2)
+    x_out = remote(x_any.at[halves], x_v.at[halves, x], t_send.at[0], t_recv.at[0], across)
+    x_part = x_v.at[halves, 1 - x]
+    x_on = remote(x_part, x_part, t_send.at[1], t_recv.at[1], mate)
+    x_out.start()
+    for item in range(2, 6):
+        swap_start(item)
+    z_out = remote(z_any.at[halves], dz_out.at[halves], z_send.at[0], z_recv.at[0], across)
+    z_part = dz_out.at[halves]
+    z_on = remote(z_part, z_part, z_send.at[1], z_recv.at[1], mate)
+    z_out.start()
+    for item in range(6, 12):
+        swap_start(item)
+
+    small_own.wait()
+    small_out_copy.wait()
+    tiny.ag_start(0)
     for item in range(3):
-        pair.start(item, item, 0)
-
-    def token(i, src, dst):
-        own = pltpu.make_async_copy(src, dst.at[:, x], t_loc.at[i])
-        out = remote(
-            src.at[pl.ds(2 * c, 2)], dst.at[pl.ds(2 * c, 2), x], t_send.at[i, 0], t_recv.at[i, 0], across
-        )
-        part = dst.at[pl.ds(2 * c, 2), 1 - x]
-        on = remote(part, part, t_send.at[i, 1], t_recv.at[i, 1], mate)
-        return own, out, on
-
-    tokens = [token(0, x_ref, x_all), token(1, z_ref, z_all)]
-    for own, out, on in tokens:
-        own.start()
-        out.start()
-    for item in range(3):
-        pair.end(item, item, 0)
+        swap_end(item)
         line.ag_start(item)
-    for i, (own, out, on) in enumerate(tokens):
-        out.wait_recv()
-        on.start()
     for t in range(1, n):
-        for item in range(3):
-            line.ag_step(item, t)
-    for own, out, on in tokens:
-        own.wait()
-        out.wait_send()
-        on.wait()
-    for item in range(3):
-        line.ag_end(item)
-
-
-def front(n, x_in, z_in, wq, wkv, wo):
-    b, r, d = x_in.shape
-    whole = jax.ShapeDtypeStruct((b, 2, r, d), BF)
-    return pl.pallas_call(
-        functools.partial(front_kernel, n),
-        out_shape=(whole, whole, jax.ShapeDtypeStruct((3, 2 * n, 256, 256), BF)),
-        in_specs=[ANY] * 5,
-        out_specs=(ANY, ANY, ANY),
-        scratch_shapes=[
-            DMA((3,)),
-            DMA((3,)),
-            DMA((3,)),
-            DMA((3, 2, n)),
-            DMA((3, n)),
-            DMA((2, 2)),
-            DMA((2, 2)),
-            DMA((2,)),
-        ],
-        compiler_params=pltpu.CompilerParams(collective_id=0, has_side_effects=True),
-        name="front",
-    )(x_in, z_in, wq, wkv, wo)
-
-
-def keys_kernel(n, own_ref, out_ref, send, recv, local):
-    l, x, y, c = place()
-    left, right = device(l - 1, x, y, c), device(l + 1, x, y, c)
-    greet([(left, l >= 1), (right, l <= n - 2)])
-    own = pltpu.make_async_copy(own_ref, out_ref.at[l], local)
-    own.start()
-
-    def copy(b, src):
-        return remote(src, out_ref.at[b], send.at[b], recv.at[b], right)
-
-    pl.when(l <= n - 2)(lambda: copy(l, own_ref).start())
-    for t in range(1, n):
-
+        tiny.ag_step(0, t)
+    for s in range(2 * n):
+        cols = slice(s * 256, (s + 1) * 256)
+        heads_row[:, cols] = small_g[0, s]
+        gain_row[:, cols] = small_g[0, s, 4:6, :].astype(F32)
+
+    def norm(m, side):
+        v = x_v[m, side].reshape(128, 256 * 2 * n).astype(F32)
+        mean = jnp.mean(v * v, axis=-1, keepdims=True)
+        v = v * lax.rsqrt(mean + EPS) * gain_row[0:1, :]
+        normed[m, side] = v.astype(BF)
+
+    own_x.wait()
+    each(4, lambda m: norm(m, x))
+    line.pump(0, 1)
+    line.pump(1, 1)
+    x_out.wait_recv()
+    x_on.start()
+    line.pump(0, 2)
+    line.pump(1, 2)
+    line.pump(2, 1)
+    x_on.wait_recv()
+    each(4, lambda m: norm(m, 1 - x))
+    for item in (3, 4):
+        swap_end(item)
+        line.ag_start(item)
+    for item in (0, 1):
+        line.pump(item, 3)
+        line.collect(item)
+    line.pump(2, 2)
+
+    def project(m):
+        a = normed[m].reshape(256, 256 * 2 * n)
+        qf = dot(a, g[0].reshape(256 * 2 * n, 256))
+        kf = dot(a, g[1].reshape(256 * 2 * n, 256))
+        gate_v[m] = jax.nn.sigmoid(dot_t(a, heads_row[...]))
+        qp[m] = qf
+        kp[m] = kf[:, :128]
+        cosine, sine = cos_ref[m], sin_ref[m]
+
+        def turn(u, gain):
+            u = u * lax.rsqrt(jnp.mean(u * u, axis=-1, keepdims=True) + EPS) * gain
+            return (u * cosine + pltpu.roll(u, 64, 1) * sine).astype(BF)
+
+        gains = small[8:10, :128].astype(F32)
+        q_v[m, :256] = turn(qf[:, :128], gains[0:1])
+        q_v[m, 256:] = turn(qf[:, 128:], gains[0:1])
+        kv[l, m, :, :128] = turn(kf[:, :128], gains[1:2])
+        kv[l, m, :, 128:] = kf[:, 128:].astype(BF)
+        pl.when(l <= n - 2)(lambda: send_kv(l, m).start())
+
+    def send_kv(b, m):
+        return remote(kv.at[b, m], kv.at[b, m], kv_send.at[b, m], kv_recv.at[b, m], right)
+
+    each(4, project)
+    put(normed, normed_out)
+    put(qp, qp_out)
+    put(kp, kp_out)
+    put(gate_v, gate_out)
+    put(q_v, q_out)
+
+    def attend(m, b, diagonal):
+        pair = kv[b, m]
+        raw = dot_t(q_v[m], pair[:, :128]) * scale
+        lo = row_lo[m][:, :1] - b * 256
+        hi = row_hi[m][:, :1] - b * 256
+        column = lax.broadcasted_iota(jnp.int32, (512, 256), 1)
+        allowed = (column >= jnp.concatenate([lo, lo], axis=0)) & (
+            column < jnp.concatenate([hi, hi], axis=0)
+        )
+        e = jnp.where(allowed, jnp.exp(raw), 0.0)
+        total = jnp.sum(e, axis=-1, keepdims=True)
+        value = dot(e.astype(BF), pair[:, 128:])
+        total = jnp.broadcast_to(total, (512, 128))
+        if diagonal:
+            tot[m] = total
+            att[m] = value
+        else:
+            tot[m] += total
+            att[m] += value
+
+    def kv_round(t):
         @pl.when(l - t >= 0)
         def _():
             b = l - t
-            copy(b, out_ref.at[b]).wait_recv()
-            pl.when(l <= n - 2)(lambda: copy(b, out_ref.at[b]).start())
-
-    for b in range(n):
-        pl.when((l >= b) & (l <= n - 2))(lambda b=b: copy(b, out_ref.at[b]).wait_send())
-    own.wait()
-
-
-def keys_forward(n, own):
+
+            def take(m):
+                send_kv(b, m).wait_recv()
+                pl.when(l <= n - 2)(lambda: send_kv(b, m).start())
+
+            each(4, take)
+            each(4, lambda m: attend(m, b, False))
+
+    line.pump(2, 3)
+    each(4, lambda m: attend(m, l, True))
+    line.pump(3, 1)
+    line.pump(4, 1)
+    kv_round(1)
+    for item in (5,):
+        swap_end(item)
+        line.ag_start(item)
+    line.pump(3, 2)
+    line.pump(4, 2)
+    line.pump(3, 3)
+    kv_round(2)
+    swap_end(6)
+    line.ag_start(6)
+    line.pump(4, 3)
+    line.pump(5, 1)
+    line.pump(5, 2)
+    kv_round(3)
+    line.collect(2)
+
+    def mate_copy(m):
+        return remote(
+            part.at[m, :, :, 1 - c], core_land.at[m], c_send.at[m], c_recv.at[m], mate
+        )
+
+    def branch(m):
+        total = tot[m]
+        lse = jnp.log(total)
+        value = att[m] / total
+        att[m] = value
+        tot[m] = lse
+        gates = gate_v[m]
+        lo, hi = gates[:, 0:2], gates[:, 2:4]
+        gates = jnp.where(x == 0, lo, hi)
+        mixed = jnp.concatenate(
+            [value[:256] * gates[:, 0:1], value[256:] * gates[:, 1:2]], axis=1
+        ).astype(BF)
+        for s in range(2 * n):
+            part[m, :, :, :, :, s * 256 : (s + 1) * 256] = (
+                dot(mixed, g[2, s]).astype(BF).reshape(2, 2, 2, 32, 256)
+            )
+        mate_copy(m).start()
+
+    each(4, branch)
+    put(att, att_out)
+    put(tot, lse_out)
+    put(kv, kv_out)
+    swap_end(7)
+    line.ag_start(7)
+    line.pump(5, 3)
+    line.pump(6, 1)
+
+    def chip_copy(m, o):
+        ox, oy = group.other(o)
+        return remote(
+            low.at[m, ox, oy],
+            chip_land.at[o - 1, m],
+            s_send.at[m, o - 1],
+            s_recv.at[m, o - 1],
+            group.chip(o),
+        )
+
+    def to_chips(m):
+        mate_copy(m).wait_recv()
+        for u in range(2):
+            for v in range(2):
+                low[m, u, v] = (
+                    part[m, u, v, c].astype(F32) + core_land[m, u, v].astype(F32)
+                ).astype(BF)
+        for o in (3, 1, 2):
+            chip_copy(m, o).start()
+
+    each(4, to_chips)
+    line.pump(6, 2)
+    swap_end(8)
+    line.ag_start(8)
+    line.pump(6, 3)
+    line.pump(7, 1)
+
+    def inner_copy(m, o):
+        here = inner.at[m, x, y, c]
+        return remote(
+            here, here, i_send.at[m, o - 1], i_recv.at[m, o - 1], group.chip(o)
+        )
+
+    def inner_mate(m, o):
+        ox, oy = group.other(o)
+        there = inner.at[m, ox, oy, c]
+        return remote(there, there, j_send.at[m, o], j_recv.at[m, o], mate)
+
+    def finish(m):
+        total = low[m, x, y].astype(F32)
+        for o in (1, 2, 3):
+            chip_copy(m, o).wait_recv()
+            total = total + chip_land[o - 1, m].astype(F32)
+        h = x_v[m, x, k].astype(F32) + total
+        hidden[m] = h
+        mean = jnp.mean(h * h, axis=-1, keepdims=True)
+        inner[m, x, y, c] = (h * lax.rsqrt(mean + EPS) * gain_row[1:2, :]).astype(BF)
+        for o in (3, 1, 2):
+            inner_copy(m, o).start()
+        inner_mate(m, 0).start()
+
+    each(4, finish)
+    put(hidden, hidden_out)
+    line.pump(7, 2)
+    line.pump(7, 3)
+    line.pump(8, 1)
+    z_out.wait_recv()
+    z_on.start()
+
+    def pass_on(m):
+        for o in (1, 2, 3):
+            inner_copy(m, o).wait_recv()
+            inner_mate(m, o).start()
+
+    each(4, pass_on)
+    line.pump(8, 2)
+    for item in (9, 10, 11):
+        swap_end(item)
+        put(g.at[item, pl.ds(2 * l, 2)], own_out.at[item - 9])
+    line.pump(8, 3)
+
+    def arrive(m):
+        for o in range(4):
+            inner_mate(m, o).wait_recv()
+
+    each(4, arrive)
+    put(inner, inner_out)
+    put(small_g, small_out)
+    for item in range(3, 9):
+        line.collect(item)
+    put(g.at[pl.ds(0, 9)], g_out)
+
+    small_out_copy_done = None
+    own_waits = [x_out, x_on, z_out, z_on]
+    for copy in own_waits:
+        copy.wait_send()
+    z_on.wait_recv()
+    tiny.ag_end(0)
+    each(9, line.ag_end)
+
+    def drain(m):
+        mate_copy(m).wait_send()
+        for o in (1, 2, 3):
+            chip_copy(m, o).wait_send()
+            inner_copy(m, o).wait_send()
+        for o in range(4):
+            inner_mate(m, o).wait_send()
+        for b in range(n):
+            pl.when((l >= b) & (l <= n - 2))(lambda b=b: send_kv(b, m).wait_send())
+
+    each(4, drain)
+    for copy in outs:
+        copy.wait()
+
+
+def head(n, x_in, z_in, wq, wkv, wo, wg, wu, wd, small, cosine, sine, row_lo, row_hi):
+    d = x_in.shape[-1]
+    m = 2 * n
+    bf = lambda *shape: jax.ShapeDtypeStruct(shape, BF)
+    f32 = lambda *shape: jax.ShapeDtypeStruct(shape, F32)
+    vb = lambda *shape: pltpu.VMEM(shape, BF)
+    vf = lambda *shape: pltpu.VMEM(shape, F32)
     return pl.pallas_call(
-        functools.partial(keys_kernel, n),
-        out_shape=jax.ShapeDtypeStruct((n,) + own.shape, BF),
-        in_specs=[VM],
-        out_specs=ANY,
-        scratch_shapes=[DMA((n,)), DMA((n,)), DMA],
-        compiler_params=pltpu.CompilerParams(collective_id=1, has_side_effects=True),
-        name="keys",
-    )(own)
+        functools.partial(head_kernel, n),
+        out_shape=(
+            bf(9, m, 256, 256),
+            bf(3, 2, 256, 256),
+            bf(4, 2, 128, d),
+            bf(n, 4, 256, 256),
+            bf(4, 512, 128),
+            f32(4, 256, 256),
+            f32(4, 256, 128),
+            f32(4, 256, 16),
+            f32(4, 512, 128),
+            f32(4, 512, 128),
+            f32(4, 32, d),
+            bf(4, 2, 2, 2, 32, d),
+            bf(4, 4, 32, d),
+            bf(1, m, 16, 256),
+        ),
+        in_specs=[ANY] * 8 + [VM] * 5,
+        out_specs=(ANY,) * 14,
+        scratch_shapes=[
+            vb(4, 2, 4, 32, d),
+            vb(4, 2, 128, d),
+            vb(12, m, 256, 256),
+            vb(1, 16, 128),
+            vb(1, m, 16, 256),
+            vf(2, d),
+            vb(16, d),
+            vb(n, 4, 256, 256),
+            vb(4, 512, 128),
+            vf(4, 256, 256),
+            vf(4, 256, 128),
+            vf(4, 256, 16),
+            vf(4, 512, 128),
+            vf(4, 512, 128),
+            vb(4, 2, 2, 2, 32, d),
+            vb(4, 2, 2, 32, d),
+            vb(4, 2, 2, 32, d),
+            vb(3, 4, 32, d),
+            vb(4, 2, 2, 2, 32, d),
+            vf(4, 32, d),
+            DMA((12,)),
+            DMA((12,)),
+            DMA((12,)),
+            DMA((12, 2, n)),
+            DMA((12, n)),
+            DMA((3,)),
+            DMA((1, 2, n)),
+            DMA((1, n)),
+            DMA((3,)),
+            DMA((2,)),
+            DMA((2,)),
+            DMA((2,)),
+            DMA((n, 4)),
+            DMA((n, 4)),
+            DMA((4,)),
+            DMA((4,)),
+            DMA((4, 3)),
+            DMA((4, 3)),
+            DMA((4, 3)),
+            DMA((4, 3)),
+            DMA((4, 4)),
+            DMA((4, 4)),
+            DMA((16,)),
+        ],
+        compiler_params=pltpu.CompilerParams(
+            collective_id=0, has_side_effects=True, vmem_limit_bytes=62 * 2**20
+        ),
+        name="head",
+    )(x_in, z_in, wq, wkv, wo, wg, wu, wd, small, cosine, sine, row_lo, row_hi)
 
 
 def keys_back_kernel(n, part_ref, out_ref, work, land, send, recv, local):
@@ -1000,63 +1385,76 @@
     )(own)
 
 
-def rows_kernel(n, part_ref, dq, dkv, do, g, land, rs_send, rs_recv, b_send, b_recv, b_loc, local):
+def rows_kernel(
+    n, part_ref, ffn_ref, dq, dkv, do, dg, du, dd, g, land, rs_send, rs_recv, b_send, b_recv, b_loc, local
+):
     line = Line(n, g, None, None, land, rs_send, rs_recv)
-    back = Back(line, (dq, dkv, do), b_send, b_recv, b_loc, 256)
-    greet(line.partners() + [back.partner()])
-    load = pltpu.make_async_copy(part_ref, g, local)
-    load.start()
-    load.wait()
+    small = Back(line, (dq, dkv, do), b_send, b_recv, b_loc, 256)
+    large = Back(line, (dg, du, dd), b_send, b_recv, b_loc, 512)
+    greet(line.partners() + [small.partner()])
+    loads = [
+        pltpu.make_async_copy(ffn_ref, g.at[pl.ds(3, 6)], local.at[1]),
+        pltpu.make_async_copy(part_ref, g.at[pl.ds(0, 3)], local.at[0]),
+    ]
+    for load in loads:
+        load.start()
+    for load in loads:
+        load.wait()
     for q in range(1, n):
-        each(3, lambda item, q=q: line.rs_step(item, q))
-    each(3, line.rs_final)
-    for item in range(3):
-        back.start(item, item, 0)
-    for item in range(3):
-        back_wait(back, item, item, 0)
-    each(3, line.rs_end)
-
-
-def rows_sum(n, parts):
+        each(9, lambda item, q=q: line.rs_step(item, q))
+    each(9, line.rs_final)
+    for item in range(9):
+        if item < 3:
+            small.start(item, item, 0)
+        else:
+            large.start(item, item % 3, item // 3 - 1)
+    for item in range(9):
+        if item < 3:
+            back_wait(small, item, item, 0)
+        else:
+            back_wait(large, item, item % 3, item // 3 - 1)
+    each(9, line.rs_end)
+
+
+def rows_sum(n, parts, ffn_parts):
+    bf = lambda *shape: jax.ShapeDtypeStruct(shape, BF)
     return pl.pallas_call(
         functools.partial(rows_kernel, n),
-        out_shape=(
-            jax.ShapeDtypeStruct((256, 512), BF),
-            jax.ShapeDtypeStruct((256, 512), BF),
-            jax.ShapeDtypeStruct((512, 256), BF),
-        ),
-        in_specs=[ANY],
-        out_specs=(ANY, ANY, ANY),
+        out_shape=(bf(256, 512), bf(256, 512), bf(512, 256), bf(256, 1024), bf(256, 1024), bf(1024, 256)),
+        in_specs=[ANY] * 2,
+        out_specs=(ANY,) * 6,
         scratch_shapes=[
-            pltpu.VMEM((3, 2 * n, 256, 256), BF),
-            pltpu.VMEM((3, 2 * n + 2, 256, 256), BF),
-            DMA((3, 2, n)),
-            DMA((3, n + 1)),
-            DMA((3,)),
-            DMA((3,)),
-            DMA((3,)),
-            DMA,
+            pltpu.VMEM((9, 2 * n, 256, 256), BF),
+            pltpu.VMEM((9, 2 * n + 2, 256, 256), BF),
+            DMA((9, 2, n)),
+            DMA((9, n + 1)),
+            DMA((9,)),
+            DMA((9,)),
+            DMA((9,)),
+            DMA((2,)),
         ],
         compiler_params=pltpu.CompilerParams(
             collective_id=8, has_side_effects=True, vmem_limit_bytes=40 * 2**20
         ),
         name="rows_sum",
-    )(parts)
+    )(parts, ffn_parts)
 
 
 def ffn_kernel(
     n,
-    chunks,
-    inner_ref,
-    dz_ref,
-    wg,
-    wu,
-    wd,
+    inner_any,
+    z_own,
+    z_other,
+    g_in,
+    own_in,
     out_ref,
     din_ref,
+    part_out,
     dgw,
     duw,
     ddw,
+    inner_ref,
+    dz_ref,
     inner_t,
     out_acc,
     din_acc,
@@ -1064,9 +1462,6 @@
     land,
     low,
     prod_t,
-    p_send,
-    p_recv,
-    p_loc,
     ag_send,
     ag_recv,
     rs_send,
@@ -1074,17 +1469,30 @@
     b_send,
     b_recv,
     b_loc,
+    in_loc,
     o_loc,
 ):
+    chunks = 3
     line = Line(n, g, ag_send, ag_recv, land, rs_send, rs_recv)
-    half = chunks * 256
-    pair = Pair(line, (wg, wu, wd), p_send, p_recv, p_loc, half)
-    back = Back(line, (dgw, duw, ddw), b_send, b_recv, b_loc, half)
-    greet(line.partners() + [pair.partner()])
+    l, x = line.l, line.x
     blocks = 2 * n
-    for j in range(chunks):
-        for kind in range(3):
-            pair.start(3 * j + kind, kind, j)
+    width = blocks * 256
+    back = Back(line, (dgw, duw, ddw), b_send, b_recv, b_loc, 256)
+    loads = [
+        pltpu.make_async_copy(own_in, g.at[pl.ds(6, 3), pl.ds(2 * l, 2)], in_loc.at[0]),
+        pltpu.make_async_copy(inner_any, inner_ref, in_loc.at[1]),
+        pltpu.make_async_copy(z_own, dz_ref.at[:, x], in_loc.at[2]),
+        pltpu.make_async_copy(z_other, dz_ref.at[:, 1 - x], in_loc.at[3]),
+        pltpu.make_async_copy(g_in.at[pl.ds(3, 6)], g.at[pl.ds(0, 6)], in_loc.at[4]),
+    ]
+    for copy in loads:
+        copy.start()
+    greet(line.partners() + [back.partner()])
+    loads[0].wait()
+    for item in range(6, 9):
+        line.ag_start(item)
+    for copy in loads[1:]:
+        copy.wait()
 
     def turn(i, unused):
         m, s = lax.div(i, blocks), lax.rem(i, blocks)
@@ -1092,10 +1500,6 @@
         inner_t[s, :, pl.ds(pl.multiple_of(m * 256, 256), 256)] = tile.T
         return 0
 
-    for j in range(chunks):
-        for kind in range(3):
-            pair.end(3 * j + kind, kind, j)
-            line.ag_start(3 * j + kind)
     lax.fori_loop(0, 4 * blocks, turn, 0)
 
     def compute(j):
@@ -1103,9 +1507,9 @@
 
         def rows(m, unused):
             a = inner_ref[m]
-            d = dz_ref[m]
-            gated = dot(a, g[base].reshape(blocks * 256, 256))
-            upward = dot(a, g[base + 1].reshape(blocks * 256, 256))
+            d = dz_ref[m].reshape(256, width)
+            gated = dot(a, g[base].reshape(width, 256))
+            upward = dot(a, g[base + 1].reshape(width, 256))
             grad = dot_t(d[:, :256], g[base + 2, 0])
             for s in range(1, blocks):
                 grad = grad + dot_t(d[:, s * 256 : (s + 1) * 256], g[base + 2, s])
@@ -1136,7 +1540,7 @@
             t = inner_t[s]
             g[base, s] = dot(t, low[0]).astype(BF)
             g[base + 1, s] = dot(t, low[1]).astype(BF)
-            z = dz_ref[:, :, pl.ds(pl.multiple_of(s * 256, 256), 256)].reshape(1024, 256)
+            z = dz_ref[:, :, :, :, pl.ds(pl.multiple_of(s * 256, 256), 256)].reshape(1024, 256)
             g[base + 2, s] = dot(prod_t[...], z).astype(BF)
             return 0
 
@@ -1145,101 +1549,91 @@
     def items(j, body):
         each(3, lambda i: body(3 * j + i))
 
-    for j in range(chunks):
-        for t in range(1, n):
-            items(j, lambda item, t=t: line.ag_step(item, t))
-            if j > 0:
-                items(j - 1, lambda item, t=t: line.rs_step(item, t))
-        items(j, line.ag_end)
-        compute(j)
-        if j > 0:
-            items(j - 1, line.rs_final)
-            for kind in range(3):
-                back.start(3 * j - 3 + kind, kind, j - 1)
-    last = chunks - 1
+    compute(0)
+    for t in range(1, n):
+        items(2, lambda item, t=t: line.pump(item, t))
+        items(0, lambda item, t=t: line.rs_step(item, t))
+    compute(1)
+    items(0, line.rs_final)
+    for kind in range(3):
+        back.start(kind, kind, 0)
+    items(2, line.collect)
+    items(2, line.ag_end)
+    compute(2)
+    parts = pltpu.make_async_copy(g.at[pl.ds(3, 6)], part_out, o_loc.at[2])
+    parts.start()
 
     def flush(m, unused):
         inner_ref[m] = out_acc[m].astype(BF)
-        dz_ref[m] = din_acc[m].astype(BF)
+        dz_ref[m] = din_acc[m].astype(BF).reshape(2, 4, 32, width)
         return 0
 
-    for t in range(1, n):
-        items(last, lambda item, t=t: line.rs_step(item, t))
     lax.fori_loop(0, 4, flush, 0)
     outs = [
         pltpu.make_async_copy(inner_ref, out_ref, o_loc.at[0]),
         pltpu.make_async_copy(dz_ref, din_ref, o_loc.at[1]),
+        parts,
     ]
-    for copy in outs:
+    for copy in outs[:2]:
         copy.start()
-    items(last, line.rs_final)
     for kind in range(3):
-        back.start(3 * last + kind, kind, last)
-    for j in range(chunks):
-        for kind in range(3):
-            back_wait(back, 3 * j + kind, kind, j)
-    for j in range(chunks):
-        items(j, line.rs_end)
+        back_wait(back, kind, kind, 0)
+    items(0, line.rs_end)
     for copy in outs:
         copy.wait()
 
 
-def ffn(n, inner, dz, wg, wu, wd):
-    d, hid = wg.shape[0] * 2 * n, wg.shape[1]
-    chunks = hid // 512
-    items = 3 * chunks
-    tokens = jax.ShapeDtypeStruct((4, 256, d), BF)
+def ffn(n, inner, z_own, z_other, g_in, own_in):
+    d = inner.shape[-1]
+    m = 2 * n
+    bf = lambda *shape: jax.ShapeDtypeStruct(shape, BF)
+    vb = lambda *shape: pltpu.VMEM(shape, BF)
     return pl.pallas_call(
-        lambda inner_any, dz_any, *rest: ffn_load(n, chunks, inner_any, dz_any, *rest),
+        functools.partial(ffn_kernel, n),
         out_shape=(
-            tokens,
-            tokens,
-            jax.ShapeDtypeStruct(wg.shape, BF),
-            jax.ShapeDtypeStruct(wu.shape, BF),
-            jax.ShapeDtypeStruct(wd.shape, BF),
+            bf(4, 256, d),
+            bf(4, 2, 4, 32, d),
+            bf(6, m, 256, 256),
+            bf(256, 512),
+            bf(256, 512),
+            bf(512, 256),
         ),
         in_specs=[ANY] * 5,
-        out_specs=(ANY,) * 5,
+        out_specs=(ANY,) * 6,
         scratch_shapes=[
-            pltpu.VMEM((4, 256, d), BF),
-            pltpu.VMEM((4, 256, d), BF),
-            DMA((2,)),
-            pltpu.VMEM((2 * n, 256, 1024), BF),
+            vb(4, 256, d),
+            vb(4, 2, 4, 32, d),
+            vb(m, 256, 1024),
             pltpu.VMEM((4, 256, d), F32),
             pltpu.VMEM((4, 256, d), F32),
-            pltpu.VMEM((items, 2 * n, 256, 256), BF),
-            pltpu.VMEM((items, 2 * n + 2, 256, 256), BF),
-            pltpu.VMEM((2, 1024, 256), BF),
-            pltpu.VMEM((256, 1024), BF),
-            DMA((items,)),
-            DMA((items,)),
-            DMA((items,)),
-            DMA((items, 2, n)),
-            DMA((items, n)),
-            DMA((items, 2, n)),
-            DMA((items, n + 1)),
-            DMA((items,)),
-            DMA((items,)),
-            DMA((items,)),
-            DMA((2,)),
+            vb(9, m, 256, 256),
+            vb(3, m + 2, 256, 256),
+            vb(2, 1024, 256),
+            vb(256, 1024),
+            DMA((9, 2, n)),
+            DMA((9, n)),
+            DMA((3, 2, n)),
+            DMA((3, n + 1)),
+            DMA((3,)),
+            DMA((3,)),
+            DMA((3,)),
+            DMA((5,)),
+            DMA((3,)),
         ],
         compiler_params=pltpu.CompilerParams(
             collective_id=9, has_side_effects=True, vmem_limit_bytes=62 * 2**20
         ),
         name="ffn",
-    )(inner, dz, wg, wu, wd)
-
-
-def ffn_load(n, chunks, inner_any, dz_any, wg, wu, wd, out, din, dgw, duw, ddw, inner_v, dz_v, in_loc, *rest):
-    loads = [
-        pltpu.make_async_copy(inner_any, inner_v, in_loc.at[0]),
-        pltpu.make_async_copy(dz_any, dz_v, in_loc.at[1]),
-    ]
-    for copy in loads:
-        copy.start()
-    for copy in loads:
-        copy.wait()
-    ffn_kernel(n, chunks, inner_v, dz_v, wg, wu, wd, out, din, dgw, duw, ddw, *rest)
+    )(inner, z_own, z_other, g_in, own_in)
+
+
+def row_layout(index, buckets, lengths):
+    ends = jnp.cumsum(buckets)
+    starts = ends - buckets
+    member = (index[:, None] >= starts[None, :]) & (index[:, None] < ends[None, :])
+    position = index - jnp.sum(jnp.where(member, starts[None, :], 0), axis=1)
+    limit = jnp.sum(jnp.where(member, lengths[None, :], 0), axis=1)
+    return (None, position, limit)
 
 
 def fast_local(
@@ -1269,90 +1663,105 @@
     gain_query = query_gain.astype(F32)
     gain_key = key_gain.astype(F32)
 
-    small = jnp.concatenate(
-        [headgate_weight.T, attention_gain[None], feedforward_gain[None]], axis=0
-    )
-    small = lax.all_gather(small, "seq", axis=1, tiled=True)
+    own_small = jnp.concatenate(
+        [
+            headgate_weight.T,
+            attention_gain[None],
+            feedforward_gain[None],
+            jnp.zeros((2, 256), BF),
+            jnp.pad(jnp.stack([query_gain, key_gain]), ((0, 0), (0, 128))),
+            jnp.zeros((6, 256), BF),
+        ],
+        axis=0,
+    )
+    paired = jnp.concatenate(
+        [key_matrix[:, :128], value_matrix[:, :128], key_matrix[:, 128:], value_matrix[:, 128:]],
+        axis=1,
+    )
+
+    def own_rows(values):
+        return lax.dynamic_slice_in_dim(values, kv * 32, 32, 1)
+
+    row_index = l * span + jnp.arange(span, dtype=jnp.int32)
+    key_index = jnp.arange(n * span, dtype=jnp.int32)
+    layouts = [row_layout(row_index, bucket_sizes[b], true_lengths[b]) for b in range(batches)]
+    positions = jnp.concatenate([item[1] for item in layouts])
+    row_lo = jnp.stack([row_index - item[1] for item in layouts])
+    limits = jnp.stack([item[2] for item in layouts])
+    row_hi = jnp.minimum(row_index + 1, row_lo + limits)
+    allowed = (
+        (key_index[None, None, :] >= row_lo[:, :, None])
+        & (key_index[None, None, :] < row_hi[:, :, None])
+    )[:, None]
+    cosine, sine = rope_tables(positions, HEAD_SIZE)
+    signed = sine * jnp.where(jnp.arange(HEAD_SIZE) < HEAD_SIZE // 2, -1.0, 1.0)
+    (
+        g_all,
+        g_own,
+        normed,
+        all_keys,
+        query,
+        query_proj,
+        key_proj,
+        gate,
+        attended,
+        log_total,
+        hidden,
+        inner,
+        z_other,
+        small,
+    ) = head(
+        n,
+        inputs.reshape(batches, 4, 32, width),
+        cotangent.reshape(batches, 4, 32, width),
+        query_weight,
+        paired,
+        output_weight,
+        gate_weight,
+        up_weight,
+        down_weight,
+        own_small,
+        cosine.reshape(batches, span, HEAD_SIZE),
+        signed.reshape(batches, span, HEAD_SIZE),
+        jnp.broadcast_to(row_lo[:, :, None], (batches, span, 128)),
+        jnp.broadcast_to(row_hi[:, :, None], (batches, span, 128)),
+    )
+    small = small[0].transpose(1, 0, 2).reshape(16, width)
     w_head = lax.dynamic_slice_in_dim(small, x * 2, 2, 0)
     gain_a = small[4].astype(F32)
     gain_f = small[5].astype(F32)
-    paired = jnp.concatenate(
-        [key_matrix[:, :128], value_matrix[:, :128], key_matrix[:, 128:], value_matrix[:, 128:]],
-        axis=1,
-    )
-    x_all, z_all, g = front(n, inputs, cotangent, query_weight, paired, output_weight)
-    w_query = g[0].reshape(width, 256)
-    w_keys = g[1].reshape(width, 256)
-    w_output = g[2]
-
-    def own_rows(values):
-        return lax.dynamic_slice_in_dim(values, kv * 32, 32, 1)
-
-    row_index = l * span + jnp.arange(span, dtype=jnp.int32)
-    key_index = jnp.arange(n * span, dtype=jnp.int32)
-    layouts = [token_layout(row_index, bucket_sizes[b], true_lengths[b]) for b in range(batches)]
-    key_layouts = [
-        token_layout(key_index, bucket_sizes[b], true_lengths[b]) for b in range(batches)
-    ]
-    positions = jnp.concatenate([item[1] for item in layouts])
-    allowed = jnp.stack(
-        [
-            (mine[0][:, None] == theirs[0][None, :])
-            & (key_index[None, :] <= row_index[:, None])
-            & theirs[2][None, :]
-            for mine, theirs in zip(layouts, key_layouts)
-        ]
-    )[:, None]
-    cosine, sine = rope_tables(positions, HEAD_SIZE)
-
-    current = x_all.reshape(batches * span, width).astype(F32)
-    normed = (current * rms_scale(current) * gain_a).astype(BF)
-    query_proj = jnp.dot(normed, w_query, preferred_element_type=F32).reshape(-1, 2, HEAD_SIZE)
-    keys_proj = jnp.dot(normed, w_keys, preferred_element_type=F32)
-    key_proj = keys_proj[:, :HEAD_SIZE].reshape(-1, 1, HEAD_SIZE)
-    value_low = keys_proj[:, HEAD_SIZE:].astype(BF)
+    w_query = g_all[0].reshape(width, 256)
+    w_keys = g_all[1].reshape(width, 256)
+    w_output = g_all[2]
+    normed = normed.reshape(batches * span, width)
+    query_proj = query_proj.reshape(-1, 2, HEAD_SIZE)
+    key_proj = key_proj.reshape(-1, 1, HEAD_SIZE)
     query_scale = rms_scale(query_proj)
     query_normal = query_proj * query_scale
     key_scale = rms_scale(key_proj)
     key_normal = key_proj * key_scale
-    query_rot = rotate_forward(query_normal * gain_query, cosine, sine).astype(BF)
-    key_rot = rotate_forward(key_normal * gain_key, cosine, sine).astype(BF)
-    gate = jax.nn.sigmoid(times_transpose(normed, w_head))
-    own_keys = jnp.concatenate([key_rot.reshape(-1, HEAD_SIZE), value_low], axis=1)
-    all_keys = keys_forward(n, own_keys).reshape(n, batches, span, 256)
+    gate = lax.dynamic_slice_in_dim(gate, x * 2, 2, 2)
     seen = (jnp.arange(n) <= l)[:, None, None, None]
     all_keys = jnp.where(seen, all_keys, 0).transpose(1, 0, 2, 3).reshape(batches, n * span, 256)
     keys, values = all_keys[..., :HEAD_SIZE], all_keys[..., HEAD_SIZE:]
-    query = query_rot.reshape(batches, span, 2, HEAD_SIZE).transpose(0, 2, 1, 3)
-
-    def weights_of(log_total=None):
-        raw = jnp.einsum("bhtd,bsd->bhts", query, keys, preferred_element_type=F32) * scale
-        if log_total is None:
-            return jnp.where(allowed, jnp.exp(raw), 0.0)
-        return jnp.where(allowed, jnp.exp(raw - log_total), 0.0)
-
-    spread = weights_of()
-    log_total = jnp.log(jnp.sum(spread, axis=-1, keepdims=True))
-    weights = weights_of(log_total)
-    attended = jnp.einsum("bhts,bsd->bhtd", weights.astype(BF), values, preferred_element_type=F32)
-    gate_heads = gate.reshape(batches, span, 2).transpose(0, 2, 1)[..., None]
+    query = query.reshape(batches, 2, span, HEAD_SIZE)
+    attended = attended.reshape(batches, 2, span, HEAD_SIZE)
+    log_total = log_total[..., :1].reshape(batches, 2, span, 1)
+    raw = jnp.einsum("bhtd,bsd->bhts", query, keys, preferred_element_type=F32) * scale
+    weights = jnp.where(allowed, jnp.exp(raw - log_total), 0.0)
+    gate_heads = gate.transpose(0, 2, 1)[..., None]
     mixed = (attended * gate_heads).astype(BF).transpose(0, 2, 1, 3).reshape(-1, 256)
-    branch = jnp.concatenate(
-        [jnp.dot(mixed, w_output[s], preferred_element_type=F32) for s in range(2 * n)], axis=1
-    ).astype(BF)
     split = (batches, 2, 2, 2, 32, width)
     own_x = own_rows(inputs).astype(F32)
-    hidden = own_x + group_sum(branch.reshape((1,) + split), 3)[0]
     scale_f = rms_scale(hidden)
     normal_f = hidden * scale_f
-    inner = group_spread((normal_f * gain_f).astype(BF), 4)
-    out_part, din_part, d_gate, d_up, d_down = ffn(
+    out_part, din_part, ffn_parts, d_gate, d_up, d_down = ffn(
         n,
         inner.reshape(batches, span, width),
-        z_all.reshape(batches, span, width),
-        gate_weight,
-        up_weight,
-        down_weight,
+        cotangent.reshape(batches, 4, 32, width),
+        z_other,
+        g_all,
+        g_own,
     )
     sums = group_sum(jnp.stack([out_part.reshape(split), din_part.reshape(split)]), 5)
     own_out = (hidden + sums[0]).astype(BF)
@@ -1413,7 +1822,9 @@
         + jnp.dot(logits_low, w_head, preferred_element_type=F32)
     ).astype(BF)
     grad_normed = group_sum(grad_partial.reshape((1,) + split), 10)[0]
-    dq, dkv, do = rows_sum(n, jnp.stack([d_query_weight, d_pair_weight, d_output]))
+    dq, dkv, do, d_gate2, d_up2, d_down2 = rows_sum(
+        n, jnp.stack([d_query_weight, d_pair_weight, d_output]), ffn_parts
+    )
     scale_a = rms_scale(own_x)
     normal_a = own_x * scale_a
     sum_attention_gain = jnp.sum(grad_normed * normal_a, axis=(0, 1))
@@ -1425,6 +1836,11 @@
     )
     head_total = lax.psum(d_head, "seq")
     own_width = width // (2 * n)
+
+    def joined(first, rest, axis):
+        a, b = jnp.split(first.astype(F32), 2, axis=axis)
+        c, d = jnp.split(rest.astype(F32), 2, axis=axis)
+        return jnp.concatenate([a, c, b, d], axis=axis)
 
     def cut(values):
         return lax.dynamic_slice_in_dim(values, seq * own_width, own_width, values.ndim - 1)
@@ -1441,9 +1857,9 @@
         jnp.concatenate([dkv[:, 128:256], dkv[:, 384:]], axis=1).astype(F32),
         cut(head_total).T,
         do.astype(F32),
-        d_gate.astype(F32),
-        d_up.astype(F32),
-        d_down.astype(F32),
+        joined(d_gate, d_gate2, 1),
+        joined(d_up, d_up2, 1),
+        joined(d_down, d_down2, 0),
     )
 
 

time: 1140 us -> 928 us (0.81)
  Pallas kernels: 849 us -> 677 us
  matrix products: 71.5 us -> 49.6 us
    pallas_call x4 -> x3, Pallas kernels: 577 us -> 475 us  [the longest x1 192 us: head(): pl.pallas_call(functools.partial(head_kernel, n), out_shape=(bf(9, m, 256...]
    pallas_call x2 -> x1, Pallas kernels: 62.7 us -> 30.1 us  [group_spread(): pl.pallas_call(spread_kernel, out_shape=jax.ShapeDtypeStruct((b, 2, 2, 2,...]
    all_gather x1 -> x0, blocking collectives: 32.2 us -> none  [fast_local(): small = lax.all_gather(small, 'seq', axis=1, tiled=True)]
    pallas_call x3 -> x2, Pallas kernels: 115 us -> 86.4 us  [group_sum(): pl.pallas_call(functools.partial(sum_kernel, m), out_shape=jax.ShapeDtype...]
    psum x1, blocking collectives: 38.9 us -> 64.4 us  [fast_local(): lax.psum(jnp.concatenate([sum_attention_gain, sum_feedforward_gain, sum_q...]
    dot_general x11 -> x1, matrix products: 22.4 us -> 4.57 us  [fast_local(): jnp.einsum('bhtd,bsd->bhts', query, keys, preferred_element_type=F32)]
    convert_element_type x8 -> x2, other arithmetic: 15.7 us -> 1.42 us  [the longest x1 1.4 us: fast_local(): grad_logits = (jnp.sum(grad_mixed * attended, axis=-1, keepdims=True) * g...]
where the time goes in v2:
time: 928 us; the launch traced here: 921 us
  Pallas kernels  677 us (73%)
  blocking collectives  101 us (11%)
  other arithmetic  56.8 us (6%)
  matrix products  49.6 us (5%)
  local copies, waits for them, and re-layouts  34.8 us (4%)
    pallas_call x1, Pallas kernels, head(): pl.pallas_call(functools.partial(head_kernel, n), out_shape=(bf(9, m, 256...  192 us
    pallas_call x1, Pallas kernels, rows_sum(): pl.pallas_call(functools.partial(rows_kernel, n), out_shape=(bf(256, 512)...  154 us
    pallas_call x1, Pallas kernels, ffn(): pl.pallas_call(functools.partial(ffn_kernel, n), out_shape=(bf(4, 256, d)...  130 us
    pallas_call x2, Pallas kernels, group_sum(): pl.pallas_call(functools.partial(sum_kernel, m), out_shape=jax.ShapeDtype...  86.4 us
    psum x1, blocking collectives, fast_local(): lax.psum(jnp.concatenate([sum_attention_gain, sum_feedforward_gain, sum_q...  64.4 us
    pallas_call x1, Pallas kernels, home(): pl.pallas_call(home_kernel, out_shape=jax.ShapeDtypeStruct((m, b, 2, 2, r...  49.8 us
    psum x1, blocking collectives, fast_local(): head_total = lax.psum(d_head, 'seq')  36.1 us
    pallas_call x1, Pallas kernels, keys_back(): pl.pallas_call(functools.partial(keys_back_kernel, n), out_shape=jax.Shap...  35.5 us

profile of v2, /device:TPU:0, one launch (start us, length us, event | category | flops | bytes accessed | tf_op | source)
XLA Modules:
  0.0 920.8 jit_solution(5799759596232836194)
XLA Ops:
  3.4 4.1 multiply_cosine_fusion.1
  13.6 191.7 %head.1 = (bf16[9,8,256,256]{3,2,1,0:T(8,128)(2,1)}, bf16[3,2,256,256]{3,2,1,0:T(8,128)(2,1)}, bf16[4,2,128,2048]{3,2,1,0:T(8,128)(2,1)}, bf16[4,4,256,256]{3,2,...) custom-call(bf16[4,4,32,2048]{3,2,1,0:T(8,128)(2,1)} %bitcast.325, ...), custom_call_target="tpu_custom_call" | custom-call | tf_op jit(solution)/shard_map/head/pallas_call | solution.py:1099
  207.4 4.6 fusion.47
  212.0 130.0 %ffn.1 = (bf16[4,256,2048]{2,1,0:T(8,128)(2,1)}, bf16[4,2,4,32,2048]{4,3,2,1,0:T(8,128)(2,1)}, bf16[6,8,256,256]{3,2,1,0:T(8,128)(2,1)}, bf16[256,512]{1,0:T(8,1...) custom-call(bf16[4,256,2048]{2,1,0:T(8,128)(2,1)} %bitcast.331, bf16[4,4,32,2048]{3,2,1,0:T(8,128)(2,1)} %bitcast.319, ...), custom_call_target="tpu_custom_call" | custom-call | tf_op jit(solution)/shard_map/ffn/pallas_call | solution.py:1591
  342.0 7.5 pad_maximum_fusion.part_ref
  349.5 55.4 %group_sum2.1 = f32[2,4,32,2048]{3,2,1,0:T(8,128)} custom-call(bf16[2,4,2,2,2,32,2048]{6,5,4,3,2,1,0:T(8,128)(2,1)} %pad_maximum_fusion.part_ref), custom_call_target="tpu_custom_call" | custom-call | tf_op jit(solution)/shard_map/group_sum2/pallas_call | solution.py:1293
  409.2 30.1 %group_spread.1 = bf16[4,2,2,2,32,2048]{5,4,3,2,1,0:T(8,128)(2,1)} custom-call(bf16[4,32,2048]{2,1,0:T(8,128)(2,1)} %get-tuple-element.97.own_ref), custom_call_target="tpu_custom_call" | custom-call | tf_op jit(solution)/shard_map/group_spread/pallas_call | solution.py:1346
  450.8 2.7 reshape.630
  456.8 3.3 multiply_reduce_fusion.2
  461.7 5.7 multiply_convert_fusion
  469.1 6.3 bitcast_convert_fusion
  475.9 35.5 %keys_back.1 = bf16[1024,256]{1,0:T(8,128)(2,1)S(1)} custom-call(bf16[4,1024,256]{2,1,0:T(8,128)(2,1)S(1)} %bitcast.298), custom_call_target="tpu_custom_call" | custom-call | tf_op jit(solution)/shard_map/keys_back/pallas_call | solution.py:1206
  527.2 2.7 reshape.626
  529.9 3.2 multiply_reduce_fusion.3
  535.9 3.2 multiply_reduce_fusion
  543.2 3.8 convolution_convert_fusion.1
  548.1 153.5 %rows_sum.1 = (bf16[256,512]{1,0:T(8,128)(2,1)S(1)}, bf16[256,512]{1,0:T(8,128)(2,1)S(1)}, bf16[512,256]{1,0:T(8,128)(2,1)S(1)}, bf16[256,1024]{1,0:T(8,128)(2,1...) custom-call(bf16[3,8,256,256]{3,2,1,0:T(8,128)(2,1)S(1)} %pad_maximum_fusion.1.part_ref, ...), custom_call_target="tpu_custom_call" | custom-call | tf_op jit(solution)/shard_map/rows_sum/pallas_call | solution.py:1421
  711.8 4.5 fusion.147
  722.5 3.2 add_convert_fusion
  725.7 31.0 %group_sum1.1 = f32[1,4,32,2048]{3,2,1,0:T(8,128)} custom-call(bf16[1,4,2,2,2,32,2048]{6,5,4,3,2,1,0:T(8,128)(2,1)} %bitcast.317), custom_call_target="tpu_custom_call" | custom-call | tf_op jit(solution)/shard_map/group_sum1/pallas_call | solution.py:1293
  758.6 64.4 %psum.14 = f32[4352]{0:T(1024)S(1)} all-reduce(f32[4352]{0:T(1024)S(1)} %pad_maximum_fusion.15), channel_id=1, replica_groups=mesh['seq'=8,'kv'=4] {'seq','kv'}, use_global_device_ids=true, to_apply=%region_26.27 | all-reduce | flops 4352 | bytes 34816 | tf_op jit(solution)/shard_map/psum | solution.py:1833
  828.0 49.8 %home.1 = bf16[2,4,2,2,32,2048]{5,4,3,2,1,0:T(8,128)(2,1)} custom-call(bf16[2,4,32,2048]{3,2,1,0:T(8,128)(2,1)} %pad_maximum_fusion.7.own_ref), custom_call_target="tpu_custom_call" | custom-call | tf_op jit(solution)/shard_map/home/pallas_call | solution.py:1377
  877.8 5.0 fusion.134
  883.8 36.1 %psum.15 = f32[4,2048]{1,0:T(4,128)S(1)} all-reduce(f32[4,2048]{1,0:T(4,128)S(1)} %broadcast_select_fusion), channel_id=1, replica_groups=mesh['seq'=8,'kv'=4] {'seq'}, use_global_device_ids=true, to_apply=%region_27.28 | all-reduce | flops 8192 | bytes 65536 | tf_op jit(solution)/shard_map/psum | solution.py:1837
  (225 shorter events, 81.3 us)
Async XLA Ops:
  0.6 10.9 %copy-start.36 = (bf16[256,256]{1,0:T(8,128)(2,1)S(1)}, bf16[256,256]{1,0:T(8,128)(2,1)}, u32[]{:S(2)}) copy-start(bf16[256,256]{1,0:T(8,128)(2,1)} %param.25) | copy-start | bytes 393220
  0.7 10.9 %copy-start.37 = (bf16[256,256]{1,0:T(8,128)(2,1)S(1)}, bf16[256,256]{1,0:T(8,128)(2,1)}, u32[]{:S(2)}) copy-start(bf16[256,256]{1,0:T(8,128)(2,1)} %param.26) | copy-start | bytes 393220
  0.7 11.7 %copy-start.42 = (bf16[256]{0:T(256)(128)(2,1)S(1)}, bf16[256]{0:T(256)(128)(2,1)}, u32[]{:S(2)}) copy-start(bf16[256]{0:T(256)(128)(2,1)} %param.20) | copy-start | bytes 1540
  0.7 11.7 %copy-start.43 = (bf16[256]{0:T(256)(128)(2,1)S(1)}, bf16[256]{0:T(256)(128)(2,1)}, u32[]{:S(2)}) copy-start(bf16[256]{0:T(256)(128)(2,1)} %param.21) | copy-start | bytes 1540
  0.7 11.7 %copy-start.41 = (bf16[128]{0:T(256)(128)(2,1)S(1)}, bf16[128]{0:T(256)(128)(2,1)}, u32[]{:S(2)}) copy-start(bf16[128]{0:T(256)(128)(2,1)} %param.22) | copy-start | bytes 772
  0.7 11.7 %copy-start.40 = (bf16[128]{0:T(256)(128)(2,1)S(1)}, bf16[128]{0:T(256)(128)(2,1)}, u32[]{:S(2)}) copy-start(bf16[128]{0:T(256)(128)(2,1)} %param.23) | copy-start | bytes 772
  0.7 11.7 %copy-start.39 = (bf16[256,4]{0,1:T(4,128)(2,1)S(1)}, bf16[256,4]{0,1:T(4,128)(2,1)}, u32[]{:S(2)}) copy-start(bf16[256,4]{0,1:T(4,128)(2,1)} %param.27) | copy-start | bytes 6148
  207.4 4.6 copy-start.11
  349.5 55.5 %copy-start.38 = (bf16[1,8,16,256]{3,2,1,0:T(8,128)(2,1)S(1)}, bf16[1,8,16,256]{3,2,1,0:T(8,128)(2,1)}, u32[]{:S(2)}) copy-start(bf16[1,8,16,256]{3,2,1,0:T(8,128)(2,1)} %get-tuple-element.47) | copy-start | bytes 196612
  349.5 55.5 %copy-start.4 = (f32[4,32,2048]{2,1,0:T(8,128)S(1)}, f32[4,32,2048]{2,1,0:T(8,128)}, u32[]{:S(2)}) copy-start(f32[4,32,2048]{2,1,0:T(8,128)} %get-tuple-element.40) | copy-start | bytes 3145732
  461.7 5.7 copy-start.34
  475.9 37.8 %copy-start.14 = (f32[4,256,128]{2,1,0:T(8,128)S(1)}, f32[4,256,128]{2,1,0:T(8,128)}, u32[]{:S(2)}) copy-start(f32[4,256,128]{2,1,0:T(8,128)} %get-tuple-element.54) | copy-start | bytes 1572868
  534.3 4.9 copy-start.6
  534.3 4.9 copy-start.7
  534.3 4.9 copy-start.9
  534.3 4.9 copy-start.10
  534.3 4.9 copy-start.19
  543.2 4.3 slice-start
  543.2 4.9 slice-start.1
  548.1 153.6 %copy-start.29 = (bf16[512,256]{1,0:T(8,128)(2,1)S(1)}, bf16[512,256]{1,0:T(8,128)(2,1)}, u32[]{:S(2)}) copy-start(bf16[512,256]{1,0:T(8,128)(2,1)} %get-tuple-element.64) | copy-start | bytes 786436
  705.9 5.8 copy-start.18
  725.7 31.0 %copy-start.13 = (bf16[4,128,2048]{2,1,0:T(8,128)(2,1)S(1)}, bf16[4,128,2048]{2,1,0:T(8,128)(2,1)}, u32[]{:S(2)}) copy-start(bf16[4,128,2048]{2,1,0:T(8,128)(2,1)} %param.16) | copy-start | bytes 6291460
  823.0 3.9 copy-start.21
  877.8 5.0 copy-start.16
  (22 other events, 57.5 us)

commit v3 on v2

--- a/solution.py
+++ b/solution.py
@@ -609,6 +609,26 @@
             pl.when(l <= n - 2)(lambda: self._take(item, left, left))
             self._rs(item, 0, left).start()
 
+    def rs_fire(self, item):
+        l, n = self.l, self.n
+        for o in range(n - 1, 0, -1):
+            pl.when(l == 0)(lambda o=o: self._rs(item, 1, o).start())
+            pl.when(l == n - 1)(lambda o=o: self._rs(item, 0, n - 1 - o).start())
+
+    def rs_mid(self, item, q):
+        l, n = self.l, self.n
+        right, left = n - q, q - 1
+
+        @pl.when((l < right) & (l >= 1))
+        def _():
+            self._take(item, right, right)
+            self._rs(item, 1, right).start()
+
+        @pl.when((l > left) & (l <= n - 2))
+        def _():
+            self._take(item, left, left)
+            self._rs(item, 0, left).start()
+
     def rs_final(self, item):
         l, n = self.l, self.n
         pl.when(l >= 1)(lambda: self._take(item, l, l))
@@ -733,8 +753,8 @@
     small_out,
     x_v,
     normed,
+    normed_t,
     g,
-    own_g,
     small_g,
     gain_row,
     heads_row,
@@ -894,7 +914,6 @@
         return remote(kv.at[b, m], kv.at[b, m], kv_send.at[b, m], kv_recv.at[b, m], right)
 
     each(4, project)
-    put(normed, normed_out)
     put(qp, qp_out)
     put(kp, kp_out)
     put(gate_v, gate_out)
@@ -934,6 +953,14 @@
 
     line.pump(2, 3)
     each(4, lambda m: attend(m, l, True))
+
+    def turned(i):
+        m, s = lax.div(i, 2 * n), lax.rem(i, 2 * n)
+        tile = normed[m, :, :, pl.ds(pl.multiple_of(s * 256, 256), 256)].reshape(256, 256)
+        normed_t[s, :, pl.ds(pl.multiple_of(m * 256, 256), 256)] = tile.T
+
+    each(8 * n, turned)
+    put(normed_t, normed_out)
     line.pump(3, 1)
     line.pump(4, 1)
     kv_round(1)
@@ -1101,7 +1128,7 @@
         out_shape=(
             bf(9, m, 256, 256),
             bf(3, 2, 256, 256),
-            bf(4, 2, 128, d),
+            bf(m, 256, 1024),
             bf(n, 4, 256, 256),
             bf(4, 512, 128),
             f32(4, 256, 256),
@@ -1119,8 +1146,8 @@
         scratch_shapes=[
             vb(4, 2, 4, 32, d),
             vb(4, 2, 128, d),
+            vb(m, 256, 1024),
             vb(12, m, 256, 256),
-            vb(1, 16, 128),
             vb(1, m, 16, 256),
             vf(2, d),
             vb(16, d),
@@ -1168,60 +1195,6 @@
     )(x_in, z_in, wq, wkv, wo, wg, wu, wd, small, cosine, sine, row_lo, row_hi)
 
 
-def keys_back_kernel(n, part_ref, out_ref, work, land, send, recv, local):
-    l, x, y, c = place()
-    left, right = device(l - 1, x, y, c), device(l + 1, x, y, c)
-    greet([(left, l >= 1), (right, l <= n - 2)])
-    load = pltpu.make_async_copy(part_ref, work, local)
-    load.start()
-    load.wait()
-
-    def copy(o):
-        return remote(work.at[o], land.at[o], send.at[o], recv.at[o], left)
-
-    def take(o):
-        copy(o).wait_recv()
-
-        def add(i, unused):
-            at = pl.ds(pl.multiple_of(i * 128, 128), 128)
-            work[o, at] = (work[o, at].astype(F32) + land[o, at].astype(F32)).astype(BF)
-            return 0
-
-        lax.fori_loop(0, work.shape[1] // 128, add, 0)
-
-    for o in range(n - 1):
-
-        @pl.when(l > o)
-        def _(o=o):
-            pl.when(l <= n - 2)(lambda: take(o))
-            copy(o).start()
-
-    pl.when(l <= n - 2)(lambda: take(l))
-    out_ref[...] = work[l]
-    for o in range(n - 1):
-        pl.when(l > o)(lambda o=o: copy(o).wait_send())
-
-
-def keys_back(n, parts):
-    return pl.pallas_call(
-        functools.partial(keys_back_kernel, n),
-        out_shape=jax.ShapeDtypeStruct(parts.shape[1:], BF),
-        in_specs=[ANY],
-        out_specs=VM,
-        scratch_shapes=[
-            pltpu.VMEM(parts.shape, BF),
-            pltpu.VMEM(parts.shape, BF),
-            DMA((n,)),
-            DMA((n,)),
-            DMA,
-        ],
-        compiler_params=pltpu.CompilerParams(
-            collective_id=2, has_side_effects=True, vmem_limit_bytes=40 * 2**20
-        ),
-        name="keys_back",
-    )(parts)
-
-
 class Group:
     def __init__(self):
         self.l, self.x, self.y, self.c = place()
@@ -1238,206 +1211,6 @@
 
     def partners(self):
         return [(self.mate, None)] + [(self.chip(i), None) for i in (1, 2, 3)]
-
-
-def sum_kernel(m, part_ref, out_ref, core_land, low, chip_land, c_send, c_recv, s_send, s_recv):
-    group = Group()
-    x, y, c = group.x, group.y, group.c
-    greet(group.partners())
-    pairs = [(i, b) for b in range(4) for i in range(m)]
-
-    def to_mate(i, b):
-        return remote(
-            part_ref.at[i, b, :, :, 1 - c],
-            core_land.at[i, b],
-            c_send.at[i, b],
-            c_recv.at[i, b],
-            group.mate,
-        )
-
-    def to_chip(i, b, o):
-        ox, oy = group.other(o)
-        return remote(
-            low.at[i, b, ox, oy],
-            chip_land.at[i, o - 1, b],
-            s_send.at[i, b, o - 1],
-            s_recv.at[i, b, o - 1],
-            group.chip(o),
-        )
-
-    for i, b in pairs:
-        to_mate(i, b).start()
-    for i, b in pairs:
-        to_mate(i, b).wait_recv()
-        for u in range(2):
-            for v in range(2):
-                low[i, b, u, v] = (
-                    part_ref[i, b, u, v, c].astype(F32) + core_land[i, b, u, v].astype(F32)
-                ).astype(BF)
-        for o in (3, 1, 2):
-            to_chip(i, b, o).start()
-    for i, b in pairs:
-        total = low[i, b, x, y].astype(F32)
-        for o in (1, 2, 3):
-            to_chip(i, b, o).wait_recv()
-            total = total + chip_land[i, o - 1, b].astype(F32)
-        out_ref[i, b] = total
-    for i, b in pairs:
-        to_mate(i, b).wait_send()
-        for o in (1, 2, 3):
-            to_chip(i, b, o).wait_send()
-
-
-def group_sum(part, collective):
-    m, d = part.shape[0], part.shape[-1]
-    return pl.pallas_call(
-        functools.partial(sum_kernel, m),
-        out_shape=jax.ShapeDtypeStruct((m, 4, 32, d), F32),
-        in_specs=[VM],
-        out_specs=VM,
-        scratch_shapes=[
-            pltpu.VMEM((m, 4, 2, 2, 32, d), BF),
-            pltpu.VMEM((m, 4, 2, 2, 32, d), BF),
-            pltpu.VMEM((m, 3, 4, 32, d), BF),
-            DMA((m, 4)),
-            DMA((m, 4)),
-            DMA((m, 4, 3)),
-            DMA((m, 4, 3)),
-        ],
-        compiler_params=pltpu.CompilerParams(
-            collective_id=collective, has_side_effects=True, vmem_limit_bytes=56 * 2**20
-        ),
-        name=f"group_sum{m}",
-    )(part)
-
-
-def spread_kernel(own_ref, out_ref, s_send, s_recv, c_send, c_recv, local):
-    group = Group()
-    x, y, c = group.x, group.y, group.c
-    greet(group.partners())
-    mine = out_ref.at[:, x, y, c]
-    keep = pltpu.make_async_copy(own_ref, mine, local)
-    keep.start()
-
-    def to_chip(o):
-        return remote(own_ref, mine, s_send.at[o - 1], s_recv.at[o - 1], group.chip(o))
-
-    def to_mate(o):
-        ox, oy = group.other(o)
-        part = out_ref.at[:, ox, oy, c]
-        src = own_ref if o == 0 else part
-        return remote(src, part, c_send.at[o], c_recv.at[o], group.mate)
-
-    for o in (3, 1, 2):
-        to_chip(o).start()
-    to_mate(0).start()
-    for o in (1, 2, 3):
-        to_chip(o).wait_recv()
-        to_mate(o).start()
-    keep.wait()
-    for o in (1, 2, 3):
-        to_chip(o).wait_send()
-    for o in range(4):
-        to_mate(o).wait()
-
-
-def group_spread(own, collective):
-    b, r, d = own.shape
-    return pl.pallas_call(
-        spread_kernel,
-        out_shape=jax.ShapeDtypeStruct((b, 2, 2, 2, r, d), own.dtype),
-        in_specs=[VM],
-        out_specs=ANY,
-        scratch_shapes=[DMA((3,)), DMA((3,)), DMA((4,)), DMA((4,)), DMA],
-        compiler_params=pltpu.CompilerParams(collective_id=collective, has_side_effects=True),
-        name="group_spread",
-    )(own)
-
-
-def home_kernel(own_ref, out_ref, s_send, s_recv, local):
-    group = Group()
-    l, x, y, c = group.l, group.x, group.y, group.c
-    others = [device(l, x, y, 1 - c), device(l, x, 1 - y, c), device(l, x, 1 - y, 1 - c)]
-    greet([(o, None) for o in others])
-    mine = out_ref.at[:, :, y, c]
-    keep = pltpu.make_async_copy(own_ref, mine, local)
-    keep.start()
-    copies = [
-        remote(own_ref, mine, s_send.at[i], s_recv.at[i], o) for i, o in enumerate(others)
-    ]
-    for copy in copies:
-        copy.start()
-    keep.wait()
-    for copy in copies:
-        copy.wait()
-
-
-def home(own):
-    m, b, r, d = own.shape
-    return pl.pallas_call(
-        home_kernel,
-        out_shape=jax.ShapeDtypeStruct((m, b, 2, 2, r, d), own.dtype),
-        in_specs=[VM],
-        out_specs=ANY,
-        scratch_shapes=[DMA((3,)), DMA((3,)), DMA],
-        compiler_params=pltpu.CompilerParams(collective_id=7, has_side_effects=True),
-        name="home",
-    )(own)
-
-
-def rows_kernel(
-    n, part_ref, ffn_ref, dq, dkv, do, dg, du, dd, g, land, rs_send, rs_recv, b_send, b_recv, b_loc, local
-):
-    line = Line(n, g, None, None, land, rs_send, rs_recv)
-    small = Back(line, (dq, dkv, do), b_send, b_recv, b_loc, 256)
-    large = Back(line, (dg, du, dd), b_send, b_recv, b_loc, 512)
-    greet(line.partners() + [small.partner()])
-    loads = [
-        pltpu.make_async_copy(ffn_ref, g.at[pl.ds(3, 6)], local.at[1]),
-        pltpu.make_async_copy(part_ref, g.at[pl.ds(0, 3)], local.at[0]),
-    ]
-    for load in loads:
-        load.start()
-    for load in loads:
-        load.wait()
-    for q in range(1, n):
-        each(9, lambda item, q=q: line.rs_step(item, q))
-    each(9, line.rs_final)
-    for item in range(9):
-        if item < 3:
-            small.start(item, item, 0)
-        else:
-            large.start(item, item % 3, item // 3 - 1)
-    for item in range(9):
-        if item < 3:
-            back_wait(small, item, item, 0)
-        else:
-            back_wait(large, item, item % 3, item // 3 - 1)
-    each(9, line.rs_end)
-
-
-def rows_sum(n, parts, ffn_parts):
-    bf = lambda *shape: jax.ShapeDtypeStruct(shape, BF)
-    return pl.pallas_call(
-        functools.partial(rows_kernel, n),
-        out_shape=(bf(256, 512), bf(256, 512), bf(512, 256), bf(256, 1024), bf(256, 1024), bf(1024, 256)),
-        in_specs=[ANY] * 2,
-        out_specs=(ANY,) * 6,
-        scratch_shapes=[
-            pltpu.VMEM((9, 2 * n, 256, 256), BF),
-            pltpu.VMEM((9, 2 * n + 2, 256, 256), BF),
-            DMA((9, 2, n)),
-            DMA((9, n + 1)),
-            DMA((9,)),
-            DMA((9,)),
-            DMA((9,)),
-            DMA((2,)),
-        ],
-        compiler_params=pltpu.CompilerParams(
-            collective_id=8, has_side_effects=True, vmem_limit_bytes=40 * 2**20
-        ),
-        name="rows_sum",
-    )(parts, ffn_parts)
 
 
 def ffn_kernel(
@@ -1627,6 +1400,598 @@
     )(inner, z_own, z_other, g_in, own_in)
 
 
+def tail_kernel(
+    n,
+    din_any,
+    out_any,
+    x_any,
+    z_any,
+    hidden_any,
+    ffn_parts,
+    normed_any,
+    g_any,
+    kv_any,
+    q_any,
+    qp_any,
+    kp_any,
+    att_any,
+    lse_any,
+    gate_ref,
+    small_g,
+    small,
+    cos_ref,
+    sin_ref,
+    row_lo,
+    row_hi,
+    res_out,
+    grad_out,
+    dq_out,
+    dkv_out,
+    do_out,
+    dg_out,
+    du_out,
+    dd_out,
+    sums_out,
+    g,
+    land,
+    w,
+    normed_t,
+    dbr,
+    kv,
+    kv_land,
+    q_v,
+    qp,
+    kp,
+    att,
+    lse,
+    core_land,
+    chip_land,
+    low,
+    hidden,
+    d_hid,
+    own_z,
+    own_x,
+    own_res,
+    own_grad,
+    mixed_t,
+    dql,
+    dpl,
+    dl,
+    dl_t,
+    gain_row,
+    gain_sum,
+    head_sum,
+    sums,
+    sum_c,
+    sum_x,
+    sum_y,
+    sum_l,
+    loads,
+    rs_send,
+    rs_recv,
+    b_send,
+    b_recv,
+    b_loc,
+    kv_send,
+    kv_recv,
+    c_send,
+    c_recv,
+    s_send,
+    s_recv,
+    i_send,
+    i_recv,
+    j_send,
+    j_recv,
+    h_send,
+    h_recv,
+    t_send,
+    t_recv,
+    o_loc,
+):
+    line = Line(n, g, None, None, land, rs_send, rs_recv)
+    l, x, y, c = line.l, line.x, line.y, line.c
+    k = y * 2 + c
+    group = Group()
+    mate = group.mate
+    left = device(l - 1, x, y, c)
+    blocks = 2 * n
+    width = blocks * 256
+    scale = HEAD_SIZE ** (-0.5)
+    first = Back(line, (dq_out, dkv_out, do_out), b_send, b_recv, b_loc, 256)
+    rest = Back(line, (dg_out, du_out, dd_out), b_send, b_recv, b_loc, 512)
+
+    def backward(item):
+        if item < 3:
+            return first, item, item, 0
+        return rest, item, item % 3, item // 3 - 1
+
+    pending = {}
+
+    def load(name, src, dst):
+        copy = pltpu.make_async_copy(src, dst, loads.at[len(pending)])
+        copy.start()
+        pending[name] = copy
+
+    load("din", din_any.at[:, :, :, c], low)
+    load("hidden", hidden_any, hidden)
+    load("z", z_any.at[:, k], own_z)
+    load("ffn", ffn_parts, g.at[pl.ds(3, 6)])
+    load("w", g_any.at[pl.ds(0, 3)], w)
+    load("kv", kv_any, kv)
+    load("q", q_any, q_v)
+    load("att", att_any, att)
+    load("lse", lse_any, lse)
+    load("qp", qp_any, qp)
+    load("kp", kp_any, kp)
+    load("normed", normed_any, normed_t)
+    load("x", x_any.at[:, k], own_x)
+
+    others = [device(lax.rem(l + d, n), x, y, c) for d in range(1, n)]
+    greet(
+        [(o, None) for o in others] + [(mate, None)] + [(group.chip(i), None) for i in (1, 2, 3)]
+    )
+
+    def mate_copy(r, src, m):
+        return remote(
+            src.at[m, :, :, 1 - c], core_land.at[r % 2, m], c_send.at[r, m], c_recv.at[r, m], mate
+        )
+
+    def chip_copy(r, m, o):
+        ox, oy = group.other(o)
+        return remote(
+            low.at[m, ox, oy],
+            chip_land.at[r % 2, o - 1, m],
+            s_send.at[r, m, o - 1],
+            s_recv.at[r, m, o - 1],
+            group.chip(o),
+        )
+
+    def to_chips(r, src, m, own):
+        mate_copy(r, src, m).wait_recv()
+        for u in range(2):
+            for v in range(2):
+                low[m, u, v] = (
+                    own(m, u, v).astype(F32) + core_land[r % 2, m, u, v].astype(F32)
+                ).astype(BF)
+        for o in (3, 1, 2):
+            chip_copy(r, m, o).start()
+
+    def total_of(r, m):
+        total = low[m, x, y].astype(F32)
+        for o in (1, 2, 3):
+            chip_copy(r, m, o).wait_recv()
+            total = total + chip_land[r % 2, o - 1, m].astype(F32)
+        return total
+
+    def group_end(r, src):
+        def done(m):
+            mate_copy(r, src, m).wait_send()
+            for o in (1, 2, 3):
+                chip_copy(r, m, o).wait_send()
+
+        each(4, done)
+
+    each(4, lambda m: mate_copy(0, din_any, m).start())
+    pending["ffn"].wait()
+    line.rs_fire(3)
+    line.rs_fire(4)
+    for s in range(blocks):
+        cols = slice(s * 256, (s + 1) * 256)
+        gain_row[:, cols] = small_g[0, s, 4:6, :].astype(F32)
+    gain_sum[...] = jnp.zeros_like(gain_sum)
+    head_sum[...] = jnp.zeros_like(head_sum)
+    pending["din"].wait()
+    pending["hidden"].wait()
+    pending["z"].wait()
+    each(4, lambda m: to_chips(0, din_any, m, lambda m, u, v: low[m, u, v]))
+    line.rs_mid(3, 1)
+
+    def spread(m, o):
+        here = dbr.at[m, x, y, c]
+        return remote(here, here, i_send.at[m, o - 1], i_recv.at[m, o - 1], group.chip(o))
+
+    def spread_mate(m, o):
+        ox, oy = group.other(o)
+        there = dbr.at[m, ox, oy, c]
+        return remote(there, there, j_send.at[m, o], j_recv.at[m, o], mate)
+
+    def finish(m):
+        total = total_of(0, m)
+        h = hidden[m]
+        r = lax.rsqrt(jnp.mean(h * h, axis=-1, keepdims=True) + EPS)
+        normal = h * r
+        gain_sum[1:2] += jnp.sum(total * normal, axis=0, keepdims=True)
+        e = total * gain_row[1:2, :]
+        grad = own_z[m].astype(F32) + r * (
+            e - normal * jnp.mean(e * normal, axis=-1, keepdims=True)
+        )
+        d_hid[m] = grad
+        dbr[m, x, y, c] = grad.astype(BF)
+        for o in (3, 1, 2):
+            spread(m, o).start()
+        spread_mate(m, 0).start()
+
+    each(4, finish)
+    line.rs_mid(3, 2)
+    line.rs_fire(5)
+    line.rs_mid(4, 1)
+    line.rs_mid(3, 3)
+    for name in ("w", "kv", "q", "att", "lse", "qp", "kp", "normed", "x"):
+        pending[name].wait()
+    line.rs_mid(4, 2)
+
+    def pass_on(m):
+        for o in (1, 2, 3):
+            spread(m, o).wait_recv()
+            spread_mate(m, o).start()
+
+    each(4, pass_on)
+    group_end(0, din_any)
+    own_low = pltpu.make_async_copy(out_any.at[:, :, :, c], low, o_loc.at[0])
+    own_low.start()
+    each(4, lambda m: mate_copy(1, out_any, m).start())
+    line.rs_fire(6)
+    line.rs_mid(4, 3)
+
+    def arrive(m):
+        for o in range(4):
+            spread_mate(m, o).wait_recv()
+
+    def attend_back(m):
+        arrive(m)
+        d = dbr[m].reshape(256, width)
+        gm = dot_t(d[:, :256], w[2, 0])
+        for s in range(1, blocks):
+            gm = gm + dot_t(d[:, s * 256 : (s + 1) * 256], w[2, s])
+        gates = gate_ref[m]
+        gates = jnp.where(x == 0, gates[:, 0:2], gates[:, 2:4])
+        g0, g1 = gates[:, 0:1], gates[:, 1:2]
+        a0, a1 = att[m, :256], att[m, 256:]
+        d0, d1 = gm[:, :128], gm[:, 128:]
+        l0 = jnp.sum(d0 * a0, axis=-1, keepdims=True) * g0 * (1.0 - g0)
+        l1 = jnp.sum(d1 * a1, axis=-1, keepdims=True) * g1 * (1.0 - g1)
+        lane = lax.broadcasted_iota(jnp.int32, (256, 128), 1)
+        logits = jnp.where(lane == 2 * x, l0, 0.0) + jnp.where(lane == 2 * x + 1, l1, 0.0)
+        logits = logits.astype(BF)
+        dl[m] = logits
+        at = pl.ds(pl.multiple_of(m * 256, 256), 256)
+        dl_t[:, at] = logits.T
+        mixed = jnp.concatenate([a0 * g0, a1 * g1], axis=1).astype(BF)
+        mixed_t[:, at] = mixed.T
+        da = jnp.concatenate([d0 * g0, d1 * g1], axis=0).astype(BF)
+        delta = jnp.sum(da.astype(F32) * att[m], axis=-1, keepdims=True)
+        log_total = lse[m][:, :1]
+        qm = q_v[m]
+        att[m] = jnp.zeros((512, 128), F32)
+
+        def block(b, unused):
+            pair = kv[b, m]
+            keys, values = pair[:, :128], pair[:, 128:]
+            raw = dot_t(qm, keys) * scale
+            lo = row_lo[m][:, :1] - b * 256
+            hi = row_hi[m][:, :1] - b * 256
+            column = lax.broadcasted_iota(jnp.int32, (512, 256), 1)
+            allowed = (column >= jnp.concatenate([lo, lo], axis=0)) & (
+                column < jnp.concatenate([hi, hi], axis=0)
+            )
+            p = jnp.where(allowed, jnp.exp(raw - log_total), 0.0)
+            ds = (p * (dot_t(da, values) - delta)).astype(BF)
+            att[m] += dot(ds, keys)
+            dk = dot(ds.T, qm) * scale
+            dv = dot(p.astype(BF).T, da)
+            kv[b, m] = jnp.concatenate([dk, dv], axis=1).astype(BF)
+            return 0
+
+        lax.fori_loop(0, l + 1, block, 0)
+
+    def kv_copy(b, m):
+        return remote(
+            kv.at[b, m], kv_land.at[b, m], kv_send.at[b, m], kv_recv.at[b, m], left
+        )
+
+    def kv_step(m):
+        for b in range(n - 1):
+
+            @pl.when(l > b)
+            def _(b=b):
+                @pl.when(l <= n - 2)
+                def _():
+                    kv_copy(b, m).wait_recv()
+                    kv[b, m] = (kv[b, m].astype(F32) + kv_land[b, m].astype(F32)).astype(BF)
+
+                kv_copy(b, m).start()
+
+    def normal_back(u, d_rot, gain, cosine, sine):
+        d = d_rot * cosine - pltpu.roll(d_rot, 64, 1) * sine
+        r = lax.rsqrt(jnp.mean(u * u, axis=-1, keepdims=True) + EPS)
+        normal = u * r
+        e = d * gain
+        grad = r * (e - normal * jnp.mean(e * normal, axis=-1, keepdims=True))
+        return grad.astype(BF), jnp.sum(d * normal, axis=0, keepdims=True)
+
+    gains = small[8:10, :128].astype(F32)
+
+    def query_back(m):
+        for h in range(2):
+            cols = slice(h * 128, (h + 1) * 128)
+            grad, total = normal_back(
+                qp[m][:, cols],
+                att[m, h * 256 : (h + 1) * 256] * scale,
+                gains[0:1],
+                cos_ref[m],
+                sin_ref[m],
+            )
+            dql[m, :, cols] = grad
+            head_sum[0:1, :128] += total
+
+    attend_back(0)
+    line.rs_mid(5, 1)
+    attend_back(1)
+    kv_step(0)
+    line.rs_mid(5, 2)
+    line.rs_fire(7)
+    attend_back(2)
+    kv_step(1)
+    line.rs_mid(5, 3)
+    line.rs_mid(6, 1)
+    attend_back(3)
+    kv_step(2)
+    kv_step(3)
+    line.rs_mid(6, 2)
+    line.rs_fire(8)
+    each(4, query_back)
+
+    def output_weights(s, unused):
+        z = dbr[:, :, :, :, :, pl.ds(pl.multiple_of(s * 256, 256), 256)].reshape(1024, 256)
+        g[2, s] = dot(mixed_t[...], z).astype(BF)
+        return 0
+
+    def query_weights(s, unused):
+        g[0, s] = dot(normed_t[s], dql[...].reshape(1024, 256)).astype(BF)
+        sums[1, s] = dot_t(dl_t[:16], normed_t[s])[:8]
+        return 0
+
+    lax.fori_loop(0, blocks, output_weights, 0)
+    line.rs_fire(2)
+    lax.fori_loop(0, blocks, query_weights, 0)
+    line.rs_fire(0)
+    line.rs_mid(6, 3)
+    line.rs_mid(7, 1)
+    own_low.wait()
+    each(4, lambda m: to_chips(1, out_any, m, lambda m, u, v: low[m, u, v]))
+    line.rs_mid(7, 2)
+
+    def key_back(m):
+        pl.when(l <= n - 2)(lambda: kv_copy(l, m).wait_recv())
+        pair = kv[l, m].astype(F32)
+        pair = pair + jnp.where(l <= n - 2, kv_land[l, m].astype(F32), 0.0)
+        grad, total = normal_back(kp[m], pair[:, :128], gains[1:2], cos_ref[m], sin_ref[m])
+        dpl[m, :, :128] = grad
+        dpl[m, :, 128:] = pair[:, 128:].astype(BF)
+        head_sum[0:1, 128:] += total
+
+    each(4, key_back)
+
+    def key_weights(s, unused):
+        g[1, s] = dot(normed_t[s], dpl[...].reshape(1024, 256)).astype(BF)
+        return 0
+
+    lax.fori_loop(0, blocks, key_weights, 0)
+    line.rs_fire(1)
+
+    def finish_out(m):
+        own_res[m] = (hidden[m] + total_of(1, m)).astype(BF)
+
+    each(4, finish_out)
+    group_end(1, out_any)
+
+    def normed_back(m):
+        a, b, e = dql[m], dpl[m], dl[m][:, :16]
+        for s in range(blocks):
+            part = dot_t(a, w[0, s]) + dot_t(b, w[1, s]) + dot(e, small_g[0, s])
+            dbr[m, :, :, :, :, s * 256 : (s + 1) * 256] = part.astype(BF).reshape(
+                2, 2, 2, 32, 256
+            )
+        mate_copy(2, dbr, m).start()
+
+    def home(i, own, out):
+        mine = out.at[:, k]
+        there = out.at[:, (1 - y) * 2 + c]
+        keep = pltpu.make_async_copy(own, mine, o_loc.at[1 + i])
+        over = remote(own, mine, h_send.at[i, 0], h_recv.at[i, 0], group.chip(2))
+        beside = remote(own, mine, h_send.at[i, 1], h_recv.at[i, 1], mate)
+        on = remote(there, there, h_send.at[i, 2], h_recv.at[i, 2], mate)
+        return keep, over, beside, on
+
+    def drain_spread(m):
+        for o in (1, 2, 3):
+            spread(m, o).wait_send()
+        for o in range(4):
+            spread_mate(m, o).wait_send()
+
+    each(4, drain_spread)
+    each(4, normed_back)
+    res_home = home(0, own_res, res_out)
+    for copy in res_home[:3]:
+        copy.start()
+    line.rs_mid(7, 3)
+    line.rs_mid(8, 1)
+    line.rs_mid(8, 2)
+    each(4, lambda m: to_chips(2, dbr, m, lambda m, u, v: dbr[m, u, v, c]))
+    line.rs_mid(8, 3)
+    line.rs_mid(2, 1)
+
+    def finish_grad(m):
+        total = total_of(2, m)
+        v = own_x[m].astype(F32)
+        r = lax.rsqrt(jnp.mean(v * v, axis=-1, keepdims=True) + EPS)
+        normal = v * r
+        gain_sum[0:1] += jnp.sum(total * normal, axis=0, keepdims=True)
+        e = total * gain_row[0:1, :]
+        own_grad[m] = (
+            d_hid[m] + r * (e - normal * jnp.mean(e * normal, axis=-1, keepdims=True))
+        ).astype(BF)
+
+    each(4, finish_grad)
+    for s in range(blocks):
+        sums[0, s, 0:2] = gain_sum[0:2, s * 256 : (s + 1) * 256]
+        sums[0, s, 2:3] = head_sum[0:1]
+        sums[0, s, 3:8] = jnp.zeros((5, 256), F32)
+    small_c = remote(sums.at[0], sum_c, t_send.at[0], t_recv.at[0], mate)
+    small_x = remote(sums, sum_x, t_send.at[1], t_recv.at[1], group.chip(1))
+    small_y = remote(sums.at[0], sum_y, t_send.at[2], t_recv.at[2], group.chip(2))
+    small_c.start()
+    grad_home = home(1, own_grad, grad_out)
+    for copy in grad_home[:3]:
+        copy.start()
+    res_home[1].wait_recv()
+    res_home[3].start()
+    line.rs_mid(2, 2)
+    line.rs_mid(2, 3)
+    small_c.wait()
+    sums[0] = sums[0] + sum_c[...]
+    small_x.start()
+    line.rs_mid(0, 1)
+    line.rs_mid(0, 2)
+    small_x.wait()
+    sums[...] = sums[...] + sum_x[...]
+    small_y.start()
+    line.rs_mid(0, 3)
+    line.rs_mid(1, 1)
+    small_y.wait()
+    sums[0] = sums[0] + sum_y[...]
+
+    def small_line(d):
+        to = lax.rem(l + d, n)
+        return remote(
+            sums.at[:, pl.ds(2 * to, 2)],
+            sum_l.at[l],
+            t_send.at[2 + d],
+            t_recv.at[2 + d],
+            device(to, x, y, c),
+        )
+
+    for d in range(1, n):
+        small_line(d).start()
+    sum_l[l] = sums[:, pl.ds(2 * l, 2)]
+    line.rs_mid(1, 2)
+    line.rs_mid(1, 3)
+    grad_home[1].wait_recv()
+    grad_home[3].start()
+    for item in (3, 4, 5, 6, 7, 8, 2, 0, 1):
+        line.rs_final(item)
+        back, item, kind, j = backward(item)
+        back.start(item, kind, j)
+    for d in range(1, n):
+        small_line(d).wait()
+    total = sum_l[0, :, x]
+    for i in range(1, n):
+        total = total + sum_l[i, :, x]
+    sums_out[...] = total
+    for item in (3, 4, 5, 6, 7, 8, 2, 0, 1):
+        back, item, kind, j = backward(item)
+        back_wait(back, item, kind, j)
+    for copies in (res_home, grad_home):
+        keep, over, beside, on = copies
+        keep.wait()
+        over.wait_send()
+        beside.wait()
+        on.wait()
+    group_end(2, dbr)
+
+    def drain(m):
+        for b in range(n - 1):
+            pl.when(l > b)(lambda b=b: kv_copy(b, m).wait_send())
+
+    each(4, drain)
+    each(9, line.rs_end)
+
+
+def tail(n, din, out, x_in, z_in, hidden, ffn_parts, normed_t, g_all, kv, q, qp, kp, att, lse, gate, small_g, small, cosine, sine, row_lo, row_hi):
+    d = x_in.shape[-1]
+    m = 2 * n
+    bf = lambda *shape: jax.ShapeDtypeStruct(shape, BF)
+    vb = lambda *shape: pltpu.VMEM(shape, BF)
+    vf = lambda *shape: pltpu.VMEM(shape, F32)
+    return pl.pallas_call(
+        functools.partial(tail_kernel, n),
+        out_shape=(
+            bf(4, 4, 32, d),
+            bf(4, 4, 32, d),
+            bf(256, 512),
+            bf(256, 512),
+            bf(512, 256),
+            bf(256, 1024),
+            bf(256, 1024),
+            bf(1024, 256),
+            jax.ShapeDtypeStruct((2, 8, 256), F32),
+        ),
+        in_specs=[ANY] * 14 + [VM] * 7,
+        out_specs=(ANY,) * 8 + (VM,),
+        scratch_shapes=[
+            vb(9, m, 256, 256),
+            vb(9, m + 2, 256, 256),
+            vb(3, m, 256, 256),
+            vb(m, 256, 1024),
+            vb(4, 2, 2, 2, 32, d),
+            vb(n, 4, 256, 256),
+            vb(n, 4, 256, 256),
+            vb(4, 512, 128),
+            vf(4, 256, 256),
+            vf(4, 256, 128),
+            vf(4, 512, 128),
+            vf(4, 512, 128),
+            vb(2, 4, 2, 2, 32, d),
+            vb(2, 3, 4, 32, d),
+            vb(4, 2, 2, 32, d),
+            vf(4, 32, d),
+            vf(4, 32, d),
+            vb(4, 32, d),
+            vb(4, 32, d),
+            vb(4, 32, d),
+            vb(4, 32, d),
+            vb(256, 1024),
+            vb(4, 256, 256),
+            vb(4, 256, 256),
+            vb(4, 256, 128),
+            vb(128, 1024),
+            vf(2, d),
+            vf(2, d),
+            vf(1, 256),
+            vf(2, m, 8, 256),
+            vf(m, 8, 256),
+            vf(2, m, 8, 256),
+            vf(m, 8, 256),
+            vf(n, 2, 2, 8, 256),
+            DMA((13,)),
+            DMA((9, 2, n)),
+            DMA((9, n + 1)),
+            DMA((9,)),
+            DMA((9,)),
+            DMA((9,)),
+            DMA((n, 4)),
+            DMA((n, 4)),
+            DMA((3, 4)),
+            DMA((3, 4)),
+            DMA((3, 4, 3)),
+            DMA((3, 4, 3)),
+            DMA((4, 3)),
+            DMA((4, 3)),
+            DMA((4, 4)),
+            DMA((4, 4)),
+            DMA((2, 3)),
+            DMA((2, 3)),
+            DMA((3 + n,)),
+            DMA((3 + n,)),
+            DMA((3,)),
+        ],
+        compiler_params=pltpu.CompilerParams(
+            collective_id=10, has_side_effects=True, vmem_limit_bytes=63 * 2**20
+        ),
+        name="tail",
+    )(din, out, x_in, z_in, hidden, ffn_parts, normed_t, g_all, kv, q, qp, kp, att, lse, gate, small_g, small, cosine, sine, row_lo, row_hi)
+
+
 def row_layout(index, buckets, lengths):
     ends = jnp.cumsum(buckets)
     starts = ends - buckets
@@ -1679,41 +2044,24 @@
         axis=1,
     )
 
-    def own_rows(values):
-        return lax.dynamic_slice_in_dim(values, kv * 32, 32, 1)
-
     row_index = l * span + jnp.arange(span, dtype=jnp.int32)
-    key_index = jnp.arange(n * span, dtype=jnp.int32)
     layouts = [row_layout(row_index, bucket_sizes[b], true_lengths[b]) for b in range(batches)]
     positions = jnp.concatenate([item[1] for item in layouts])
     row_lo = jnp.stack([row_index - item[1] for item in layouts])
     limits = jnp.stack([item[2] for item in layouts])
     row_hi = jnp.minimum(row_index + 1, row_lo + limits)
-    allowed = (
-        (key_index[None, None, :] >= row_lo[:, :, None])
-        & (key_index[None, None, :] < row_hi[:, :, None])
-    )[:, None]
     cosine, sine = rope_tables(positions, HEAD_SIZE)
     signed = sine * jnp.where(jnp.arange(HEAD_SIZE) < HEAD_SIZE // 2, -1.0, 1.0)
-    (
-        g_all,
-        g_own,
-        normed,
-        all_keys,
-        query,
-        query_proj,
-        key_proj,
-        gate,
-        attended,
-        log_total,
-        hidden,
-        inner,
-        z_other,
-        small,
-    ) = head(
+    x_split = inputs.reshape(batches, 4, 32, width)
+    z_split = cotangent.reshape(batches, 4, 32, width)
+    cosine = cosine.reshape(batches, span, HEAD_SIZE)
+    signed = signed.reshape(batches, span, HEAD_SIZE)
+    row_lo = jnp.broadcast_to(row_lo[:, :, None], (batches, span, 128))
+    row_hi = jnp.broadcast_to(row_hi[:, :, None], (batches, span, 128))
+    (g_all, g_own, normed_t, kv_all, query, query_proj, key_proj, gate, attended, log_total, hidden, inner, z_other, small) = head(
         n,
-        inputs.reshape(batches, 4, 32, width),
-        cotangent.reshape(batches, 4, 32, width),
+        x_split,
+        z_split,
         query_weight,
         paired,
         output_weight,
@@ -1721,141 +2069,56 @@
         up_weight,
         down_weight,
         own_small,
-        cosine.reshape(batches, span, HEAD_SIZE),
-        signed.reshape(batches, span, HEAD_SIZE),
-        jnp.broadcast_to(row_lo[:, :, None], (batches, span, 128)),
-        jnp.broadcast_to(row_hi[:, :, None], (batches, span, 128)),
+        cosine,
+        signed,
+        row_lo,
+        row_hi,
     )
-    small = small[0].transpose(1, 0, 2).reshape(16, width)
-    w_head = lax.dynamic_slice_in_dim(small, x * 2, 2, 0)
-    gain_a = small[4].astype(F32)
-    gain_f = small[5].astype(F32)
-    w_query = g_all[0].reshape(width, 256)
-    w_keys = g_all[1].reshape(width, 256)
-    w_output = g_all[2]
-    normed = normed.reshape(batches * span, width)
-    query_proj = query_proj.reshape(-1, 2, HEAD_SIZE)
-    key_proj = key_proj.reshape(-1, 1, HEAD_SIZE)
-    query_scale = rms_scale(query_proj)
-    query_normal = query_proj * query_scale
-    key_scale = rms_scale(key_proj)
-    key_normal = key_proj * key_scale
-    gate = lax.dynamic_slice_in_dim(gate, x * 2, 2, 2)
-    seen = (jnp.arange(n) <= l)[:, None, None, None]
-    all_keys = jnp.where(seen, all_keys, 0).transpose(1, 0, 2, 3).reshape(batches, n * span, 256)
-    keys, values = all_keys[..., :HEAD_SIZE], all_keys[..., HEAD_SIZE:]
-    query = query.reshape(batches, 2, span, HEAD_SIZE)
-    attended = attended.reshape(batches, 2, span, HEAD_SIZE)
-    log_total = log_total[..., :1].reshape(batches, 2, span, 1)
-    raw = jnp.einsum("bhtd,bsd->bhts", query, keys, preferred_element_type=F32) * scale
-    weights = jnp.where(allowed, jnp.exp(raw - log_total), 0.0)
-    gate_heads = gate.transpose(0, 2, 1)[..., None]
-    mixed = (attended * gate_heads).astype(BF).transpose(0, 2, 1, 3).reshape(-1, 256)
     split = (batches, 2, 2, 2, 32, width)
-    own_x = own_rows(inputs).astype(F32)
-    scale_f = rms_scale(hidden)
-    normal_f = hidden * scale_f
     out_part, din_part, ffn_parts, d_gate, d_up, d_down = ffn(
+        n, inner.reshape(batches, span, width), z_split, z_other, g_all, g_own
+    )
+    (own_out, own_grad, dq, dkv, do, d_gate2, d_up2, d_down2, sums) = tail(
         n,
-        inner.reshape(batches, span, width),
-        cotangent.reshape(batches, 4, 32, width),
-        z_other,
+        din_part.reshape(split),
+        out_part.reshape(split),
+        x_split,
+        z_split,
+        hidden,
+        ffn_parts,
+        normed_t,
         g_all,
-        g_own,
+        kv_all,
+        query,
+        query_proj,
+        key_proj,
+        attended,
+        log_total,
+        gate,
+        small,
+        own_small,
+        cosine,
+        signed,
+        row_lo,
+        row_hi,
     )
-    sums = group_sum(jnp.stack([out_part.reshape(split), din_part.reshape(split)]), 5)
-    own_out = (hidden + sums[0]).astype(BF)
-    grad_inner = sums[1]
-    own_dz = own_rows(cotangent).astype(F32)
-    sum_feedforward_gain = jnp.sum(grad_inner * normal_f, axis=(0, 1))
-    grad_hidden = own_dz + norm_backward(grad_inner * gain_f, normal_f, scale_f)
-    grad_branch = group_spread(grad_hidden.astype(BF), 6).reshape(-1, width)
-    d_output = jnp.stack(
-        [outer_sum(mixed, grad_branch[:, s * 256 : (s + 1) * 256]).astype(BF) for s in range(2 * n)]
-    )
-    grad_mixed = sum(
-        times_transpose(grad_branch[:, s * 256 : (s + 1) * 256], w_output[s]) for s in range(2 * n)
-    )
-    grad_mixed = grad_mixed.reshape(batches, span, 2, HEAD_SIZE).transpose(0, 2, 1, 3)
-    grad_heads = (grad_mixed * gate_heads).astype(BF)
-    grad_logits = (
-        jnp.sum(grad_mixed * attended, axis=-1, keepdims=True) * gate_heads * (1.0 - gate_heads)
-    ).astype(BF)
-    delta = jnp.sum(grad_heads.astype(F32) * attended, axis=-1, keepdims=True)
-    grad_weights = jnp.einsum("bhtd,bsd->bhts", grad_heads, values, preferred_element_type=F32)
-    grad_scores = (weights * (grad_weights - delta)).astype(BF)
-    grad_query = scale * jnp.einsum(
-        "bhts,bsd->bhtd", grad_scores, keys, preferred_element_type=F32
-    )
-    grad_keys = scale * jnp.einsum(
-        "bhts,bhtd->bsd", grad_scores, query, preferred_element_type=F32
-    )
-    grad_values = jnp.einsum(
-        "bhts,bhtd->bsd", weights.astype(BF), grad_heads, preferred_element_type=F32
-    )
-    grad_pair = jnp.concatenate([grad_keys, grad_values], axis=-1).astype(BF)
-    grad_pair = grad_pair.reshape(batches, n, span, 256).transpose(1, 0, 2, 3)
-    local_pair = keys_back(n, grad_pair.reshape(n, batches * span, 256)).astype(F32)
-
-    grad_query_rot = grad_query.transpose(0, 2, 1, 3).reshape(-1, 2, HEAD_SIZE)
-    grad_query_norm = rotate_backward(grad_query_rot, cosine, sine)
-    sum_query_gain = jnp.sum(grad_query_norm * query_normal, axis=(0, 1))
-    d_query = (
-        norm_backward(grad_query_norm * gain_query, query_normal, query_scale)
-        .astype(BF)
-        .reshape(-1, 256)
-    )
-    grad_key_norm = rotate_backward(local_pair[:, None, :HEAD_SIZE], cosine, sine)
-    sum_key_gain = jnp.sum(grad_key_norm * key_normal, axis=(0, 1))
-    d_key = norm_backward(grad_key_norm * gain_key, key_normal, key_scale).astype(BF)
-    d_pair = jnp.concatenate(
-        [d_key.reshape(-1, HEAD_SIZE), local_pair[:, HEAD_SIZE:].astype(BF)], axis=1
-    )
-    logits_low = grad_logits[..., 0].transpose(0, 2, 1).reshape(-1, 2)
-    d_head = outer_sum(logits_low, normed)
-    d_head = jnp.where(jnp.arange(2)[:, None, None] == x, d_head[None], 0.0).reshape(4, width)
-    d_query_weight = outer_sum(normed, d_query).astype(BF).reshape(2 * n, 256, 256)
-    d_pair_weight = outer_sum(normed, d_pair).astype(BF).reshape(2 * n, 256, 256)
-    grad_partial = (
-        times_transpose(d_query, w_query)
-        + times_transpose(d_pair, w_keys)
-        + jnp.dot(logits_low, w_head, preferred_element_type=F32)
-    ).astype(BF)
-    grad_normed = group_sum(grad_partial.reshape((1,) + split), 10)[0]
-    dq, dkv, do, d_gate2, d_up2, d_down2 = rows_sum(
-        n, jnp.stack([d_query_weight, d_pair_weight, d_output]), ffn_parts
-    )
-    scale_a = rms_scale(own_x)
-    normal_a = own_x * scale_a
-    sum_attention_gain = jnp.sum(grad_normed * normal_a, axis=(0, 1))
-    own_grad = (grad_hidden + norm_backward(grad_normed * gain_a, normal_a, scale_a)).astype(BF)
-    outs = home(jnp.stack([own_out, own_grad])).reshape(2, batches, rows, width)
-    gains = lax.psum(
-        jnp.concatenate([sum_attention_gain, sum_feedforward_gain, sum_query_gain, sum_key_gain]),
-        ("seq", "kv"),
-    )
-    head_total = lax.psum(d_head, "seq")
-    own_width = width // (2 * n)
 
     def joined(first, rest, axis):
         a, b = jnp.split(first.astype(F32), 2, axis=axis)
         c, d = jnp.split(rest.astype(F32), 2, axis=axis)
         return jnp.concatenate([a, c, b, d], axis=axis)
 
-    def cut(values):
-        return lax.dynamic_slice_in_dim(values, seq * own_width, own_width, values.ndim - 1)
-
     return (
-        outs[0],
-        outs[1],
-        cut(gains[:width]),
-        cut(gains[width : 2 * width]),
-        gains[2 * width : 2 * width + HEAD_SIZE],
-        gains[2 * width + HEAD_SIZE :],
+        own_out.reshape(batches, rows, width),
+        own_grad.reshape(batches, rows, width),
+        sums[0, 0],
+        sums[0, 1],
+        sums[0, 2, :HEAD_SIZE],
+        sums[0, 2, HEAD_SIZE:],
         dq.astype(F32),
         jnp.concatenate([dkv[:, :128], dkv[:, 256:384]], axis=1).astype(F32),
         jnp.concatenate([dkv[:, 128:256], dkv[:, 384:]], axis=1).astype(F32),
-        cut(head_total).T,
+        sums[1, :4].T,
         do.astype(F32),
         joined(d_gate, d_gate2, 1),
         joined(d_up, d_up2, 1),

time: 928 us -> 620 us (0.67)
  Pallas kernels: 677 us -> 575 us
  blocking collectives: 101 us -> 0 us
  matrix products: 49.6 us -> 0 us
  other arithmetic: 56.8 us -> 16.5 us
  local copies, waits for them, and re-layouts: 34.8 us -> 17.8 us
    pallas_call x6 -> x1, Pallas kernels: 355 us -> 254 us  [tail(): pl.pallas_call(functools.partial(tail_kernel, n), out_shape=(bf(4, 4, 32,...]
    psum x2 -> x0, blocking collectives: 101 us -> none  [the longest x1 64.4 us: fast_local(): lax.psum(jnp.concatenate([sum_attention_gain, sum_feedforward_gain, sum_q...]
    dot_general x27 -> x0, matrix products: 49.6 us -> none  [the longest x10 19.2 us: times_transpose(): lax.dot_general(left, weight, (((1,), (1,)), ((), ())), preferred_element...]
    reduce_sum x9 -> x0, other arithmetic: 14.9 us -> none  [the longest x4 3.76 us: rms_scale(): return lax.rsqrt(jnp.mean(values * values, axis=-1, keepdims=True) + EPS)]
    another operation x9 -> x4, other arithmetic: 14.1 us -> 0.71 us  [the longest x1 7.54 us: fast_local(): jnp.stack([out_part.reshape(split), din_part.reshape(split)])]
where the time goes in v3:
time: 620 us; the launch traced here: 611 us
  Pallas kernels  575 us (93%)
  local copies, waits for them, and re-layouts  17.8 us (3%)
  other arithmetic  16.5 us (3%)
    pallas_call x1, Pallas kernels, tail(): pl.pallas_call(functools.partial(tail_kernel, n), out_shape=(bf(4, 4, 32,...  254 us
    pallas_call x1, Pallas kernels, head(): pl.pallas_call(functools.partial(head_kernel, n), out_shape=(bf(9, m, 256...  192 us
    pallas_call x1, Pallas kernels, ffn(): pl.pallas_call(functools.partial(ffn_kernel, n), out_shape=(bf(4, 256, d)...  130 us

profile of v3, /device:TPU:0, one launch (start us, length us, event | category | flops | bytes accessed | tf_op | source)
XLA Modules:
  0.0 610.5 jit_solution(12662173378452871453)
XLA Ops:
  4.2 1.9 concatenate.47.small
  6.1 0.8 fusion.16
  7.3 1.0 fusion.25
  9.0 1.0 broadcast_in_dim.126.row_hi
  10.0 1.0 broadcast_in_dim.117.row_lo
  11.0 3.4 multiply_sine_fusion
  14.4 1.0 maximum_multiply_fusion.sin_ref
  15.4 1.0 pad_maximum_fusion.3.cos_ref
  16.4 191.7 %head.1 = (bf16[9,8,256,256]{3,2,1,0:T(8,128)(2,1)}, bf16[3,2,256,256]{3,2,1,0:T(8,128)(2,1)}, bf16[8,256,1024]{2,1,0:T(8,128)(2,1)}, bf16[4,4,256,256]{3,2,1,0:...) custom-call(bf16[4,4,32,2048]{3,2,1,0:T(8,128)(2,1)} %bitcast.79, ...), custom_call_target="tpu_custom_call" | custom-call | tf_op jit(solution)/shard_map/head/pallas_call | solution.py:1126
  208.1 130.1 %ffn.1 = (bf16[4,256,2048]{2,1,0:T(8,128)(2,1)}, bf16[4,2,4,32,2048]{4,3,2,1,0:T(8,128)(2,1)}, bf16[6,8,256,256]{3,2,1,0:T(8,128)(2,1)}, bf16[256,512]{1,0:T(8,1...) custom-call(bf16[4,256,2048]{2,1,0:T(8,128)(2,1)} %bitcast.83, bf16[4,4,32,2048]{3,2,1,0:T(8,128)(2,1)} %bitcast.77, ...), custom_call_target="tpu_custom_call" | custom-call | tf_op jit(solution)/shard_map/ffn/pallas_call | solution.py:1364
  338.2 253.6 %tail.1 = (bf16[4,4,32,2048]{3,2,1,0:T(8,128)(2,1)}, bf16[4,4,32,2048]{3,2,1,0:T(8,128)(2,1)}, bf16[256,512]{1,0:T(8,128)(2,1)}, bf16[256,512]{1,0:T(8,128)(2,1)...) custom-call(bf16[4,2,2,2,32,2048]{5,4,3,2,1,0:T(8,128)(2,1)} %bitcas, ...), custom_call_target="tpu_custom_call" | custom-call | tf_op jit(solution)/shard_map/tail/pallas_call | solution.py:1916
  591.8 1.3 slice_bitcast_fusion.1
  593.0 1.3 fusion.27
  594.4 1.3 slice_bitcast_fusion
  595.7 1.0 fusion.24
  598.1 1.8 convert_element_type.53
  600.9 0.8 copy-done.4
  601.9 1.3 pad_maximum_fusion
  603.3 1.3 pad_maximum_fusion.1
  604.7 1.2 pad_maximum_fusion.2
  605.9 0.9 copy-done.1
  606.8 1.3 copy.32
  608.2 1.0 copy-done
  609.2 1.3 copy.33
  (52 shorter events, 7.3 us)
Async XLA Ops:
  591.7 8.1 %copy-start.8 = (bf16[512,256]{1,0:T(8,128)(2,1)S(1)}, bf16[512,256]{1,0:T(8,128)(2,1)}, u32[]{:S(2)}) copy-start(bf16[512,256]{1,0:T(8,128)(2,1)} %get-tuple-element.65) | copy-start | bytes 786436
  591.8 8.9 %copy-start.7 = (bf16[256,512]{1,0:T(8,128)(2,1)S(1)}, bf16[256,512]{1,0:T(8,128)(2,1)}, u32[]{:S(2)}) copy-start(bf16[256,512]{1,0:T(8,128)(2,1)} %get-tuple-element.66) | copy-start | bytes 786436
  597.3 3.4 copy-start.6
  599.9 1.0 copy-start.5
  600.7 1.1 copy-start.4
  601.9 1.3 copy-start.3
  603.3 1.3 copy-start.2
  604.7 2.2 copy-start.1
  606.8 2.3 copy-start

commit v4 on v3

--- a/solution.py
+++ b/solution.py
@@ -532,6 +532,12 @@
         pl.when(l >= 1)(lambda: self._ag(item, 0, l).start())
         pl.when(l <= self.n - 2)(lambda: self._ag(item, 1, l).start())
 
+    def ag_left(self, item):
+        pl.when(self.l >= 1)(lambda: self._ag(item, 0, self.l).start())
+
+    def ag_right(self, item):
+        pl.when(self.l <= self.n - 2)(lambda: self._ag(item, 1, self.l).start())
+
     def ag_step(self, item, t):
         l, n = self.l, self.n
 
@@ -629,6 +635,34 @@
             self._take(item, left, left)
             self._rs(item, 0, left).start()
 
+    def rs_near(self, item):
+        l, n = self.l, self.n
+
+        @pl.when(l == 1)
+        def _():
+            for o in range(n - 1, 1, -1):
+                self._take(item, o, o)
+                self._rs(item, 1, o).start()
+
+        @pl.when(l == n - 2)
+        def _():
+            for o in range(n - 2):
+                self._take(item, o, o)
+                self._rs(item, 0, o).start()
+
+    def rs_far(self, item):
+        l, n = self.l, self.n
+
+        @pl.when(l == 1)
+        def _():
+            self._take(item, 0, 0)
+            self._rs(item, 0, 0).start()
+
+        @pl.when(l == n - 2)
+        def _():
+            self._take(item, n - 1, n - 1)
+            self._rs(item, 1, n - 1).start()
+
     def rs_final(self, item):
         l, n = self.l, self.n
         pl.when(l >= 1)(lambda: self._take(item, l, l))
@@ -659,7 +693,8 @@
         return (device(line.l, 1 - line.x, line.y, line.c), None)
 
     def _part(self, ref, kind, j, x):
-        at = pl.multiple_of(x * self.half + j * 256, 256)
+        half = self.half if isinstance(self.half, int) else self.half[kind]
+        at = pl.multiple_of(x * half + j * 256, 256)
         return ref.at[pl.ds(at, 256), :] if kind == 2 else ref.at[:, pl.ds(at, 256)]
 
     def _copies(self, item, kind, j):
@@ -836,6 +871,7 @@
     small_own.start()
     swap_start(0)
     swap_start(1)
+    swap_start(2)
     own_x = pltpu.make_async_copy(x_any, x_v.at[:, x], t_send.at[2])
     own_x.start()
     halves = pl.ds(2 * c, 2)
@@ -843,7 +879,7 @@
     x_part = x_v.at[halves, 1 - x]
     x_on = remote(x_part, x_part, t_send.at[1], t_recv.at[1], mate)
     x_out.start()
-    for item in range(2, 6):
+    for item in range(3, 6):
         swap_start(item)
     z_out = remote(z_any.at[halves], dz_out.at[halves], z_send.at[0], z_recv.at[0], across)
     z_part = dz_out.at[halves]
@@ -855,11 +891,14 @@
     small_own.wait()
     small_out_copy.wait()
     tiny.ag_start(0)
-    for item in range(3):
+    for item in (0, 1):
         swap_end(item)
         line.ag_start(item)
     for t in range(1, n):
         tiny.ag_step(0, t)
+    line.pump(0, 1)
+    line.pump(1, 1)
+    swap_end(2)
     for s in range(2 * n):
         cols = slice(s * 256, (s + 1) * 256)
         heads_row[:, cols] = small_g[0, s]
@@ -873,22 +912,19 @@
 
     own_x.wait()
     each(4, lambda m: norm(m, x))
-    line.pump(0, 1)
-    line.pump(1, 1)
+    line.pump(0, 2)
+    line.pump(1, 2)
+    line.ag_start(2)
     x_out.wait_recv()
     x_on.start()
-    line.pump(0, 2)
-    line.pump(1, 2)
     line.pump(2, 1)
+    for item in (3, 4, 5):
+        swap_end(item)
+        line.ag_left(item)
     x_on.wait_recv()
     each(4, lambda m: norm(m, 1 - x))
-    for item in (3, 4):
-        swap_end(item)
-        line.ag_start(item)
     for item in (0, 1):
-        line.pump(item, 3)
         line.collect(item)
-    line.pump(2, 2)
 
     def project(m):
         a = normed[m].reshape(256, 256 * 2 * n)
@@ -908,7 +944,6 @@
         q_v[m, 256:] = turn(qf[:, 128:], gains[0:1])
         kv[l, m, :, :128] = turn(kf[:, :128], gains[1:2])
         kv[l, m, :, 128:] = kf[:, 128:].astype(BF)
-        pl.when(l <= n - 2)(lambda: send_kv(l, m).start())
 
     def send_kv(b, m):
         return remote(kv.at[b, m], kv.at[b, m], kv_send.at[b, m], kv_recv.at[b, m], right)
@@ -939,45 +974,12 @@
             tot[m] += total
             att[m] += value
 
-    def kv_round(t):
-        @pl.when(l - t >= 0)
-        def _():
-            b = l - t
-
-            def take(m):
-                send_kv(b, m).wait_recv()
-                pl.when(l <= n - 2)(lambda: send_kv(b, m).start())
-
-            each(4, take)
-            each(4, lambda m: attend(m, b, False))
-
-    line.pump(2, 3)
-    each(4, lambda m: attend(m, l, True))
+    line.pump(2, 2)
 
     def turned(i):
         m, s = lax.div(i, 2 * n), lax.rem(i, 2 * n)
         tile = normed[m, :, :, pl.ds(pl.multiple_of(s * 256, 256), 256)].reshape(256, 256)
         normed_t[s, :, pl.ds(pl.multiple_of(m * 256, 256), 256)] = tile.T
-
-    each(8 * n, turned)
-    put(normed_t, normed_out)
-    line.pump(3, 1)
-    line.pump(4, 1)
-    kv_round(1)
-    for item in (5,):
-        swap_end(item)
-        line.ag_start(item)
-    line.pump(3, 2)
-    line.pump(4, 2)
-    line.pump(3, 3)
-    kv_round(2)
-    swap_end(6)
-    line.ag_start(6)
-    line.pump(4, 3)
-    line.pump(5, 1)
-    line.pump(5, 2)
-    kv_round(3)
-    line.collect(2)
 
     def mate_copy(m):
         return remote(
@@ -1002,15 +1004,6 @@
             )
         mate_copy(m).start()
 
-    each(4, branch)
-    put(att, att_out)
-    put(tot, lse_out)
-    put(kv, kv_out)
-    swap_end(7)
-    line.ag_start(7)
-    line.pump(5, 3)
-    line.pump(6, 1)
-
     def chip_copy(m, o):
         ox, oy = group.other(o)
         return remote(
@@ -1031,12 +1024,35 @@
         for o in (3, 1, 2):
             chip_copy(m, o).start()
 
-    each(4, to_chips)
-    line.pump(6, 2)
-    swap_end(8)
-    line.ag_start(8)
-    line.pump(6, 3)
-    line.pump(7, 1)
+    def ahead(m):
+        pl.when(l <= n - 2)(lambda: send_kv(l, m).start())
+        attend(m, l, True)
+
+        def step(t, unused):
+            b = l - t
+            send_kv(b, m).wait_recv()
+            pl.when(l <= n - 2)(lambda: send_kv(b, m).start())
+            attend(m, b, False)
+            return 0
+
+        lax.fori_loop(1, l + 1, step, 0)
+
+    for m in range(4):
+        ahead(m)
+        if m == 0:
+            each(8 * n, turned)
+            line.collect(2)
+        branch(m)
+        if m > 0:
+            to_chips(m - 1)
+    to_chips(3)
+    for item in (3, 4, 5):
+        line.ag_right(item)
+    put(normed_t, normed_out)
+    put(att, att_out)
+    put(tot, lse_out)
+    put(kv, kv_out)
+    line.pump(3, 1)
 
     def inner_copy(m, o):
         here = inner.at[m, x, y, c]
@@ -1064,11 +1080,11 @@
 
     each(4, finish)
     put(hidden, hidden_out)
-    line.pump(7, 2)
-    line.pump(7, 3)
-    line.pump(8, 1)
+    line.pump(3, 2)
+    line.pump(4, 1)
     z_out.wait_recv()
     z_on.start()
+    line.pump(4, 2)
 
     def pass_on(m):
         for o in (1, 2, 3):
@@ -1076,11 +1092,11 @@
             inner_mate(m, o).start()
 
     each(4, pass_on)
-    line.pump(8, 2)
-    for item in (9, 10, 11):
+    line.pump(5, 1)
+    for item in range(6, 12):
         swap_end(item)
-        put(g.at[item, pl.ds(2 * l, 2)], own_out.at[item - 9])
-    line.pump(8, 3)
+        put(g.at[item, pl.ds(2 * l, 2)], own_out.at[item - 6])
+    line.pump(5, 2)
 
     def arrive(m):
         for o in range(4):
@@ -1089,9 +1105,9 @@
     each(4, arrive)
     put(inner, inner_out)
     put(small_g, small_out)
-    for item in range(3, 9):
+    for item in range(3, 6):
         line.collect(item)
-    put(g.at[pl.ds(0, 9)], g_out)
+    put(g.at[pl.ds(0, 6)], g_out)
 
     small_out_copy_done = None
     own_waits = [x_out, x_on, z_out, z_on]
@@ -1099,7 +1115,7 @@
         copy.wait_send()
     z_on.wait_recv()
     tiny.ag_end(0)
-    each(9, line.ag_end)
+    each(6, line.ag_end)
 
     def drain(m):
         mate_copy(m).wait_send()
@@ -1126,8 +1142,8 @@
     return pl.pallas_call(
         functools.partial(head_kernel, n),
         out_shape=(
-            bf(9, m, 256, 256),
-            bf(3, 2, 256, 256),
+            bf(6, m, 256, 256),
+            bf(6, 2, 256, 256),
             bf(m, 256, 1024),
             bf(n, 4, 256, 256),
             bf(4, 512, 128),
@@ -1186,7 +1202,7 @@
             DMA((4, 3)),
             DMA((4, 4)),
             DMA((4, 4)),
-            DMA((16,)),
+            DMA((24,)),
         ],
         compiler_params=pltpu.CompilerParams(
             collective_id=0, has_side_effects=True, vmem_limit_bytes=62 * 2**20
@@ -1250,19 +1266,19 @@
     l, x = line.l, line.x
     blocks = 2 * n
     width = blocks * 256
-    back = Back(line, (dgw, duw, ddw), b_send, b_recv, b_loc, 256)
+    back = Back(line, (dgw, duw, ddw), b_send, b_recv, b_loc, (512, 512, 256))
     loads = [
-        pltpu.make_async_copy(own_in, g.at[pl.ds(6, 3), pl.ds(2 * l, 2)], in_loc.at[0]),
+        pltpu.make_async_copy(own_in, g.at[pl.ds(3, 6), pl.ds(2 * l, 2)], in_loc.at[0]),
         pltpu.make_async_copy(inner_any, inner_ref, in_loc.at[1]),
         pltpu.make_async_copy(z_own, dz_ref.at[:, x], in_loc.at[2]),
         pltpu.make_async_copy(z_other, dz_ref.at[:, 1 - x], in_loc.at[3]),
-        pltpu.make_async_copy(g_in.at[pl.ds(3, 6)], g.at[pl.ds(0, 6)], in_loc.at[4]),
+        pltpu.make_async_copy(g_in.at[pl.ds(3, 3)], g.at[pl.ds(0, 3)], in_loc.at[4]),
     ]
     for copy in loads:
         copy.start()
     greet(line.partners() + [back.partner()])
     loads[0].wait()
-    for item in range(6, 9):
+    for item in range(3, 6):
         line.ag_start(item)
     for copy in loads[1:]:
         copy.wait()
@@ -1319,21 +1335,46 @@
 
         lax.fori_loop(0, blocks, weights, 0)
 
-    def items(j, body):
-        each(3, lambda i: body(3 * j + i))
+    def homeward(item):
+        line.rs_final(item)
+        back.start(item, item % 3, item // 3)
 
     compute(0)
-    for t in range(1, n):
-        items(2, lambda item, t=t: line.pump(item, t))
-        items(0, lambda item, t=t: line.rs_step(item, t))
+    for item in (0, 1, 2):
+        line.rs_fire(item)
+    for t in (1, 2):
+        for item in (3, 4, 5):
+            line.pump(item, t)
+    for item in (6, 7, 8):
+        line.ag_start(item)
+    line.rs_near(0)
+    line.rs_near(1)
+    line.rs_far(0)
+    for item in (3, 4, 5):
+        line.collect(item)
+        line.ag_end(item)
     compute(1)
-    items(0, line.rs_final)
-    for kind in range(3):
-        back.start(kind, kind, 0)
-    items(2, line.collect)
-    items(2, line.ag_end)
+    for item in (3, 4):
+        line.rs_fire(item)
+    for item in (6, 7, 8):
+        line.pump(item, 1)
+    line.rs_near(2)
+    line.rs_far(1)
+    for item in (6, 7, 8):
+        line.pump(item, 2)
+    homeward(0)
+    line.rs_near(3)
+    line.rs_far(2)
+    homeward(1)
+    line.rs_near(4)
+    line.rs_far(3)
+    homeward(2)
+    line.rs_far(4)
+    for item in (6, 7, 8):
+        line.collect(item)
+        line.ag_end(item)
     compute(2)
-    parts = pltpu.make_async_copy(g.at[pl.ds(3, 6)], part_out, o_loc.at[2])
+    parts = pltpu.make_async_copy(g.at[pl.ds(5, 4)], part_out, o_loc.at[2])
     parts.start()
 
     def flush(m, unused):
@@ -1349,9 +1390,11 @@
     ]
     for copy in outs[:2]:
         copy.start()
-    for kind in range(3):
-        back_wait(back, kind, kind, 0)
-    items(0, line.rs_end)
+    homeward(3)
+    homeward(4)
+    for item in range(5):
+        back_wait(back, item, item % 3, item // 3)
+    each(5, line.rs_end)
     for copy in outs:
         copy.wait()
 
@@ -1366,9 +1409,9 @@
         out_shape=(
             bf(4, 256, d),
             bf(4, 2, 4, 32, d),
-            bf(6, m, 256, 256),
-            bf(256, 512),
-            bf(256, 512),
+            bf(4, m, 256, 256),
+            bf(256, 1024),
+            bf(256, 1024),
             bf(512, 256),
         ),
         in_specs=[ANY] * 5,
@@ -1380,16 +1423,16 @@
             pltpu.VMEM((4, 256, d), F32),
             pltpu.VMEM((4, 256, d), F32),
             vb(9, m, 256, 256),
-            vb(3, m + 2, 256, 256),
+            vb(5, m + 2, 256, 256),
             vb(2, 1024, 256),
             vb(256, 1024),
             DMA((9, 2, n)),
             DMA((9, n)),
-            DMA((3, 2, n)),
-            DMA((3, n + 1)),
-            DMA((3,)),
-            DMA((3,)),
-            DMA((3,)),
+            DMA((5, 2, n)),
+            DMA((5, n + 1)),
+            DMA((5,)),
+            DMA((5,)),
+            DMA((5,)),
             DMA((5,)),
             DMA((3,)),
         ],
@@ -1498,12 +1541,17 @@
     width = blocks * 256
     scale = HEAD_SIZE ** (-0.5)
     first = Back(line, (dq_out, dkv_out, do_out), b_send, b_recv, b_loc, 256)
-    rest = Back(line, (dg_out, du_out, dd_out), b_send, b_recv, b_loc, 512)
+    rest = Back(line, (dg_out, du_out, dd_out), b_send, b_recv, b_loc, (256, 256, 512))
 
     def backward(item):
         if item < 3:
             return first, item, item, 0
-        return rest, item, item % 3, item // 3 - 1
+        return rest, item, (item + 2) % 3, 1 if item == 6 else 0
+
+    def homeward(item):
+        line.rs_final(item)
+        back, item, kind, j = backward(item)
+        back.start(item, kind, j)
 
     pending = {}
 
@@ -1515,7 +1563,7 @@
     load("din", din_any.at[:, :, :, c], low)
     load("hidden", hidden_any, hidden)
     load("z", z_any.at[:, k], own_z)
-    load("ffn", ffn_parts, g.at[pl.ds(3, 6)])
+    load("ffn", ffn_parts, g.at[pl.ds(3, 4)])
     load("w", g_any.at[pl.ds(0, 3)], w)
     load("kv", kv_any, kv)
     load("q", q_any, q_v)
@@ -1584,7 +1632,7 @@
     pending["hidden"].wait()
     pending["z"].wait()
     each(4, lambda m: to_chips(0, din_any, m, lambda m, u, v: low[m, u, v]))
-    line.rs_mid(3, 1)
+    line.rs_near(3)
 
     def spread(m, o):
         here = dbr.at[m, x, y, c]
@@ -1612,13 +1660,11 @@
         spread_mate(m, 0).start()
 
     each(4, finish)
-    line.rs_mid(3, 2)
     line.rs_fire(5)
-    line.rs_mid(4, 1)
-    line.rs_mid(3, 3)
     for name in ("w", "kv", "q", "att", "lse", "qp", "kp", "normed", "x"):
         pending[name].wait()
-    line.rs_mid(4, 2)
+    line.rs_near(4)
+    line.rs_far(3)
 
     def pass_on(m):
         for o in (1, 2, 3):
@@ -1630,8 +1676,7 @@
     own_low = pltpu.make_async_copy(out_any.at[:, :, :, c], low, o_loc.at[0])
     own_low.start()
     each(4, lambda m: mate_copy(1, out_any, m).start())
-    line.rs_fire(6)
-    line.rs_mid(4, 3)
+    line.rs_far(4)
 
     def arrive(m):
         for o in range(4):
@@ -1725,20 +1770,14 @@
             head_sum[0:1, :128] += total
 
     attend_back(0)
-    line.rs_mid(5, 1)
     attend_back(1)
     kv_step(0)
-    line.rs_mid(5, 2)
-    line.rs_fire(7)
     attend_back(2)
     kv_step(1)
-    line.rs_mid(5, 3)
-    line.rs_mid(6, 1)
     attend_back(3)
     kv_step(2)
     kv_step(3)
-    line.rs_mid(6, 2)
-    line.rs_fire(8)
+    line.rs_fire(6)
     each(4, query_back)
 
     def output_weights(s, unused):
@@ -1755,11 +1794,13 @@
     line.rs_fire(2)
     lax.fori_loop(0, blocks, query_weights, 0)
     line.rs_fire(0)
-    line.rs_mid(6, 3)
-    line.rs_mid(7, 1)
+    line.rs_near(5)
+    homeward(3)
     own_low.wait()
     each(4, lambda m: to_chips(1, out_any, m, lambda m, u, v: low[m, u, v]))
-    line.rs_mid(7, 2)
+    line.rs_near(6)
+    line.rs_far(5)
+    homeward(4)
 
     def key_back(m):
         pl.when(l <= n - 2)(lambda: kv_copy(l, m).wait_recv())
@@ -1814,12 +1855,12 @@
     res_home = home(0, own_res, res_out)
     for copy in res_home[:3]:
         copy.start()
-    line.rs_mid(7, 3)
-    line.rs_mid(8, 1)
-    line.rs_mid(8, 2)
+    line.rs_near(2)
+    line.rs_far(6)
+    homeward(5)
     each(4, lambda m: to_chips(2, dbr, m, lambda m, u, v: dbr[m, u, v, c]))
-    line.rs_mid(8, 3)
-    line.rs_mid(2, 1)
+    line.rs_near(0)
+    line.rs_far(2)
 
     def finish_grad(m):
         total = total_of(2, m)
@@ -1846,18 +1887,16 @@
         copy.start()
     res_home[1].wait_recv()
     res_home[3].start()
-    line.rs_mid(2, 2)
-    line.rs_mid(2, 3)
     small_c.wait()
     sums[0] = sums[0] + sum_c[...]
     small_x.start()
-    line.rs_mid(0, 1)
-    line.rs_mid(0, 2)
+    line.rs_near(1)
+    line.rs_far(0)
+    homeward(6)
     small_x.wait()
     sums[...] = sums[...] + sum_x[...]
     small_y.start()
-    line.rs_mid(0, 3)
-    line.rs_mid(1, 1)
+    homeward(2)
     small_y.wait()
     sums[0] = sums[0] + sum_y[...]
 
@@ -1874,21 +1913,18 @@
     for d in range(1, n):
         small_line(d).start()
     sum_l[l] = sums[:, pl.ds(2 * l, 2)]
-    line.rs_mid(1, 2)
-    line.rs_mid(1, 3)
+    line.rs_far(1)
     grad_home[1].wait_recv()
     grad_home[3].start()
-    for item in (3, 4, 5, 6, 7, 8, 2, 0, 1):
-        line.rs_final(item)
-        back, item, kind, j = backward(item)
-        back.start(item, kind, j)
+    homeward(0)
+    homeward(1)
     for d in range(1, n):
         small_line(d).wait()
     total = sum_l[0, :, x]
     for i in range(1, n):
         total = total + sum_l[i, :, x]
     sums_out[...] = total
-    for item in (3, 4, 5, 6, 7, 8, 2, 0, 1):
+    for item in (3, 4, 5, 6, 2, 0, 1):
         back, item, kind, j = backward(item)
         back_wait(back, item, kind, j)
     for copies in (res_home, grad_home):
@@ -1904,7 +1940,7 @@
             pl.when(l > b)(lambda b=b: kv_copy(b, m).wait_send())
 
     each(4, drain)
-    each(9, line.rs_end)
+    each(7, line.rs_end)
 
 
 def tail(n, din, out, x_in, z_in, hidden, ffn_parts, normed_t, g_all, kv, q, qp, kp, att, lse, gate, small_g, small, cosine, sine, row_lo, row_hi):
@@ -1921,16 +1957,16 @@
             bf(256, 512),
             bf(256, 512),
             bf(512, 256),
-            bf(256, 1024),
-            bf(256, 1024),
+            bf(256, 512),
+            bf(256, 512),
             bf(1024, 256),
             jax.ShapeDtypeStruct((2, 8, 256), F32),
         ),
         in_specs=[ANY] * 14 + [VM] * 7,
         out_specs=(ANY,) * 8 + (VM,),
         scratch_shapes=[
-            vb(9, m, 256, 256),
-            vb(9, m + 2, 256, 256),
+            vb(7, m, 256, 256),
+            vb(7, m + 2, 256, 256),
             vb(3, m, 256, 256),
             vb(m, 256, 1024),
             vb(4, 2, 2, 2, 32, d),
@@ -1964,11 +2000,11 @@
             vf(m, 8, 256),
             vf(n, 2, 2, 8, 256),
             DMA((13,)),
-            DMA((9, 2, n)),
-            DMA((9, n + 1)),
-            DMA((9,)),
-            DMA((9,)),
-            DMA((9,)),
+            DMA((7, 2, n)),
+            DMA((7, n + 1)),
+            DMA((7,)),
+            DMA((7,)),
+            DMA((7,)),
             DMA((n, 4)),
             DMA((n, 4)),
             DMA((3, 4)),

time: 620 us -> 549 us (0.89)
  Pallas kernels: 575 us -> 504 us
    pallas_call x1, Pallas kernels: 254 us -> 200 us  [tail(): pl.pallas_call(functools.partial(tail_kernel, n), out_shape=(bf(4, 4, 32,...]
    pallas_call x1, Pallas kernels: 192 us -> 155 us  [head(): pl.pallas_call(functools.partial(head_kernel, n), out_shape=(bf(6, m, 256...]
    pallas_call x1, Pallas kernels: 130 us -> 150 us  [ffn(): pl.pallas_call(functools.partial(ffn_kernel, n), out_shape=(bf(4, 256, d)...]
where the time goes in v4:
time: 549 us; the launch traced here: 540 us
  Pallas kernels  504 us (92%)
  local copies, waits for them, and re-layouts  17.8 us (3%)
  other arithmetic  16.5 us (3%)
    pallas_call x1, Pallas kernels, tail(): pl.pallas_call(functools.partial(tail_kernel, n), out_shape=(bf(4, 4, 32,...  200 us
    pallas_call x1, Pallas kernels, head(): pl.pallas_call(functools.partial(head_kernel, n), out_shape=(bf(6, m, 256...  155 us
    pallas_call x1, Pallas kernels, ffn(): pl.pallas_call(functools.partial(ffn_kernel, n), out_shape=(bf(4, 256, d)...  150 us

profile of v4, /device:TPU:0, one launch (start us, length us, event | category | flops | bytes accessed | tf_op | source)
XLA Modules:
  0.0 539.9 jit_solution(8085683391461560704)
XLA Ops:
  4.2 1.9 concatenate.47.small
  6.1 0.8 fusion.16
  7.3 1.0 fusion.25
  9.0 1.0 broadcast_in_dim.126.row_hi
  10.0 1.0 broadcast_in_dim.117.row_lo
  11.0 3.4 multiply_sine_fusion
  14.4 1.0 maximum_multiply_fusion.sin_ref
  15.4 1.0 pad_maximum_fusion.3.cos_ref
  16.4 154.7 %head.1 = (bf16[6,8,256,256]{3,2,1,0:T(8,128)(2,1)}, bf16[6,2,256,256]{3,2,1,0:T(8,128)(2,1)}, bf16[8,256,1024]{2,1,0:T(8,128)(2,1)}, bf16[4,4,256,256]{3,2,1,0:...) custom-call(bf16[4,4,32,2048]{3,2,1,0:T(8,128)(2,1)} %bitcast.79, ...), custom_call_target="tpu_custom_call" | custom-call | tf_op jit(solution)/shard_map/head/pallas_call | solution.py:1142
  171.1 149.5 %ffn.1 = (bf16[4,256,2048]{2,1,0:T(8,128)(2,1)}, bf16[4,2,4,32,2048]{4,3,2,1,0:T(8,128)(2,1)}, bf16[4,8,256,256]{3,2,1,0:T(8,128)(2,1)}, bf16[256,1024]{1,0:T(8,...) custom-call(bf16[4,256,2048]{2,1,0:T(8,128)(2,1)} %bitcast.83, bf16[4,4,32,2048]{3,2,1,0:T(8,128)(2,1)} %bitcast.77, ...), custom_call_target="tpu_custom_call" | custom-call | tf_op jit(solution)/shard_map/ffn/pallas_call | solution.py:1407
  320.6 200.1 %tail.1 = (bf16[4,4,32,2048]{3,2,1,0:T(8,128)(2,1)}, bf16[4,4,32,2048]{3,2,1,0:T(8,128)(2,1)}, bf16[256,512]{1,0:T(8,128)(2,1)}, bf16[256,512]{1,0:T(8,128)(2,1)...) custom-call(bf16[4,2,2,2,32,2048]{5,4,3,2,1,0:T(8,128)(2,1)} %bitcas, ...), custom_call_target="tpu_custom_call" | custom-call | tf_op jit(solution)/shard_map/tail/pallas_call | solution.py:1952
  520.8 1.3 slice_bitcast_fusion.1
  522.0 1.3 fusion.27
  523.4 1.3 slice_bitcast_fusion
  524.7 1.0 fusion.24
  527.1 1.8 convert_element_type.53
  529.9 0.8 copy-done.4
  530.9 1.2 pad_maximum_fusion.2
  532.3 1.3 pad_maximum_fusion
  533.7 1.3 pad_maximum_fusion.1
  535.0 0.9 copy-done.1
  535.8 1.3 copy.32
  537.2 1.0 copy-done
  538.2 1.3 copy.33
  (52 shorter events, 7.3 us)
Async XLA Ops:
  520.8 8.1 %copy-start.8 = (bf16[512,256]{1,0:T(8,128)(2,1)S(1)}, bf16[512,256]{1,0:T(8,128)(2,1)}, u32[]{:S(2)}) copy-start(bf16[512,256]{1,0:T(8,128)(2,1)} %get-tuple-element.65) | copy-start | bytes 786436
  520.8 8.9 %copy-start.7 = (bf16[256,512]{1,0:T(8,128)(2,1)S(1)}, bf16[256,512]{1,0:T(8,128)(2,1)}, u32[]{:S(2)}) copy-start(bf16[256,512]{1,0:T(8,128)(2,1)} %get-tuple-element.67) | copy-start | bytes 786436
  526.4 3.4 copy-start.6
  528.9 1.0 copy-start.5
  529.7 1.1 copy-start.4
  530.9 1.3 copy-start.3
  532.2 1.3 copy-start.2
  533.7 2.2 copy-start.1
  535.8 2.3 copy-start

commit v5 on v0

--- a/solution.py
+++ b/solution.py
@@ -1,8 +1,11 @@
+import functools
 import math
 
 import jax
 import jax.numpy as jnp
 from jax import lax
+from jax.experimental import pallas as pl
+from jax.experimental.pallas import tpu as pltpu
 from jax.sharding import PartitionSpec as P
 
 HEAD_SIZE = 128
@@ -450,7 +453,1386 @@
     )
 
 
+BF = jnp.bfloat16
+F32 = jnp.float32
+ANY = pl.BlockSpec(memory_space=pl.ANY)
+VM = pl.BlockSpec(memory_space=pltpu.VMEM)
+DMA = pltpu.SemaphoreType.DMA
+
+
+def place():
+    s = lax.axis_index("seq")
+    k = lax.axis_index("kv")
+    return (lax.div(s, 2), lax.rem(s, 2), lax.div(k, 2), lax.rem(k, 2))
+
+
+def device(l, x, y, c):
+    return (l * 2 + x, y * 2 + c)
+
+
+def remote(src, dst, send, recv, target):
+    return pltpu.make_async_remote_copy(
+        src_ref=src,
+        dst_ref=dst,
+        send_sem=send,
+        recv_sem=recv,
+        device_id=target,
+        device_id_type=pl.DeviceIdType.MESH,
+    )
+
+
+def greet(partners):
+    barrier = pltpu.get_barrier_semaphore()
+    count = 0
+    for target, there in partners:
+
+        def call(target=target):
+            pl.semaphore_signal(
+                barrier, inc=1, device_id=target, device_id_type=pl.DeviceIdType.MESH
+            )
+
+        if there is None:
+            call()
+            count = count + 1
+        else:
+            pl.when(there)(call)
+            count = count + jnp.where(there, 1, 0)
+    pl.semaphore_wait(barrier, count)
+
+
+class Line:
+    def __init__(self, length, g, ag_send, ag_recv, land=None, rs_send=None, rs_recv=None):
+        self.n = length
+        self.g, self.ag_send, self.ag_recv = g, ag_send, ag_recv
+        self.land, self.rs_send, self.rs_recv = land, rs_send, rs_recv
+        self.l, self.x, self.y, self.c = place()
+
+    def partners(self):
+        l, x, y, c = self.l, self.x, self.y, self.c
+        return [
+            (device(l - 1, x, y, c), l >= 1),
+            (device(l + 1, x, y, c), l <= self.n - 2),
+        ]
+
+    def block(self, item, b):
+        return self.g.at[item, pl.ds(2 * b, 2)]
+
+    def _ag(self, item, way, b):
+        step = -1 if way == 0 else 1
+        return remote(
+            self.block(item, b),
+            self.block(item, b),
+            self.ag_send.at[item, way, b],
+            self.ag_recv.at[item, b],
+            device(self.l + step, self.x, self.y, self.c),
+        )
+
+    def ag_start(self, item):
+        l = self.l
+        pl.when(l >= 1)(lambda: self._ag(item, 0, l).start())
+        pl.when(l <= self.n - 2)(lambda: self._ag(item, 1, l).start())
+
+    def ag_left(self, item):
+        pl.when(self.l >= 1)(lambda: self._ag(item, 0, self.l).start())
+
+    def ag_right(self, item):
+        l, n = self.l, self.n
+        pl.when((l >= 1) & (l <= n - 2))(lambda: self._ag(item, 1, l).start())
+
+    def ag_right_end(self, item):
+        pl.when(self.l == 0)(lambda: self._ag(item, 1, self.l).start())
+
+    def ag_step(self, item, t):
+        l, n = self.l, self.n
+
+        @pl.when(l + t <= n - 1)
+        def _():
+            self._ag(item, 0, l + t).wait_recv()
+            pl.when(l >= 1)(lambda: self._ag(item, 0, l + t).start())
+
+        @pl.when(l - t >= 0)
+        def _():
+            self._ag(item, 1, l - t).wait_recv()
+            pl.when(l <= n - 2)(lambda: self._ag(item, 1, l - t).start())
+
+    def pump(self, item, t):
+        l, n = self.l, self.n
+
+        @pl.when((l + t <= n - 1) & (l >= 1))
+        def _():
+            self._ag(item, 0, l + t).wait_recv()
+            self._ag(item, 0, l + t).start()
+
+        @pl.when((l - t >= 0) & (l <= n - 2))
+        def _():
+            self._ag(item, 1, l - t).wait_recv()
+            self._ag(item, 1, l - t).start()
+
+    def collect(self, item):
+        l, n = self.l, self.n
+        for t in range(1, n):
+            pl.when(l == 0)(lambda t=t: self._ag(item, 0, t).wait_recv())
+            pl.when(l == n - 1)(lambda t=t: self._ag(item, 1, n - 1 - t).wait_recv())
+
+    def ag_end(self, item):
+        l, n = self.l, self.n
+        for b in range(n):
+            pl.when((l >= 1) & (l <= b))(lambda b=b: self._ag(item, 0, b).wait_send())
+            pl.when((l <= n - 2) & (l >= b))(lambda b=b: self._ag(item, 1, b).wait_send())
+
+    @staticmethod
+    def seat(item):
+        return item + 3 if item < 3 else item
+
+    @staticmethod
+    def berth(item):
+        return item + 3 if item < 3 else (item - 3) % 6
+
+    def sum_block(self, item, b):
+        return self.g.at[self.seat(item), pl.ds(2 * b, 2)]
+
+    def _slot(self, item, slot):
+        return self.land.at[self.berth(item), pl.ds(2 * slot, 2)]
+
+    def _rs(self, item, way, o):
+        if way == 0:
+            target = self.l - 1
+            slot = jnp.where(target == o, self.n, o)
+        else:
+            target = self.l + 1
+            slot = o
+        return remote(
+            self.sum_block(item, o),
+            self._slot(item, slot),
+            self.rs_send.at[item, way, o],
+            self.rs_recv.at[item, slot],
+            device(target, self.x, self.y, self.c),
+        )
+
+    def _take(self, item, o, slot):
+        here = self._slot(item, slot)
+        pltpu.make_async_copy(here, here, self.rs_recv.at[item, slot]).wait()
+        seat, berth = self.seat(item), self.berth(item)
+        for h in range(2):
+            total = self.g[seat, 2 * o + h].astype(F32) + self.land[berth, 2 * slot + h].astype(F32)
+            self.g[seat, 2 * o + h] = total.astype(BF)
+
+    def rs_fire(self, item):
+        l, n = self.l, self.n
+        for o in range(n - 1, 0, -1):
+            pl.when(l == 0)(lambda o=o: self._rs(item, 1, o).start())
+            pl.when(l == n - 1)(lambda o=o: self._rs(item, 0, n - 1 - o).start())
+
+    def rs_near(self, item):
+        l, n = self.l, self.n
+
+        @pl.when(l == 1)
+        def _():
+            for o in range(n - 1, 1, -1):
+                self._take(item, o, o)
+                self._rs(item, 1, o).start()
+
+        @pl.when(l == n - 2)
+        def _():
+            for o in range(n - 2):
+                self._take(item, o, o)
+                self._rs(item, 0, o).start()
+
+    def rs_far(self, item):
+        l, n = self.l, self.n
+
+        @pl.when(l == 1)
+        def _():
+            self._take(item, 0, 0)
+            self._rs(item, 0, 0).start()
+
+        @pl.when(l == n - 2)
+        def _():
+            self._take(item, n - 1, n - 1)
+            self._rs(item, 1, n - 1).start()
+
+    def rs_final(self, item):
+        l, n = self.l, self.n
+        pl.when(l >= 1)(lambda: self._take(item, l, l))
+        pl.when(l <= n - 2)(lambda: self._take(item, l, n))
+
+    def rs_end(self, item):
+        l, n = self.l, self.n
+        for o in range(n):
+            pl.when(l < o)(lambda o=o: self._rs(item, 1, o).wait_send())
+            pl.when(l > o)(lambda o=o: self._rs(item, 0, o).wait_send())
+
+
+def each(count, body):
+    def step(i, unused):
+        body(i)
+        return 0
+
+    lax.fori_loop(0, count, step, 0)
+
+
+class Pair:
+    def __init__(self, line, refs, send, recv, local, half):
+        self.line, self.refs = line, refs
+        self.send, self.recv, self.local, self.half = send, recv, local, half
+
+    def partner(self):
+        line = self.line
+        return (device(line.l, 1 - line.x, line.y, line.c), None)
+
+    def _part(self, ref, kind, j, x):
+        half = self.half if isinstance(self.half, int) else self.half[kind]
+        at = pl.multiple_of(x * half + j * 256, 256)
+        return ref.at[pl.ds(at, 256), :] if kind == 2 else ref.at[:, pl.ds(at, 256)]
+
+    def _copies(self, item, kind, j):
+        line = self.line
+        mine = line.g.at[item, 2 * line.l + line.x]
+        out = remote(
+            self._part(self.refs[kind], kind, j, 1 - line.x),
+            mine,
+            self.send.at[item],
+            self.recv.at[item],
+            self.partner()[0],
+        )
+        here = pltpu.make_async_copy(
+            self._part(self.refs[kind], kind, j, line.x), mine, self.local.at[item]
+        )
+        return out, here
+
+    def start(self, item, kind, j):
+        for copy in self._copies(item, kind, j):
+            copy.start()
+
+    def end(self, item, kind, j):
+        out, here = self._copies(item, kind, j)
+        here.wait()
+        out.wait_send()
+        out.wait_recv()
+
+
+class Back(Pair):
+    def _copies(self, item, kind, j):
+        line = self.line
+        home = self._part(self.refs[kind], kind, j, line.x)
+        out = remote(
+            line.g.at[line.seat(item), 2 * line.l + 1 - line.x],
+            home,
+            self.send.at[item],
+            self.recv.at[item],
+            self.partner()[0],
+        )
+        here = pltpu.make_async_copy(
+            line.g.at[line.seat(item), 2 * line.l + line.x], home, self.local.at[item]
+        )
+        return out, here
+
+
+def back_wait(back, item, kind, j):
+    line = back.line
+    out, here = back._copies(item, kind, j)
+    here.wait()
+    out.wait_send()
+    there = back._part(back.refs[kind], kind, j, 1 - line.x)
+    pltpu.make_async_copy(there, there, back.recv.at[item]).wait()
+
+
+def dot(a, b):
+    return lax.dot_general(a, b, (((1,), (0,)), ((), ())), preferred_element_type=F32)
+
+
+def dot_t(a, b):
+    return lax.dot_general(a, b, (((1,), (1,)), ((), ())), preferred_element_type=F32)
+
+
+def layer_kernel(
+    n,
+    x_any,
+    z_any,
+    wq,
+    wkv,
+    wo,
+    wg,
+    wu,
+    wd,
+    small,
+    cos_ref,
+    sin_ref,
+    row_range,
+    res_out,
+    grad_out,
+    dq_out,
+    dkv_out,
+    do_out,
+    dgw,
+    duw,
+    ddw,
+    sums_out,
+    late_out,
+    normed_out,
+    dz_out,
+    x_v,
+    normed,
+    normed_t,
+    g,
+    small_g,
+    gain_row,
+    heads_row,
+    kv,
+    q_v,
+    qp,
+    kp,
+    gate_v,
+    att,
+    tot,
+    part,
+    core_land,
+    low,
+    chip_land,
+    inner,
+    hidden,
+    land,
+    d_low,
+    prod_t,
+    kv_land,
+    d_hid,
+    own_z,
+    own_x,
+    dl,
+    dl_t,
+    gain_sum,
+    head_sum,
+    sums,
+    sum_c,
+    sum_x,
+    sum_y,
+    sum_l,
+    late,
+    late_core,
+    late_chip,
+    late_l,
+    p_send,
+    p_recv,
+    p_loc,
+    ag_send,
+    ag_recv,
+    sp_sem,
+    sa_send,
+    sa_recv,
+    t_send,
+    t_recv,
+    z_send,
+    z_recv,
+    kv_send,
+    kv_recv,
+    c_send,
+    c_recv,
+    s_send,
+    s_recv,
+    i_send,
+    i_recv,
+    j_send,
+    j_recv,
+    rs_send,
+    rs_recv,
+    b_send,
+    b_recv,
+    b_loc,
+    d_send,
+    d_recv,
+    h_send,
+    h_recv,
+    u_send,
+    u_recv,
+    o_loc,
+):
+    line = Line(n, g, ag_send, ag_recv, land, rs_send, rs_recv)
+    l, x, y, c = line.l, line.x, line.y, line.c
+    k = y * 2 + c
+    group = Group()
+    across, mate = device(l, 1 - x, y, c), group.mate
+    right = device(l + 1, x, y, c)
+    tiny = Line(n, small_g, sa_send, sa_recv)
+    scale = HEAD_SIZE ** (-0.5)
+    width = 256 * 2 * n
+    back = Back(line, (dgw, duw, ddw), b_send, b_recv, b_loc, 768)
+    back_first = Back(line, (dq_out, dkv_out, do_out), b_send, b_recv, b_loc, 256)
+    left = device(l - 1, x, y, c)
+    blocks = 2 * n
+    first = Pair(line, (wq, wkv, wo), p_send, p_recv, p_loc, 256)
+    rest = Pair(line, (wg, wu, wd), p_send, p_recv, p_loc, 768)
+
+    def swap(item):
+        if item < 3:
+            return first, item, item, 0
+        return rest, item, item % 3, item // 3 - 1
+
+    def swap_start(item):
+        pair, item, kind, j = swap(item)
+        pair.start(item, kind, j)
+
+    def swap_end(item):
+        pair, item, kind, j = swap(item)
+        pair.end(item, kind, j)
+
+    used = iter(range(16))
+
+    def put(src, dst):
+        copy = pltpu.make_async_copy(src, dst, o_loc.at[next(used)])
+        copy.start()
+        return copy
+
+    others = [device(lax.rem(l + d, n), x, y, c) for d in range(1, n)]
+    greet(
+        [(o, None) for o in others] + [(mate, None)] + [(group.chip(i), None) for i in (1, 2, 3)]
+    )
+
+    small_here = small_g.at[0, 2 * l + x]
+    small_out_copy = remote(small, small_here, sp_sem.at[0], sp_sem.at[1], across)
+    small_own = pltpu.make_async_copy(small, small_here, sp_sem.at[2])
+    swap_start(0)
+    small_out_copy.start()
+    small_own.start()
+    swap_start(1)
+    swap_start(2)
+    x_here = pltpu.make_async_copy(x_any, x_v.at[:, x], t_send.at[2])
+    x_here.start()
+    halves = pl.ds(2 * c, 2)
+    x_out = remote(x_any.at[halves], x_v.at[halves, x], t_send.at[0], t_recv.at[0], across)
+    x_part = x_v.at[halves, 1 - x]
+    x_on = remote(x_part, x_part, t_send.at[1], t_recv.at[1], mate)
+    x_out.start()
+    for item in range(3, 12):
+        swap_start(item)
+    z_out = remote(z_any.at[halves], dz_out.at[halves], z_send.at[0], z_recv.at[0], across)
+    z_part = dz_out.at[halves]
+    z_on = remote(z_part, z_part, z_send.at[1], z_recv.at[1], mate)
+    z_out.start()
+
+    swap_end(0)
+    line.ag_start(0)
+    small_own.wait()
+    small_out_copy.wait()
+    tiny.ag_start(0)
+    swap_end(1)
+    line.ag_start(1)
+    for t in range(1, n):
+        tiny.ag_step(0, t)
+    line.pump(0, 1)
+    line.pump(1, 1)
+    swap_end(2)
+    for s in range(2 * n):
+        cols = slice(s * 256, (s + 1) * 256)
+        heads_row[:, cols] = small_g[0, s]
+        gain_row[:, cols] = small_g[0, s, 4:6, :].astype(F32)
+
+    def norm(m, side):
+        v = x_v[m, side].reshape(128, 256 * 2 * n).astype(F32)
+        mean = jnp.mean(v * v, axis=-1, keepdims=True)
+        v = v * lax.rsqrt(mean + EPS) * gain_row[0:1, :]
+        normed[m, side] = v.astype(BF).reshape(2, 2, 32, 256 * 2 * n)
+
+    x_here.wait()
+    each(4, lambda m: norm(m, x))
+    line.pump(0, 2)
+    line.pump(1, 2)
+    line.ag_start(2)
+    x_out.wait_recv()
+    x_on.start()
+    line.pump(2, 1)
+    for item in (3, 4):
+        swap_end(item)
+        line.ag_left(item)
+    x_on.wait_recv()
+    each(4, lambda m: norm(m, 1 - x))
+    for item in (0, 1):
+        line.collect(item)
+
+    def project(m):
+        a = normed[m].reshape(256, 256 * 2 * n)
+        qf = dot(a, g[0].reshape(256 * 2 * n, 256))
+        kf = dot(a, g[1].reshape(256 * 2 * n, 256))
+        gate_v[m] = jax.nn.sigmoid(dot_t(a, heads_row[...]))
+        qp[m] = qf
+        kp[m] = kf[:, :128]
+        cosine, sine = cos_ref[m], sin_ref[m]
+
+        def turn(u, gain):
+            u = u * lax.rsqrt(jnp.mean(u * u, axis=-1, keepdims=True) + EPS) * gain
+            return (u * cosine + pltpu.roll(u, 64, 1) * sine).astype(BF)
+
+        gains = small[8:10, :128].astype(F32)
+        q_v[m, :256] = turn(qf[:, :128], gains[0:1])
+        q_v[m, 256:] = turn(qf[:, 128:], gains[0:1])
+        kv[l, m, :, :128] = turn(kf[:, :128], gains[1:2])
+        kv[l, m, :, 128:] = kf[:, 128:].astype(BF)
+
+    def send_kv(b, m):
+        return remote(kv.at[b, m], kv.at[b, m], kv_send.at[b, m], kv_recv.at[b, m], right)
+
+    each(4, project)
+    z_copy = put(z_any.at[:, k], own_z)
+    x_copy = put(x_any.at[:, k], own_x)
+
+    def attend(m, b, diagonal):
+        pair = kv[b, m]
+        raw = dot_t(q_v[m], pair[:, :128]) * scale
+        lo = row_range[m][:, :1] - b * 256
+        hi = row_range[m][:, 1:2] - b * 256
+        column = lax.broadcasted_iota(jnp.int32, (512, 256), 1)
+        allowed = (column >= jnp.concatenate([lo, lo], axis=0)) & (
+            column < jnp.concatenate([hi, hi], axis=0)
+        )
+        e = jnp.where(allowed, jnp.exp(raw), 0.0)
+        total = jnp.sum(e, axis=-1, keepdims=True)
+        value = dot(e.astype(BF), pair[:, 128:])
+        total = jnp.broadcast_to(total, (512, 128))
+        if diagonal:
+            tot[m] = total
+            att[m] = value
+        else:
+            tot[m] += total
+            att[m] += value
+
+    line.pump(2, 2)
+
+    def turned(i):
+        m, s = lax.div(i, 2 * n), lax.rem(i, 2 * n)
+        tile = normed[m, :, :, :, :, pl.ds(pl.multiple_of(s * 256, 256), 256)].reshape(256, 256)
+        normed_t[s, :, pl.ds(pl.multiple_of(m * 256, 256), 256)] = tile.T
+
+    def branch(m):
+        total = tot[m]
+        lse = jnp.log(total)
+        value = att[m] / total
+        att[m] = value
+        tot[m] = lse
+        gates = gate_v[m]
+        lo, hi = gates[:, 0:2], gates[:, 2:4]
+        gates = jnp.where(x == 0, lo, hi)
+        mixed = jnp.concatenate(
+            [value[:256] * gates[:, 0:1], value[256:] * gates[:, 1:2]], axis=1
+        ).astype(BF)
+        for s in range(2 * n):
+            part[m, :, :, :, :, s * 256 : (s + 1) * 256] = (
+                dot(mixed, g[2, s]).astype(BF).reshape(2, 2, 2, 32, 256)
+            )
+        mate_copy(m).start()
+
+    sources = (part, normed, part, normed)
+
+    def mate_place(m, r):
+        return x_v.at[m, :, pl.ds(0, 2)] if r == 2 else core_land.at[m]
+
+    def chip_place(m, o, r):
+        return x_v.at[m, (o - 1) // 2, 2 + (o - 1) % 2] if r == 2 else chip_land.at[o - 1, m]
+
+    def mate_copy(m, r=0):
+        return remote(
+            sources[r].at[m, :, :, 1 - c], mate_place(m, r), c_send.at[r, m], c_recv.at[r, m], mate
+        )
+
+    def chip_copy(m, o, r=0):
+        ox, oy = group.other(o)
+        return remote(
+            low.at[m, ox, oy],
+            chip_place(m, o, r),
+            s_send.at[r, m, o - 1],
+            s_recv.at[r, m, o - 1],
+            group.chip(o),
+        )
+
+    def to_chips(m, r=0):
+        mate_copy(m, r).wait_recv()
+        for u in range(2):
+            for v in range(2):
+                there = x_v[m, u, v] if r == 2 else core_land[m, u, v]
+                low[m, u, v] = (sources[r][m, u, v, c].astype(F32) + there.astype(F32)).astype(BF)
+        for o in (3, 1, 2):
+            chip_copy(m, o, r).start()
+
+    def total_of(m, r=0):
+        total = low[m, x, y].astype(F32)
+        for o in (1, 2, 3):
+            chip_copy(m, o, r).wait_recv()
+            there = x_v[m, (o - 1) // 2, 2 + (o - 1) % 2] if r == 2 else chip_land[o - 1, m]
+            total = total + there.astype(F32)
+        return total
+
+    def sum_end(m, r=0):
+        mate_copy(m, r).wait_send()
+        for o in (1, 2, 3):
+            chip_copy(m, o, r).wait_send()
+
+    def ahead(m):
+        pl.when(l <= n - 2)(lambda: send_kv(l, m).start())
+        attend(m, l, True)
+
+        def step(t, unused):
+            b = l - t
+            send_kv(b, m).wait_recv()
+            pl.when(l <= n - 2)(lambda: send_kv(b, m).start())
+            attend(m, b, False)
+            return 0
+
+        lax.fori_loop(1, l + 1, step, 0)
+
+    for m in range(4):
+        ahead(m)
+        if m == 0:
+            each(8 * n, turned)
+            line.collect(2)
+            normed_copy = put(normed_t, normed_out)
+        branch(m)
+        if m > 0:
+            to_chips(m - 1)
+        for item in (3 + 2 * m + 2, 3 + 2 * m + 3):
+            if item < 12:
+                swap_end(item)
+                line.ag_left(item)
+    to_chips(3)
+    for item in range(3, 12):
+        line.ag_right_end(item)
+    for item in (3, 4, 5):
+        line.ag_right(item)
+    for item in (3, 4, 5):
+        line.pump(item, 1)
+
+    def inner_copy(m, o, r=0):
+        here = inner.at[m, x, y, c]
+        return remote(
+            here, here, i_send.at[r, m, o - 1], i_recv.at[r, m, o - 1], group.chip(o)
+        )
+
+    def inner_mate(m, o, r=0):
+        ox, oy = group.other(o)
+        there = inner.at[m, ox, oy, c]
+        return remote(there, there, j_send.at[r, m, o], j_recv.at[r, m, o], mate)
+
+    def finish(m):
+        h = x_v[m, x, k].astype(F32) + total_of(m)
+        hidden[m] = h
+        mean = jnp.mean(h * h, axis=-1, keepdims=True)
+        inner[m, x, y, c] = (h * lax.rsqrt(mean + EPS) * gain_row[1:2, :]).astype(BF)
+        for o in (3, 1, 2):
+            inner_copy(m, o).start()
+        inner_mate(m, 0).start()
+
+    each(4, finish)
+    for item in (3, 4, 5):
+        line.pump(item, 2)
+    for item in (6, 7, 8):
+        line.ag_right(item)
+    z_out.wait_recv()
+    z_on.start()
+
+    def pass_on(m, r=0):
+        for o in (1, 2, 3):
+            inner_copy(m, o, r).wait_recv()
+            inner_mate(m, o, r).start()
+
+    each(4, pass_on)
+    for item in (6, 7, 8):
+        line.pump(item, 1)
+    x_out.wait_send()
+    x_on.wait_send()
+    z_on.wait_recv()
+    dz_own = pltpu.make_async_copy(z_any, x_v.at[:, x], z_send.at[2])
+    dz_other = pltpu.make_async_copy(dz_out, x_v.at[:, 1 - x], z_send.at[3])
+    dz_own.start()
+    dz_other.start()
+
+    def arrive(m, r=0):
+        for o in range(4):
+            inner_mate(m, o, r).wait_recv()
+
+    def spread_end(m, r=0):
+        for o in (1, 2, 3):
+            inner_copy(m, o, r).wait_send()
+        for o in range(4):
+            inner_mate(m, o, r).wait_send()
+
+    each(4, arrive)
+    normed_copy.wait()
+
+    def turn_inner(i):
+        m, s = lax.div(i, 2 * n), lax.rem(i, 2 * n)
+        tile = inner[m, :, :, :, :, pl.ds(pl.multiple_of(s * 256, 256), 256)].reshape(256, 256)
+        normed_t[s, :, pl.ds(pl.multiple_of(m * 256, 256), 256)] = tile.T
+
+    each(8 * n, turn_inner)
+    each(4, sum_end)
+    each(4, spread_end)
+
+    def kv_sent(m):
+        for b in range(n):
+            pl.when((l >= b) & (l <= n - 2))(lambda b=b: send_kv(b, m).wait_send())
+
+    each(4, kv_sent)
+    dz_own.wait()
+    dz_other.wait()
+
+    def compute(j):
+        base = 3 * j + 3
+
+        def rows(m, unused):
+            a = inner[m].reshape(256, width)
+            d = x_v[m].reshape(256, width)
+            gated = dot(a, g[base].reshape(width, 256))
+            upward = dot(a, g[base + 1].reshape(width, 256))
+            grad = dot_t(d[:, :256], g[base + 2, 0])
+            for s in range(1, 2 * n):
+                grad = grad + dot_t(d[:, s * 256 : (s + 1) * 256], g[base + 2, s])
+            sigma = jax.nn.sigmoid(gated)
+            swish = gated * sigma
+            product = (swish * upward).astype(BF)
+            d_gated = (grad * upward * sigma * (1.0 + gated * (1.0 - sigma))).astype(BF)
+            d_upward = (grad * swish).astype(BF)
+            at = pl.ds(pl.multiple_of(m * 256, 256), 256)
+            d_low[0, at] = d_gated
+            d_low[1, at] = d_upward
+            prod_t[:, at] = product.T
+            for s in range(2 * n):
+                cols = slice(s * 256, (s + 1) * 256)
+                o = dot(product, g[base + 2, s])
+                i = dot_t(d_gated, g[base, s]) + dot_t(d_upward, g[base + 1, s])
+                if j > 0:
+                    o = o + part[m, :, :, :, :, cols].reshape(256, 256).astype(F32)
+                    i = i + normed[m, :, :, :, :, cols].reshape(256, 256).astype(F32)
+                part[m, :, :, :, :, cols] = o.astype(BF).reshape(2, 2, 2, 32, 256)
+                normed[m, :, :, :, :, cols] = i.astype(BF).reshape(2, 2, 2, 32, 256)
+            return 0
+
+        lax.fori_loop(0, 4, rows, 0)
+
+        def weights(s, unused):
+            t = normed_t[s]
+            g[base, s] = dot(t, d_low[0]).astype(BF)
+            g[base + 1, s] = dot(t, d_low[1]).astype(BF)
+            z = x_v[:, :, :, :, pl.ds(pl.multiple_of(s * 256, 256), 256)].reshape(1024, 256)
+            g[base + 2, s] = dot(prod_t[...], z).astype(BF)
+            return 0
+
+        lax.fori_loop(0, 2 * n, weights, 0)
+
+    def backward(item):
+        if item < 3:
+            return back_first, item, item, 0
+        return back, item, item % 3, item // 3 - 1
+
+    def homeward(item):
+        line.rs_final(item)
+        way, item, kind, j = backward(item)
+        way.start(item, kind, j)
+
+    inside = (l >= 1) & (l <= n - 2)
+
+    def homeward_in(item):
+        pl.when(inside)(lambda: homeward(item))
+
+    def homeward_end(item):
+        pl.when(jnp.logical_not(inside))(lambda: homeward(item))
+
+    for item in (3, 4, 5):
+        line.collect(item)
+        line.ag_end(item)
+    compute(0)
+    for item in (3, 4, 5):
+        line.rs_fire(item)
+    for item in (6, 7, 8):
+        line.pump(item, 2)
+    for item in (9, 10, 11):
+        line.ag_right(item)
+    for item in (9, 10, 11):
+        line.pump(item, 1)
+    line.rs_near(3)
+    line.rs_near(4)
+    for item in (6, 7, 8):
+        line.collect(item)
+        line.ag_end(item)
+    compute(1)
+    for item in (6, 7, 8):
+        line.rs_fire(item)
+    for item in (9, 10, 11):
+        line.pump(item, 2)
+    line.rs_near(5)
+    homeward_in(3)
+    line.rs_far(3)
+    homeward_in(4)
+    line.rs_far(4)
+    line.rs_near(6)
+    homeward_in(5)
+    line.rs_far(5)
+    line.rs_near(7)
+    for item in (9, 10, 11):
+        line.collect(item)
+        line.ag_end(item)
+    compute(2)
+    each(4, lambda m: mate_copy(m, 1).start())
+    for item in (3, 4, 5):
+        homeward_end(item)
+    for item in (9, 10, 11):
+        line.rs_fire(item)
+    gain_sum[...] = jnp.zeros_like(gain_sum)
+    head_sum[...] = jnp.zeros_like(head_sum)
+    homeward_in(6)
+    line.rs_far(6)
+    each(4, lambda m: to_chips(m, 1))
+    line.rs_near(8)
+    homeward_in(7)
+    line.rs_far(7)
+    homeward_in(8)
+    line.rs_far(8)
+    z_copy.wait()
+    x_copy.wait()
+    normed_back_copy = put(normed_out, normed_t)
+
+    def finish_hidden(m):
+        total = total_of(m, 1)
+        h = hidden[m]
+        r = lax.rsqrt(jnp.mean(h * h, axis=-1, keepdims=True) + EPS)
+        normal = h * r
+        gain_sum[1:2] += jnp.sum(total * normal, axis=0, keepdims=True)
+        e = total * gain_row[1:2, :]
+        grad = own_z[m].astype(F32) + r * (
+            e - normal * jnp.mean(e * normal, axis=-1, keepdims=True)
+        )
+        d_hid[m] = grad
+        inner[m, x, y, c] = grad.astype(BF)
+        for o in (3, 1, 2):
+            inner_copy(m, o, 1).start()
+        inner_mate(m, 0, 1).start()
+
+    each(4, finish_hidden)
+    each(4, lambda m: sum_end(m, 1))
+    for item in (6, 7, 8):
+        homeward_end(item)
+    line.rs_near(9)
+    each(4, lambda m: pass_on(m, 1))
+    each(4, lambda m: mate_copy(m, 2).start())
+    line.rs_near(10)
+    line.rs_far(9)
+
+    def attend_back(m):
+        arrive(m, 1)
+        d = inner[m].reshape(256, width)
+        gm = dot_t(d[:, :256], g[2, 0])
+        for s in range(1, blocks):
+            gm = gm + dot_t(d[:, s * 256 : (s + 1) * 256], g[2, s])
+        gates = gate_v[m]
+        gates = jnp.where(x == 0, gates[:, 0:2], gates[:, 2:4])
+        g0, g1 = gates[:, 0:1], gates[:, 1:2]
+        a0, a1 = att[m, :256], att[m, 256:]
+        d0, d1 = gm[:, :128], gm[:, 128:]
+        l0 = jnp.sum(d0 * a0, axis=-1, keepdims=True) * g0 * (1.0 - g0)
+        l1 = jnp.sum(d1 * a1, axis=-1, keepdims=True) * g1 * (1.0 - g1)
+        lane = lax.broadcasted_iota(jnp.int32, (256, 128), 1)
+        logits = jnp.where(lane == 2 * x, l0, 0.0) + jnp.where(lane == 2 * x + 1, l1, 0.0)
+        logits = logits.astype(BF)
+        dl[m] = logits
+        at = pl.ds(pl.multiple_of(m * 256, 256), 256)
+        dl_t[:, at] = logits.T[:16]
+        mixed = jnp.concatenate([a0 * g0, a1 * g1], axis=1).astype(BF)
+        prod_t[:, at] = mixed.T
+        da = jnp.concatenate([d0 * g0, d1 * g1], axis=0).astype(BF)
+        delta = jnp.sum(da.astype(F32) * att[m], axis=-1, keepdims=True)
+        log_total = tot[m][:, :1]
+        qm = q_v[m]
+        att[m] = jnp.zeros((512, 128), F32)
+
+        def block(b, unused):
+            pair = kv[b, m]
+            keys, values = pair[:, :128], pair[:, 128:]
+            raw = dot_t(qm, keys) * scale
+            lo = row_range[m][:, :1] - b * 256
+            hi = row_range[m][:, 1:2] - b * 256
+            column = lax.broadcasted_iota(jnp.int32, (512, 256), 1)
+            allowed = (column >= jnp.concatenate([lo, lo], axis=0)) & (
+                column < jnp.concatenate([hi, hi], axis=0)
+            )
+            p = jnp.where(allowed, jnp.exp(raw - log_total), 0.0)
+            ds = (p * (dot_t(da, values) - delta)).astype(BF)
+            att[m] += dot(ds, keys)
+            dk = dot(ds.T, qm) * scale
+            dv = dot(p.astype(BF).T, da)
+            kv[b, m] = jnp.concatenate([dk, dv], axis=1).astype(BF)
+            return 0
+
+        lax.fori_loop(0, l + 1, block, 0)
+
+    def kv_copy(b, m):
+        return remote(
+            kv.at[b, m], kv_land.at[b, m], d_send.at[b, m], d_recv.at[b, m], left
+        )
+
+    def kv_fire(m):
+        for b in range(n - 1):
+            pl.when(l == n - 1)(lambda b=b: kv_copy(b, m).start())
+
+    def kv_step(m):
+        for b in range(n - 2):
+
+            @pl.when((l > b) & (l <= n - 2))
+            def _(b=b):
+                kv_copy(b, m).wait_recv()
+                kv[b, m] = (kv[b, m].astype(F32) + kv_land[b, m].astype(F32)).astype(BF)
+                kv_copy(b, m).start()
+
+    def normal_back(u, d_rot, gain, cosine, sine):
+        d = d_rot * cosine - pltpu.roll(d_rot, 64, 1) * sine
+        r = lax.rsqrt(jnp.mean(u * u, axis=-1, keepdims=True) + EPS)
+        normal = u * r
+        e = d * gain
+        grad = r * (e - normal * jnp.mean(e * normal, axis=-1, keepdims=True))
+        return grad.astype(BF), jnp.sum(d * normal, axis=0, keepdims=True)
+
+    gains = small[8:10, :128].astype(F32)
+
+    def query_back(m):
+        for h in range(2):
+            cols = slice(h * 128, (h + 1) * 128)
+            grad, total = normal_back(
+                qp[m][:, cols],
+                att[m, h * 256 : (h + 1) * 256] * scale,
+                gains[0:1],
+                cos_ref[m],
+                sin_ref[m],
+            )
+            d_low[0, pl.ds(pl.multiple_of(m * 256, 256), 256), cols] = grad
+            head_sum[0:1, :128] += total
+
+    for m in range(4):
+        attend_back(m)
+        kv_fire(m)
+        if m == 1:
+            each(4, lambda m: to_chips(m, 2))
+    line.rs_near(11)
+    line.rs_far(10)
+    for item in (3, 4, 5):
+        way, item, kind, j = backward(item)
+        back_wait(way, item, kind, j)
+        line.rs_end(item)
+    each(4, query_back)
+    normed_back_copy.wait()
+
+    def output_weights(s, unused):
+        z = inner[:, :, :, :, :, pl.ds(pl.multiple_of(s * 256, 256), 256)].reshape(1024, 256)
+        g[5, s] = dot(prod_t[...], z).astype(BF)
+        return 0
+
+    def query_weights(s, unused):
+        g[3, s] = dot(normed_t[s], d_low[0]).astype(BF)
+        sums[1, s] = dot_t(dl_t[...], normed_t[s])[:8]
+        return 0
+
+    lax.fori_loop(0, blocks, output_weights, 0)
+    line.rs_fire(2)
+    lax.fori_loop(0, blocks, query_weights, 0)
+    line.rs_fire(0)
+    for m in range(4):
+        kv_step(m)
+
+    def key_back(m):
+        pl.when(l <= n - 2)(lambda: kv_copy(l, m).wait_recv())
+        pair = kv[l, m].astype(F32)
+        pair = pair + jnp.where(l <= n - 2, kv_land[l, m].astype(F32), 0.0)
+        grad, total = normal_back(kp[m], pair[:, :128], gains[1:2], cos_ref[m], sin_ref[m])
+        at = pl.ds(pl.multiple_of(m * 256, 256), 256)
+        d_low[1, at, :128] = grad
+        d_low[1, at, 128:] = pair[:, 128:].astype(BF)
+        head_sum[0:1, 128:] += total
+
+    each(4, key_back)
+
+    def key_weights(s, unused):
+        g[4, s] = dot(normed_t[s], d_low[1]).astype(BF)
+        return 0
+
+    lax.fori_loop(0, blocks, key_weights, 0)
+    line.rs_fire(1)
+
+    def normed_back(m):
+        at = pl.ds(pl.multiple_of(m * 256, 256), 256)
+        a, b, e = d_low[0, at], d_low[1, at], dl[m][:, :16]
+        for s in range(blocks):
+            part = dot_t(a, g[0, s]) + dot_t(b, g[1, s]) + dot(e, small_g[0, s])
+            normed[m, :, :, :, :, s * 256 : (s + 1) * 256] = part.astype(BF).reshape(
+                2, 2, 2, 32, 256
+            )
+        mate_copy(m, 3).start()
+
+    def home(i, own, out):
+        mine = out.at[:, k]
+        there = out.at[:, (1 - y) * 2 + c]
+        keep = pltpu.make_async_copy(own, mine, o_loc.at[14 + i])
+        over = remote(own, mine, h_send.at[i, 0], h_recv.at[i, 0], group.chip(2))
+        beside = remote(own, mine, h_send.at[i, 1], h_recv.at[i, 1], mate)
+        on = remote(there, there, h_send.at[i, 2], h_recv.at[i, 2], mate)
+        return keep, over, beside, on
+
+    each(4, normed_back)
+    line.rs_far(11)
+    for s in range(blocks):
+        sums[0, s, 0:1] = gain_sum[1:2, s * 256 : (s + 1) * 256]
+        sums[0, s, 1:2] = head_sum[0:1]
+        sums[0, s, 2:8] = jnp.zeros((6, 256), F32)
+    small_c = remote(sums.at[0], sum_c, u_send.at[0], u_recv.at[0], mate)
+    small_x = remote(sums, sum_x, u_send.at[1], u_recv.at[1], group.chip(1))
+    small_y = remote(sums.at[0], sum_y, u_send.at[2], u_recv.at[2], group.chip(2))
+    small_c.start()
+
+    def finish_out(m):
+        own_z[m] = (hidden[m] + total_of(m, 2)).astype(BF)
+
+    each(4, finish_out)
+    each(4, lambda m: sum_end(m, 2))
+    each(4, lambda m: to_chips(m, 3))
+    small_c.wait()
+    sums[0] = sums[0] + sum_c[...]
+    small_x.start()
+    res_home = home(0, own_z, res_out)
+    for copy in res_home[:3]:
+        copy.start()
+    line.rs_near(2)
+    line.rs_near(0)
+    homeward(9)
+    line.rs_far(2)
+    small_x.wait()
+    sums[...] = sums[...] + sum_x[...]
+    small_y.start()
+    homeward(10)
+    homeward(11)
+    line.rs_near(1)
+    line.rs_far(0)
+    small_y.wait()
+    sums[0] = sums[0] + sum_y[...]
+
+    def small_line(d):
+        to = lax.rem(l + d, n)
+        return remote(
+            sums.at[:, pl.ds(2 * to, 2)],
+            sum_l.at[l],
+            u_send.at[2 + d],
+            u_recv.at[2 + d],
+            device(to, x, y, c),
+        )
+
+    for d in range(1, n):
+        small_line(d).start()
+    sum_l[l] = sums[:, pl.ds(2 * l, 2)]
+
+    def finish_grad(m):
+        total = total_of(m, 3)
+        v = own_x[m].astype(F32)
+        r = lax.rsqrt(jnp.mean(v * v, axis=-1, keepdims=True) + EPS)
+        normal = v * r
+        gain_sum[0:1] += jnp.sum(total * normal, axis=0, keepdims=True)
+        e = total * gain_row[0:1, :]
+        own_x[m] = (
+            d_hid[m] + r * (e - normal * jnp.mean(e * normal, axis=-1, keepdims=True))
+        ).astype(BF)
+
+    each(4, finish_grad)
+    for s in range(blocks):
+        late[s : s + 1] = gain_sum[0:1, s * 256 : (s + 1) * 256]
+    late_c = remote(late, late_core, u_send.at[6], u_recv.at[6], mate)
+    late_c.start()
+    grad_home = home(1, own_x, grad_out)
+    grad_home[0].start()
+    grad_home[2].start()
+    res_home[1].wait_recv()
+    res_home[3].start()
+    line.rs_far(1)
+    late_c.wait()
+    late[...] = late[...] + late_core[...]
+    late_s = [
+        remote(
+            late, late_chip.at[x * 2 + y], u_send.at[6 + o], u_recv.at[6 + o], group.chip(o)
+        )
+        for o in (1, 2, 3)
+    ]
+    for copy in late_s:
+        copy.start()
+    grad_home[1].start()
+    late_chip[x * 2 + y] = late[...]
+    for copy in late_s:
+        copy.wait()
+    late[...] = late_chip[0] + late_chip[1] + late_chip[2] + late_chip[3]
+
+    def late_line(d):
+        to = lax.rem(l + d, n)
+        return remote(
+            late, late_l.at[l], u_send.at[9 + d], u_recv.at[9 + d], device(to, x, y, c)
+        )
+
+    for d in range(1, n):
+        late_line(d).start()
+    late_l[l] = late[...]
+    homeward(2)
+    homeward(0)
+    for d in range(1, n):
+        small_line(d).wait()
+    total = sum_l[0, :, x]
+    for i in range(1, n):
+        total = total + sum_l[i, :, x]
+    sums_out[...] = total
+    grad_home[1].wait_recv()
+    grad_home[3].start()
+    for d in range(1, n):
+        late_line(d).wait()
+    total = late_l[0]
+    for i in range(1, n):
+        total = total + late_l[i]
+    late_out[...] = total
+    homeward(1)
+    for item in (6, 7, 8, 9, 10, 11, 2, 0, 1):
+        way, item, kind, j = backward(item)
+        back_wait(way, item, kind, j)
+        line.rs_end(item)
+    for copies in (res_home, grad_home):
+        keep, over, beside, on = copies
+        keep.wait()
+        over.wait_send()
+        beside.wait()
+        on.wait()
+    z_out.wait_send()
+    z_on.wait_send()
+    tiny.ag_end(0)
+    each(3, line.ag_end)
+
+    def drain(m):
+        sum_end(m, 3)
+        spread_end(m, 1)
+        for b in range(n - 1):
+            pl.when(l > b)(lambda b=b: kv_copy(b, m).wait_send())
+
+    each(4, drain)
+
+
+def layer(n, x_in, z_in, wq, wkv, wo, wg, wu, wd, small, cosine, sine, row_range):
+    d = x_in.shape[-1]
+    m = 2 * n
+    bf = lambda *shape: jax.ShapeDtypeStruct(shape, BF)
+    vb = lambda *shape: pltpu.VMEM(shape, BF)
+    vf = lambda *shape: pltpu.VMEM(shape, F32)
+    return pl.pallas_call(
+        functools.partial(layer_kernel, n),
+        out_shape=(
+            bf(4, 4, 32, d),
+            bf(4, 4, 32, d),
+            bf(256, 512),
+            bf(256, 512),
+            bf(512, 256),
+            bf(256, 1536),
+            bf(256, 1536),
+            bf(1536, 256),
+            jax.ShapeDtypeStruct((2, 8, 256), F32),
+            jax.ShapeDtypeStruct((m, 256), F32),
+            bf(m, 256, 1024),
+            bf(4, 4, 32, d),
+        ),
+        in_specs=[ANY] * 8 + [VM] * 4,
+        out_specs=(ANY,) * 8 + (VM,) * 2 + (ANY,) * 2,
+        scratch_shapes=[
+            vb(4, 2, 4, 32, d),
+            vb(4, 2, 2, 2, 32, d),
+            vb(m, 256, 1024),
+            vb(12, m, 256, 256),
+            vb(1, m, 16, 256),
+            vf(2, d),
+            vb(16, d),
+            vb(n, 4, 256, 256),
+            vb(4, 512, 128),
+            vf(4, 256, 256),
+            vf(4, 256, 128),
+            vf(4, 256, 16),
+            vf(4, 512, 128),
+            vf(4, 512, 128),
+            vb(4, 2, 2, 2, 32, d),
+            vb(4, 2, 2, 32, d),
+            vb(4, 2, 2, 32, d),
+            vb(3, 4, 32, d),
+            vb(4, 2, 2, 2, 32, d),
+            vf(4, 32, d),
+            vb(6, m + 2, 256, 256),
+            vb(2, 1024, 256),
+            vb(256, 1024),
+            vb(n, 4, 256, 256),
+            vf(4, 32, d),
+            vb(4, 32, d),
+            vb(4, 32, d),
+            vb(4, 256, 128),
+            vb(16, 1024),
+            vf(2, d),
+            vf(1, 256),
+            vf(2, m, 8, 256),
+            vf(m, 8, 256),
+            vf(2, m, 8, 256),
+            vf(m, 8, 256),
+            vf(n, 2, 2, 8, 256),
+            vf(m, 256),
+            vf(m, 256),
+            vf(4, m, 256),
+            vf(n, m, 256),
+            DMA((12,)),
+            DMA((12,)),
+            DMA((12,)),
+            DMA((12, 2, n)),
+            DMA((12, n)),
+            DMA((3,)),
+            DMA((1, 2, n)),
+            DMA((1, n)),
+            DMA((3,)),
+            DMA((2,)),
+            DMA((4,)),
+            DMA((2,)),
+            DMA((n, 4)),
+            DMA((n, 4)),
+            DMA((4, 4)),
+            DMA((4, 4)),
+            DMA((4, 4, 3)),
+            DMA((4, 4, 3)),
+            DMA((2, 4, 3)),
+            DMA((2, 4, 3)),
+            DMA((2, 4, 4)),
+            DMA((2, 4, 4)),
+            DMA((12, 2, n)),
+            DMA((12, n + 1)),
+            DMA((12,)),
+            DMA((12,)),
+            DMA((12,)),
+            DMA((n, 4)),
+            DMA((n, 4)),
+            DMA((2, 3)),
+            DMA((2, 3)),
+            DMA((9 + n,)),
+            DMA((9 + n,)),
+            DMA((16,)),
+        ],
+        compiler_params=pltpu.CompilerParams(
+            collective_id=0, has_side_effects=True, vmem_limit_bytes=63 * 2**20
+        ),
+        name="layer",
+    )(x_in, z_in, wq, wkv, wo, wg, wu, wd, small, cosine, sine, row_range)
+
+class Group:
+    def __init__(self):
+        self.l, self.x, self.y, self.c = place()
+        self.mate = device(self.l, self.x, self.y, 1 - self.c)
+
+    def other(self, i):
+        x = 1 - self.x if i & 1 else self.x
+        y = 1 - self.y if i & 2 else self.y
+        return x, y
+
+    def chip(self, i):
+        x, y = self.other(i)
+        return device(self.l, x, y, self.c)
+
+    def partners(self):
+        return [(self.mate, None)] + [(self.chip(i), None) for i in (1, 2, 3)]
+
+
+def row_layout(index, buckets, lengths):
+    ends = jnp.cumsum(buckets)
+    starts = ends - buckets
+    member = (index[:, None] >= starts[None, :]) & (index[:, None] < ends[None, :])
+    position = index - jnp.sum(jnp.where(member, starts[None, :], 0), axis=1)
+    limit = jnp.sum(jnp.where(member, lengths[None, :], 0), axis=1)
+    return (None, position, limit)
+
+
+def fast_local(
+    inputs,
+    cotangent,
+    bucket_sizes,
+    true_lengths,
+    attention_gain,
+    feedforward_gain,
+    query_gain,
+    key_gain,
+    query_weight,
+    key_matrix,
+    value_matrix,
+    headgate_weight,
+    output_weight,
+    gate_weight,
+    up_weight,
+    down_weight,
+):
+    batches, rows, width = inputs.shape
+    n = lax.axis_size("seq") // 2
+    seq, kv = lax.axis_index("seq"), lax.axis_index("kv")
+    l, x = seq // 2, seq % 2
+    scale = HEAD_SIZE ** (-0.5)
+    span = 2 * rows
+    gain_query = query_gain.astype(F32)
+    gain_key = key_gain.astype(F32)
+
+    own_small = jnp.concatenate(
+        [
+            headgate_weight.T,
+            attention_gain[None],
+            feedforward_gain[None],
+            jnp.zeros((2, 256), BF),
+            jnp.pad(jnp.stack([query_gain, key_gain]), ((0, 0), (0, 128))),
+            jnp.zeros((6, 256), BF),
+        ],
+        axis=0,
+    )
+    paired = jnp.concatenate(
+        [key_matrix[:, :128], value_matrix[:, :128], key_matrix[:, 128:], value_matrix[:, 128:]],
+        axis=1,
+    )
+
+    row_index = l * span + jnp.arange(span, dtype=jnp.int32)
+    layouts = [row_layout(row_index, bucket_sizes[b], true_lengths[b]) for b in range(batches)]
+    positions = jnp.concatenate([item[1] for item in layouts])
+    row_lo = jnp.stack([row_index - item[1] for item in layouts])
+    limits = jnp.stack([item[2] for item in layouts])
+    row_hi = jnp.minimum(row_index + 1, row_lo + limits)
+    cosine, sine = rope_tables(positions, HEAD_SIZE)
+    signed = sine * jnp.where(jnp.arange(HEAD_SIZE) < HEAD_SIZE // 2, -1.0, 1.0)
+    x_split = inputs.reshape(batches, 4, 32, width)
+    z_split = cotangent.reshape(batches, 4, 32, width)
+    cosine = cosine.reshape(batches, span, HEAD_SIZE)
+    signed = signed.reshape(batches, span, HEAD_SIZE)
+    row_range = jnp.where(jnp.arange(128) == 0, row_lo[:, :, None], row_hi[:, :, None])
+    own_out, own_grad, dq, dkv, do, d_gate, d_up, d_down, sums, late, unused, unused = layer(
+        n,
+        x_split,
+        z_split,
+        query_weight,
+        paired,
+        output_weight,
+        gate_weight,
+        up_weight,
+        down_weight,
+        own_small,
+        cosine,
+        signed,
+        row_range,
+    )
+    return (
+        own_out.reshape(batches, rows, width),
+        own_grad.reshape(batches, rows, width),
+        lax.dynamic_index_in_dim(late, seq, 0, keepdims=False),
+        sums[0, 0],
+        sums[0, 1, :HEAD_SIZE],
+        sums[0, 1, HEAD_SIZE:],
+        dq.astype(F32),
+        jnp.concatenate([dkv[:, :128], dkv[:, 256:384]], axis=1).astype(F32),
+        jnp.concatenate([dkv[:, 128:256], dkv[:, 384:]], axis=1).astype(F32),
+        sums[1, :4].T,
+        do.astype(F32),
+        d_gate.astype(F32),
+        d_up.astype(F32),
+        d_down.astype(F32),
+    )
+
+
 def solution(mesh):
+    chosen = fast_local if dict(mesh.shape) == {"seq": 8, "kv": 4} else local
     in_specs = (
         P(None, "seq", None),
         P(None, "seq", None),
@@ -485,4 +1867,4 @@
         P("seq", "kv"),
         P("kv", "seq"),
     )
-    return jax.shard_map(local, mesh=mesh, in_specs=in_specs, out_specs=out_specs, check_vma=False)
+    return jax.shard_map(chosen, mesh=mesh, in_specs=in_specs, out_specs=out_specs, check_vma=False)

time: 2100 us -> 487 us (0.23)
  waiting for transfers between devices: 1030 us -> 0 us
  Pallas kernels: 0 us -> 445 us
  blocking collectives: 389 us -> 0 us
  matrix products: 323 us -> 0 us
  other arithmetic: 184 us -> 17.7 us
  local copies, waits for them, and re-layouts: 138 us -> 14.8 us
    reduce_scatter x11 -> x0, waiting for transfers between devices: 714 us -> none  [the longest x4 242 us: local(): lax.psum_scatter(grad_values.astype(jnp.bfloat16), 'seq', scatter_dimensi...]
    pallas_call x0 -> x1, Pallas kernels: none -> 445 us  [layer(): pl.pallas_call(functools.partial(layer_kernel, n), out_shape=(bf(4, 4, 32...]
    all_gather x11 -> x0, blocking collectives: 326 us -> none  [the longest x4 136 us: local(): lax.all_gather(value_low, 'seq', axis=0, tiled=True)]
    dot_general x152 -> x0, matrix products: 323 us -> none  [the longest x32 128 us: outer_sum(): lax.dot_general(left, right, (((0,), (0,)), ((), ())), preferred_element_...]
    psum x4 -> x0, waiting for transfers between devices: 184 us -> none  [the longest x1 88.2 us: local(): lax.psum(jnp.dot(product, w_down, preferred_element_type=jnp.float32).ast...]
    unnamed x32 -> x0, waiting for transfers between devices: 112 us -> none
    reduce_sum x54 -> x1, other arithmetic: 55.7 us -> 0.11 us  [row_layout(): limit = jnp.sum(jnp.where(member, lengths[None, :], 0), axis=1)]
    psum x1 -> x0, blocking collectives: 40.3 us -> none  [local(): lax.psum((sum_query_gain, sum_key_gain), ('seq', 'kv'))]
  transfers between devices with their start and end apart: 27 -> 0, of which waited for: 18 -> 0; matrix products, arithmetic and copies ran while one was open for 25% -> 0% of each run, Pallas kernels for 0% -> 0%
where the time goes in v5:
time: 487 us; the launch traced here: 479 us
  Pallas kernels  445 us (91%)
  other arithmetic  17.7 us (4%)
  local copies, waits for them, and re-layouts  14.8 us (3%)
    pallas_call x1, Pallas kernels, layer(): pl.pallas_call(functools.partial(layer_kernel, n), out_shape=(bf(4, 4, 32...  445 us

profile of v5, /device:TPU:0, one launch (start us, length us, event | category | flops | bytes accessed | tf_op | source)
XLA Modules:
  0.0 478.8 jit_solution(10657044132658105392)
XLA Ops:
  2.7 0.8 slice_bitcast_fusion.9
  4.3 1.9 concatenate.38.small
  6.2 0.8 fusion.16
  7.3 1.0 fusion.19
  8.3 0.7 pad_maximum_fusion.1.wkv
  9.0 1.1 broadcast_select_fusion.row_range
  10.1 3.4 multiply_sine_fusion
  13.5 1.0 maximum_multiply_fusion.sin_ref
  14.5 1.0 pad_maximum_fusion.cos_ref
  15.5 445.0 %layer.1 = (bf16[4,4,32,2048]{3,2,1,0:T(8,128)(2,1)}, bf16[4,4,32,2048]{3,2,1,0:T(8,128)(2,1)}, bf16[256,512]{1,0:T(8,128)(2,1)}, bf16[256,512]{1,0:T(8,128)(2,1...) custom-call(bf16[4,4,32,2048]{3,2,1,0:T(8,128)(2,1)} %bitcast.73, ...), custom_call_target="tpu_custom_call" | custom-call | tf_op jit(solution)/shard_map/layer/pallas_call | solution.py:1618
  460.6 1.4 constant_dynamic-slice_fusion
  461.9 1.3 slice.72
  463.2 1.2 slice_bitcast_fusion.1
  464.4 1.3 slice_bitcast_fusion
  465.7 1.0 fusion.18
  466.7 0.7 maximum_convert_fusion.1
  468.1 1.8 convert_element_type.44
  469.9 0.8 convert_element_type.47
  470.7 1.3 convert_element_type.48
  472.1 1.3 convert_element_type.49
  473.4 1.3 convert_element_type.50
  474.7 1.3 copy.32
  476.0 1.0 copy-done
  477.0 1.3 copy.33
  (39 shorter events, 3.7 us)
Async XLA Ops:
  460.6 9.3 %copy-start.5 = (bf16[512,256]{1,0:T(8,128)(2,1)S(1)}, bf16[512,256]{1,0:T(8,128)(2,1)}, u32[]{:S(2)}) copy-start(bf16[512,256]{1,0:T(8,128)(2,1)} %get-tuple-element.30) | copy-start | bytes 786436
  460.6 10.2 %copy-start.4 = (bf16[256,1536]{1,0:T(8,128)(2,1)S(1)}, bf16[256,1536]{1,0:T(8,128)(2,1)}, u32[]{:S(2)}) copy-start(bf16[256,1536]{1,0:T(8,128)(2,1)} %get-tuple-element.31) | copy-start | bytes 2359300
  467.4 4.7 copy-start.3
  470.7 2.7 copy-start.2
  472.1 2.6 copy-start.1
  474.7 2.3 copy-start

commit v6 on v5

--- a/solution.py
+++ b/solution.py
@@ -532,15 +532,27 @@
         pl.when(l >= 1)(lambda: self._ag(item, 0, l).start())
         pl.when(l <= self.n - 2)(lambda: self._ag(item, 1, l).start())
 
+    def ag_half(self, item, x, src):
+        l, n = self.l, self.n
+
+        def half(way):
+            step = -1 if way == 0 else 1
+            return remote(
+                src,
+                self.g.at[item, 2 * l + x],
+                self.ag_send.at[item, way, l],
+                self.ag_recv.at[item, l],
+                device(l + step, self.x, self.y, self.c),
+            )
+
+        pl.when(l >= 1)(lambda: half(0).start())
+        pl.when(l <= n - 2)(lambda: half(1).start())
+
     def ag_left(self, item):
         pl.when(self.l >= 1)(lambda: self._ag(item, 0, self.l).start())
 
-    def ag_right(self, item):
-        l, n = self.l, self.n
-        pl.when((l >= 1) & (l <= n - 2))(lambda: self._ag(item, 1, l).start())
-
-    def ag_right_end(self, item):
-        pl.when(self.l == 0)(lambda: self._ag(item, 1, self.l).start())
+    def ag_right(self, item, plane):
+        pl.when(self.l == plane)(lambda: self._ag(item, 1, self.l).start())
 
     def ag_step(self, item, t):
         l, n = self.l, self.n
@@ -623,33 +635,25 @@
             pl.when(l == 0)(lambda o=o: self._rs(item, 1, o).start())
             pl.when(l == n - 1)(lambda o=o: self._rs(item, 0, n - 1 - o).start())
 
-    def rs_near(self, item):
+    def rs_near(self, item, plane):
         l, n = self.l, self.n
-
-        @pl.when(l == 1)
+        way = 1 if plane == 1 else 0
+        owners = range(n - 1, 1, -1) if plane == 1 else range(n - 2)
+
+        @pl.when(l == plane)
         def _():
-            for o in range(n - 1, 1, -1):
+            for o in owners:
                 self._take(item, o, o)
-                self._rs(item, 1, o).start()
-
-        @pl.when(l == n - 2)
+                self._rs(item, way, o).start()
+
+    def rs_far(self, item, plane):
+        l, n = self.l, self.n
+        way, o = (0, 0) if plane == 1 else (1, n - 1)
+
+        @pl.when(l == plane)
         def _():
-            for o in range(n - 2):
-                self._take(item, o, o)
-                self._rs(item, 0, o).start()
-
-    def rs_far(self, item):
-        l, n = self.l, self.n
-
-        @pl.when(l == 1)
-        def _():
-            self._take(item, 0, 0)
-            self._rs(item, 0, 0).start()
-
-        @pl.when(l == n - 2)
-        def _():
-            self._take(item, n - 1, n - 1)
-            self._rs(item, 1, n - 1).start()
+            self._take(item, o, o)
+            self._rs(item, way, o).start()
 
     def rs_final(self, item):
         l, n = self.l, self.n
@@ -681,60 +685,64 @@
         return (device(line.l, 1 - line.x, line.y, line.c), None)
 
     def _part(self, ref, kind, j, x):
-        half = self.half if isinstance(self.half, int) else self.half[kind]
-        at = pl.multiple_of(x * half + j * 256, 256)
+        at = pl.multiple_of(x * self.half + j * 256, 256)
         return ref.at[pl.ds(at, 256), :] if kind == 2 else ref.at[:, pl.ds(at, 256)]
+
+    def _pieces(self, block, item, kind, j, x):
+        ref = self.refs[kind]
+        if not isinstance(ref, tuple):
+            return [(self._part(ref, kind, j, x), block, item)]
+        at = pl.ds(pl.multiple_of(x * (self.half // 2 if item == 1 else self.half) + j * 128, 128), 128)
+        return [
+            (one.at[:, at], block.at[:, pl.ds(128 * i, 128)], item + 12 * i)
+            for i, one in enumerate(ref)
+        ]
 
     def _copies(self, item, kind, j):
         line = self.line
         mine = line.g.at[item, 2 * line.l + line.x]
-        out = remote(
-            self._part(self.refs[kind], kind, j, 1 - line.x),
-            mine,
-            self.send.at[item],
-            self.recv.at[item],
-            self.partner()[0],
-        )
-        here = pltpu.make_async_copy(
-            self._part(self.refs[kind], kind, j, line.x), mine, self.local.at[item]
-        )
-        return out, here
+        away = self._pieces(mine, item, kind, j, 1 - line.x)
+        stay = self._pieces(mine, item, kind, j, line.x)
+        pairs = []
+        for (src, block, sem), (own, unused, unused2) in zip(away, stay):
+            out = remote(src, block, self.send.at[sem], self.recv.at[sem], self.partner()[0])
+            here = pltpu.make_async_copy(own, block, self.local.at[sem])
+            pairs.append((out, here))
+        return pairs
 
     def start(self, item, kind, j):
-        for copy in self._copies(item, kind, j):
-            copy.start()
+        for out, here in self._copies(item, kind, j):
+            out.start()
+            here.start()
 
     def end(self, item, kind, j):
-        out, here = self._copies(item, kind, j)
-        here.wait()
-        out.wait_send()
-        out.wait_recv()
+        for out, here in self._copies(item, kind, j):
+            here.wait()
+            out.wait_send()
+            out.wait_recv()
 
 
 class Back(Pair):
     def _copies(self, item, kind, j):
         line = self.line
-        home = self._part(self.refs[kind], kind, j, line.x)
-        out = remote(
-            line.g.at[line.seat(item), 2 * line.l + 1 - line.x],
-            home,
-            self.send.at[item],
-            self.recv.at[item],
-            self.partner()[0],
-        )
-        here = pltpu.make_async_copy(
-            line.g.at[line.seat(item), 2 * line.l + line.x], home, self.local.at[item]
-        )
-        return out, here
-
-
-def back_wait(back, item, kind, j):
-    line = back.line
-    out, here = back._copies(item, kind, j)
-    here.wait()
-    out.wait_send()
-    there = back._part(back.refs[kind], kind, j, 1 - line.x)
-    pltpu.make_async_copy(there, there, back.recv.at[item]).wait()
+        seat = line.seat(item)
+        away = self._pieces(line.g.at[seat, 2 * line.l + 1 - line.x], item, kind, j, line.x)
+        stay = self._pieces(line.g.at[seat, 2 * line.l + line.x], item, kind, j, line.x)
+        pairs = []
+        for (home, block, sem), (unused, own, unused2) in zip(away, stay):
+            out = remote(block, home, self.send.at[sem], self.recv.at[sem], self.partner()[0])
+            here = pltpu.make_async_copy(own, home, self.local.at[sem])
+            pairs.append((out, here))
+        return pairs
+
+    def end(self, item, kind, j):
+        line = self.line
+        block = line.g.at[line.seat(item), 2 * line.l]
+        there = self._pieces(block, item, kind, j, 1 - line.x)
+        for (out, here), (home, unused, sem) in zip(self._copies(item, kind, j), there):
+            here.wait()
+            out.wait_send()
+            pltpu.make_async_copy(home, home, self.recv.at[sem]).wait()
 
 
 def dot(a, b):
@@ -750,19 +758,20 @@
     x_any,
     z_any,
     wq,
-    wkv,
+    wk,
+    wv,
     wo,
     wg,
     wu,
     wd,
     small,
-    cos_ref,
-    sin_ref,
-    row_range,
+    sizes,
+    lengths,
     res_out,
     grad_out,
     dq_out,
-    dkv_out,
+    dk_out,
+    dv_out,
     do_out,
     dgw,
     duw,
@@ -811,6 +820,11 @@
     late_core,
     late_chip,
     late_l,
+    cos_ref,
+    sin_ref,
+    row_range,
+    free,
+    done,
     p_send,
     p_recv,
     p_loc,
@@ -842,6 +856,7 @@
     d_recv,
     h_send,
     h_recv,
+    h_loc,
     u_send,
     u_recv,
     o_loc,
@@ -855,17 +870,21 @@
     tiny = Line(n, small_g, sa_send, sa_recv)
     scale = HEAD_SIZE ** (-0.5)
     width = 256 * 2 * n
-    back = Back(line, (dgw, duw, ddw), b_send, b_recv, b_loc, 768)
-    back_first = Back(line, (dq_out, dkv_out, do_out), b_send, b_recv, b_loc, 256)
+    back = Back(line, ((dgw, duw), (dgw, duw), ddw), b_send, b_recv, b_loc, 768)
+    back_first = Back(line, (dq_out, (dk_out, dv_out), do_out), b_send, b_recv, b_loc, 256)
     left = device(l - 1, x, y, c)
     blocks = 2 * n
-    first = Pair(line, (wq, wkv, wo), p_send, p_recv, p_loc, 256)
-    rest = Pair(line, (wg, wu, wd), p_send, p_recv, p_loc, 768)
+    first = Pair(line, (wq, (wk, wv), wo), p_send, p_recv, p_loc, 256)
+    rest = Pair(line, ((wg, wu), (wg, wu), wd), p_send, p_recv, p_loc, 768)
+
+    def half_of(item):
+        chunk = item // 3 - 1
+        return chunk if item % 3 == 2 else 2 * chunk + item % 3
 
     def swap(item):
         if item < 3:
             return first, item, item, 0
-        return rest, item, item % 3, item // 3 - 1
+        return rest, item, item % 3, half_of(item)
 
     def swap_start(item):
         pair, item, kind, j = swap(item)
@@ -891,6 +910,7 @@
     small_out_copy = remote(small, small_here, sp_sem.at[0], sp_sem.at[1], across)
     small_own = pltpu.make_async_copy(small, small_here, sp_sem.at[2])
     swap_start(0)
+    line.ag_half(0, x, first._part(wq, 0, 0, x))
     small_out_copy.start()
     small_own.start()
     swap_start(1)
@@ -902,7 +922,8 @@
     x_part = x_v.at[halves, 1 - x]
     x_on = remote(x_part, x_part, t_send.at[1], t_recv.at[1], mate)
     x_out.start()
-    for item in range(3, 12):
+    ffn_items = (5, 3, 4, 8, 6, 7, 11, 9, 10)
+    for item in ffn_items:
         swap_start(item)
     z_out = remote(z_any.at[halves], dz_out.at[halves], z_send.at[0], z_recv.at[0], across)
     z_part = dz_out.at[halves]
@@ -910,7 +931,7 @@
     z_out.start()
 
     swap_end(0)
-    line.ag_start(0)
+    line.ag_half(0, 1 - x, g.at[0, 2 * l + 1 - x])
     small_own.wait()
     small_out_copy.wait()
     tiny.ag_start(0)
@@ -932,15 +953,32 @@
         v = v * lax.rsqrt(mean + EPS) * gain_row[0:1, :]
         normed[m, side] = v.astype(BF).reshape(2, 2, 32, 256 * 2 * n)
 
+    def tables(m):
+        i = l * 256 + lax.broadcasted_iota(jnp.int32, (256, 128), 0)
+        lane = lax.broadcasted_iota(jnp.int32, (256, 128), 1)
+        end = sizes[m, 0]
+        start = jnp.zeros_like(i)
+        valid = jnp.full_like(i, lengths[m, 0])
+        for bucket in range(1, sizes.shape[1]):
+            start = jnp.where(i >= end, end, start)
+            valid = jnp.where(i >= end, lengths[m, bucket], valid)
+            end = end + sizes[m, bucket]
+        row_range[m] = jnp.where(lane == 0, start, jnp.minimum(i + 1, start + valid))
+        steps = (lane & 63).astype(F32) * (2.0 / HEAD_SIZE)
+        angle = (i - start).astype(F32) * jnp.exp(-steps * math.log(ROPE_BASE))
+        cos_ref[m] = jnp.cos(angle)
+        sin_ref[m] = jnp.sin(angle) * jnp.where(lane < 64, -1.0, 1.0)
+
     x_here.wait()
     each(4, lambda m: norm(m, x))
     line.pump(0, 2)
     line.pump(1, 2)
     line.ag_start(2)
+    each(4, tables)
     x_out.wait_recv()
     x_on.start()
     line.pump(2, 1)
-    for item in (3, 4):
+    for item in ffn_items[:2]:
         swap_end(item)
         line.ag_left(item)
     x_on.wait_recv()
@@ -1086,16 +1124,17 @@
         branch(m)
         if m > 0:
             to_chips(m - 1)
-        for item in (3 + 2 * m + 2, 3 + 2 * m + 3):
-            if item < 12:
-                swap_end(item)
-                line.ag_left(item)
+        for item in ffn_items[2 + 2 * m : 4 + 2 * m]:
+            swap_end(item)
+            line.ag_left(item)
     to_chips(3)
-    for item in range(3, 12):
-        line.ag_right_end(item)
-    for item in (3, 4, 5):
-        line.ag_right(item)
-    for item in (3, 4, 5):
+    for item in ffn_items:
+        line.ag_right(item, 0)
+    for item in (5, 3, 4):
+        line.ag_right(item, 1)
+    for item in (5, 3):
+        line.ag_right(item, 2)
+    for item in (5, 3):
         line.pump(item, 1)
 
     def inner_copy(m, o, r=0):
@@ -1119,10 +1158,10 @@
         inner_mate(m, 0).start()
 
     each(4, finish)
-    for item in (3, 4, 5):
+    for item in (5, 3):
         line.pump(item, 2)
-    for item in (6, 7, 8):
-        line.ag_right(item)
+    line.ag_right(4, 2)
+    line.pump(4, 1)
     z_out.wait_recv()
     z_on.start()
 
@@ -1132,7 +1171,12 @@
             inner_mate(m, o, r).start()
 
     each(4, pass_on)
-    for item in (6, 7, 8):
+    line.pump(4, 2)
+    for item in (8, 6, 7):
+        line.ag_right(item, 1)
+    for item in (8, 6):
+        line.ag_right(item, 2)
+    for item in (8, 6):
         line.pump(item, 1)
     x_out.wait_send()
     x_on.wait_send()
@@ -1172,31 +1216,32 @@
     dz_own.wait()
     dz_other.wait()
 
-    def compute(j):
-        base = 3 * j + 3
+    def compute(j, h):
+        pair_of, down_of = 3 * j + 3 + h, 3 * j + 5
+        here = slice(128 * h, 128 * h + 128)
 
         def rows(m, unused):
             a = inner[m].reshape(256, width)
             d = x_v[m].reshape(256, width)
-            gated = dot(a, g[base].reshape(width, 256))
-            upward = dot(a, g[base + 1].reshape(width, 256))
-            grad = dot_t(d[:, :256], g[base + 2, 0])
+            both = dot(a, g[pair_of].reshape(width, 256))
+            gated, upward = both[:, :128], both[:, 128:]
+            grad = dot_t(d[:, :256], g[down_of, 0, here])
             for s in range(1, 2 * n):
-                grad = grad + dot_t(d[:, s * 256 : (s + 1) * 256], g[base + 2, s])
+                grad = grad + dot_t(d[:, s * 256 : (s + 1) * 256], g[down_of, s, here])
             sigma = jax.nn.sigmoid(gated)
             swish = gated * sigma
             product = (swish * upward).astype(BF)
-            d_gated = (grad * upward * sigma * (1.0 + gated * (1.0 - sigma))).astype(BF)
-            d_upward = (grad * swish).astype(BF)
+            d_both = jnp.concatenate(
+                [grad * upward * sigma * (1.0 + gated * (1.0 - sigma)), grad * swish], axis=1
+            ).astype(BF)
             at = pl.ds(pl.multiple_of(m * 256, 256), 256)
-            d_low[0, at] = d_gated
-            d_low[1, at] = d_upward
-            prod_t[:, at] = product.T
+            d_low[0, at] = d_both
+            prod_t[:128, at] = product.T
             for s in range(2 * n):
                 cols = slice(s * 256, (s + 1) * 256)
-                o = dot(product, g[base + 2, s])
-                i = dot_t(d_gated, g[base, s]) + dot_t(d_upward, g[base + 1, s])
-                if j > 0:
+                o = dot(product, g[down_of, s, here])
+                i = dot_t(d_both, g[pair_of, s])
+                if j + h > 0:
                     o = o + part[m, :, :, :, :, cols].reshape(256, 256).astype(F32)
                     i = i + normed[m, :, :, :, :, cols].reshape(256, 256).astype(F32)
                 part[m, :, :, :, :, cols] = o.astype(BF).reshape(2, 2, 2, 32, 256)
@@ -1205,84 +1250,131 @@
 
         lax.fori_loop(0, 4, rows, 0)
 
-        def weights(s, unused):
-            t = normed_t[s]
-            g[base, s] = dot(t, d_low[0]).astype(BF)
-            g[base + 1, s] = dot(t, d_low[1]).astype(BF)
+        def weights(s):
+            g[pair_of, s] = dot(normed_t[s], d_low[0]).astype(BF)
             z = x_v[:, :, :, :, pl.ds(pl.multiple_of(s * 256, 256), 256)].reshape(1024, 256)
-            g[base + 2, s] = dot(prod_t[...], z).astype(BF)
-            return 0
-
-        lax.fori_loop(0, 2 * n, weights, 0)
+            g[down_of, s, here] = dot(prod_t[:128], z).astype(BF)
+
+        each(2 * n, weights)
 
     def backward(item):
         if item < 3:
             return back_first, item, item, 0
-        return back, item, item % 3, item // 3 - 1
-
-    def homeward(item):
-        line.rs_final(item)
+        return back, item, item % 3, half_of(item)
+
+    def near(*items):
+        for item in items:
+            line.rs_near(item, 1)
+            line.rs_near(item, n - 2)
+
+    def far(*items):
+        for item in items:
+            line.rs_far(item, 1)
+            line.rs_far(item, n - 2)
+
+    def send_home(item):
         way, item, kind, j = backward(item)
         way.start(item, kind, j)
 
     inside = (l >= 1) & (l <= n - 2)
 
-    def homeward_in(item):
-        pl.when(inside)(lambda: homeward(item))
-
-    def homeward_end(item):
-        pl.when(jnp.logical_not(inside))(lambda: homeward(item))
-
-    for item in (3, 4, 5):
-        line.collect(item)
-        line.ag_end(item)
-    compute(0)
-    for item in (3, 4, 5):
-        line.rs_fire(item)
-    for item in (6, 7, 8):
+    def final_in(item):
+        pl.when(inside)(lambda: line.rs_final(item))
+
+    def final_end(item):
+        pl.when(jnp.logical_not(inside))(lambda: line.rs_final(item))
+
+    def ready(*items):
+        for item in items:
+            line.collect(item)
+            line.ag_end(item)
+
+    def free_give(i):
+        def tell(target):
+            pl.semaphore_signal(
+                free.at[i], inc=1, device_id=target, device_id_type=pl.DeviceIdType.MESH
+            )
+
+        pl.when(l == 1)(lambda: tell(device(l - 1, x, y, c)))
+        pl.when(l == n - 2)(lambda: tell(device(l + 1, x, y, c)))
+
+    def done_give(i):
+        def tell(target):
+            pl.semaphore_signal(
+                done.at[i], inc=1, device_id=target, device_id_type=pl.DeviceIdType.MESH
+            )
+
+        pl.when(l == 0)(lambda: tell(device(l + 1, x, y, c)))
+        pl.when(l == n - 1)(lambda: tell(device(l - 1, x, y, c)))
+
+    def done_take(i):
+        pl.when(inside)(lambda: pl.semaphore_wait(done.at[i], 1))
+
+    def free_take(i):
+        pl.when(jnp.logical_not(inside))(lambda: pl.semaphore_wait(free.at[i], 1))
+
+    ready(5, 3)
+    compute(0, 0)
+    line.rs_fire(3)
+    for item in (8, 6):
         line.pump(item, 2)
-    for item in (9, 10, 11):
-        line.ag_right(item)
-    for item in (9, 10, 11):
+    line.ag_right(7, 2)
+    line.pump(7, 1)
+    ready(4)
+    compute(0, 1)
+    line.rs_fire(4)
+    line.rs_fire(5)
+    line.pump(7, 2)
+    for item in (11, 9, 10):
+        line.ag_right(item, 1)
+    for item in (11, 9):
+        line.ag_right(item, 2)
+    for item in (11, 9):
         line.pump(item, 1)
-    line.rs_near(3)
-    line.rs_near(4)
-    for item in (6, 7, 8):
-        line.collect(item)
-        line.ag_end(item)
-    compute(1)
-    for item in (6, 7, 8):
-        line.rs_fire(item)
-    for item in (9, 10, 11):
+    near(3)
+    ready(8, 6)
+    compute(1, 0)
+    line.rs_fire(6)
+    for item in (11, 9):
         line.pump(item, 2)
-    line.rs_near(5)
-    homeward_in(3)
-    line.rs_far(3)
-    homeward_in(4)
-    line.rs_far(4)
-    line.rs_near(6)
-    homeward_in(5)
-    line.rs_far(5)
-    line.rs_near(7)
-    for item in (9, 10, 11):
-        line.collect(item)
-        line.ag_end(item)
-    compute(2)
+    line.ag_right(10, 2)
+    line.pump(10, 1)
+    near(4)
+    final_in(3)
+    free_give(0)
+    ready(7)
+    compute(1, 1)
+    line.rs_fire(7)
+    line.rs_fire(8)
+    line.pump(10, 2)
+    near(5)
+    far(3)
+    final_in(4)
+    free_give(1)
+    near(6)
+    final_in(5)
+    free_give(2)
+    far(4)
+    ready(11, 9)
+    compute(2, 0)
+    free_take(0)
+    line.rs_fire(9)
+    ready(10)
+    compute(2, 1)
     each(4, lambda m: mate_copy(m, 1).start())
-    for item in (3, 4, 5):
-        homeward_end(item)
-    for item in (9, 10, 11):
-        line.rs_fire(item)
+    free_take(1)
+    line.rs_fire(10)
+    free_take(2)
+    line.rs_fire(11)
     gain_sum[...] = jnp.zeros_like(gain_sum)
     head_sum[...] = jnp.zeros_like(head_sum)
-    homeward_in(6)
-    line.rs_far(6)
     each(4, lambda m: to_chips(m, 1))
-    line.rs_near(8)
-    homeward_in(7)
-    line.rs_far(7)
-    homeward_in(8)
-    line.rs_far(8)
+    near(7)
+    far(5)
+    final_in(6)
+    far(6)
+    near(8)
+    line.rs_near(9, 1)
     z_copy.wait()
     x_copy.wait()
     normed_back_copy = put(normed_out, normed_t)
@@ -1305,13 +1397,14 @@
 
     each(4, finish_hidden)
     each(4, lambda m: sum_end(m, 1))
-    for item in (6, 7, 8):
-        homeward_end(item)
-    line.rs_near(9)
-    each(4, lambda m: pass_on(m, 1))
-    each(4, lambda m: mate_copy(m, 2).start())
-    line.rs_near(10)
-    line.rs_far(9)
+    for item in (3, 4, 5):
+        final_end(item)
+        send_home(item)
+    done_give(0)
+    line.rs_near(9, 2)
+    final_in(7)
+    far(7)
+    line.rs_near(10, 1)
 
     def attend_back(m):
         arrive(m, 1)
@@ -1401,16 +1494,29 @@
             d_low[0, pl.ds(pl.multiple_of(m * 256, 256), 256), cols] = grad
             head_sum[0:1, :128] += total
 
+    pass_on(0, 1)
     for m in range(4):
+        if m < 3:
+            pass_on(m + 1, 1)
+        if m == 2:
+            each(4, lambda m: mate_copy(m, 2).start())
         attend_back(m)
         kv_fire(m)
-        if m == 1:
-            each(4, lambda m: to_chips(m, 2))
-    line.rs_near(11)
-    line.rs_far(10)
+        if m == 0:
+            line.rs_near(10, 2)
+    each(4, lambda m: to_chips(m, 2))
+    final_in(8)
+    far(8)
+    line.rs_near(11, 1)
+    for item in (6, 7, 8):
+        final_end(item)
+        send_home(item)
+    done_give(1)
+    done_take(0)
+    far(9)
     for item in (3, 4, 5):
         way, item, kind, j = backward(item)
-        back_wait(way, item, kind, j)
+        way.end(item, kind, j)
         line.rs_end(item)
     each(4, query_back)
     normed_back_copy.wait()
@@ -1431,6 +1537,44 @@
     line.rs_fire(0)
     for m in range(4):
         kv_step(m)
+    line.rs_near(11, 2)
+    line.rs_near(2, 1)
+    line.rs_near(0, 1)
+    far(10)
+
+    def home(i, m, own, out):
+        mine = out.at[m, k]
+        there = out.at[m, (1 - y) * 2 + c]
+        keep = pltpu.make_async_copy(own.at[m], mine, h_loc.at[i, m])
+        over = remote(own.at[m], mine, h_send.at[i, m, 0], h_recv.at[i, m, 0], group.chip(2))
+        beside = remote(own.at[m], mine, h_send.at[i, m, 1], h_recv.at[i, m, 1], mate)
+        on = remote(there, there, h_send.at[i, m, 2], h_recv.at[i, m, 2], mate)
+        return keep, over, beside, on
+
+    homes = ((own_z, res_out), (own_x, grad_out))
+
+    def home_start(i, m):
+        for copy in home(i, m, *homes[i])[:3]:
+            copy.start()
+
+    def home_on(i, m):
+        keep, over, beside, on = home(i, m, *homes[i])
+        over.wait_recv()
+        on.start()
+
+    def home_end(i, m):
+        keep, over, beside, on = home(i, m, *homes[i])
+        keep.wait()
+        over.wait_send()
+        beside.wait()
+        on.wait()
+
+    def finish_out(m):
+        own_z[m] = (hidden[m] + total_of(m, 2)).astype(BF)
+        home_start(0, m)
+
+    each(4, finish_out)
+    each(4, lambda m: sum_end(m, 2))
 
     def key_back(m):
         pl.when(l <= n - 2)(lambda: kv_copy(l, m).wait_recv())
@@ -1461,17 +1605,8 @@
             )
         mate_copy(m, 3).start()
 
-    def home(i, own, out):
-        mine = out.at[:, k]
-        there = out.at[:, (1 - y) * 2 + c]
-        keep = pltpu.make_async_copy(own, mine, o_loc.at[14 + i])
-        over = remote(own, mine, h_send.at[i, 0], h_recv.at[i, 0], group.chip(2))
-        beside = remote(own, mine, h_send.at[i, 1], h_recv.at[i, 1], mate)
-        on = remote(there, there, h_send.at[i, 2], h_recv.at[i, 2], mate)
-        return keep, over, beside, on
-
     each(4, normed_back)
-    line.rs_far(11)
+    far(11)
     for s in range(blocks):
         sums[0, s, 0:1] = gain_sum[1:2, s * 256 : (s + 1) * 256]
         sums[0, s, 1:2] = head_sum[0:1]
@@ -1480,32 +1615,16 @@
     small_x = remote(sums, sum_x, u_send.at[1], u_recv.at[1], group.chip(1))
     small_y = remote(sums.at[0], sum_y, u_send.at[2], u_recv.at[2], group.chip(2))
     small_c.start()
-
-    def finish_out(m):
-        own_z[m] = (hidden[m] + total_of(m, 2)).astype(BF)
-
-    each(4, finish_out)
-    each(4, lambda m: sum_end(m, 2))
     each(4, lambda m: to_chips(m, 3))
     small_c.wait()
     sums[0] = sums[0] + sum_c[...]
-    small_x.start()
-    res_home = home(0, own_z, res_out)
-    for copy in res_home[:3]:
-        copy.start()
-    line.rs_near(2)
-    line.rs_near(0)
-    homeward(9)
-    line.rs_far(2)
-    small_x.wait()
-    sums[...] = sums[...] + sum_x[...]
-    small_y.start()
-    homeward(10)
-    homeward(11)
-    line.rs_near(1)
-    line.rs_far(0)
-    small_y.wait()
-    sums[0] = sums[0] + sum_y[...]
+    done_take(1)
+    line.rs_far(2, 2)
+    line.rs_near(2, 2)
+    for item in (9, 10, 11):
+        line.rs_final(item)
+    line.rs_far(0, 2)
+    line.rs_near(1, 1)
 
     def small_line(d):
         to = lax.rem(l + d, n)
@@ -1516,10 +1635,6 @@
             u_recv.at[2 + d],
             device(to, x, y, c),
         )
-
-    for d in range(1, n):
-        small_line(d).start()
-    sum_l[l] = sums[:, pl.ds(2 * l, 2)]
 
     def finish_grad(m):
         total = total_of(m, 3)
@@ -1531,18 +1646,20 @@
         own_x[m] = (
             d_hid[m] + r * (e - normal * jnp.mean(e * normal, axis=-1, keepdims=True))
         ).astype(BF)
+        home_start(1, m)
 
     each(4, finish_grad)
     for s in range(blocks):
         late[s : s + 1] = gain_sum[0:1, s * 256 : (s + 1) * 256]
     late_c = remote(late, late_core, u_send.at[6], u_recv.at[6], mate)
     late_c.start()
-    grad_home = home(1, own_x, grad_out)
-    grad_home[0].start()
-    grad_home[2].start()
-    res_home[1].wait_recv()
-    res_home[3].start()
-    line.rs_far(1)
+    small_x.start()
+    each(4, lambda m: home_on(0, m))
+    for item in (9, 10, 11):
+        send_home(item)
+    line.rs_near(0, 2)
+    line.rs_far(1, 2)
+    line.rs_far(2, 1)
     late_c.wait()
     late[...] = late[...] + late_core[...]
     late_s = [
@@ -1553,8 +1670,11 @@
     ]
     for copy in late_s:
         copy.start()
-    grad_home[1].start()
     late_chip[x * 2 + y] = late[...]
+    small_x.wait()
+    sums[...] = sums[...] + sum_x[...]
+    small_y.start()
+    each(4, lambda m: home_on(1, m))
     for copy in late_s:
         copy.wait()
     late[...] = late_chip[0] + late_chip[1] + late_chip[2] + late_chip[3]
@@ -1568,33 +1688,36 @@
     for d in range(1, n):
         late_line(d).start()
     late_l[l] = late[...]
-    homeward(2)
-    homeward(0)
+    small_y.wait()
+    sums[0] = sums[0] + sum_y[...]
+    for d in range(1, n):
+        small_line(d).start()
+    sum_l[l] = sums[:, pl.ds(2 * l, 2)]
+    line.rs_near(1, 2)
+    line.rs_far(0, 1)
+    line.rs_final(2)
+    send_home(2)
+    line.rs_far(1, 1)
+    line.rs_final(0)
+    send_home(0)
     for d in range(1, n):
         small_line(d).wait()
     total = sum_l[0, :, x]
     for i in range(1, n):
         total = total + sum_l[i, :, x]
     sums_out[...] = total
-    grad_home[1].wait_recv()
-    grad_home[3].start()
     for d in range(1, n):
         late_line(d).wait()
     total = late_l[0]
     for i in range(1, n):
         total = total + late_l[i]
     late_out[...] = total
-    homeward(1)
+    line.rs_final(1)
+    send_home(1)
     for item in (6, 7, 8, 9, 10, 11, 2, 0, 1):
         way, item, kind, j = backward(item)
-        back_wait(way, item, kind, j)
+        way.end(item, kind, j)
         line.rs_end(item)
-    for copies in (res_home, grad_home):
-        keep, over, beside, on = copies
-        keep.wait()
-        over.wait_send()
-        beside.wait()
-        on.wait()
     z_out.wait_send()
     z_on.wait_send()
     tiny.ag_end(0)
@@ -1603,13 +1726,15 @@
     def drain(m):
         sum_end(m, 3)
         spread_end(m, 1)
+        home_end(0, m)
+        home_end(1, m)
         for b in range(n - 1):
             pl.when(l > b)(lambda b=b: kv_copy(b, m).wait_send())
 
     each(4, drain)
 
 
-def layer(n, x_in, z_in, wq, wkv, wo, wg, wu, wd, small, cosine, sine, row_range):
+def layer(n, x_in, z_in, wq, wk, wv, wo, wg, wu, wd, small, sizes, lengths):
     d = x_in.shape[-1]
     m = 2 * n
     bf = lambda *shape: jax.ShapeDtypeStruct(shape, BF)
@@ -1621,7 +1746,8 @@
             bf(4, 4, 32, d),
             bf(4, 4, 32, d),
             bf(256, 512),
-            bf(256, 512),
+            bf(256, 256),
+            bf(256, 256),
             bf(512, 256),
             bf(256, 1536),
             bf(256, 1536),
@@ -1631,8 +1757,8 @@
             bf(m, 256, 1024),
             bf(4, 4, 32, d),
         ),
-        in_specs=[ANY] * 8 + [VM] * 4,
-        out_specs=(ANY,) * 8 + (VM,) * 2 + (ANY,) * 2,
+        in_specs=[ANY] * 9 + [VM] + [pl.BlockSpec(memory_space=pltpu.SMEM)] * 2,
+        out_specs=(ANY,) * 9 + (VM,) * 2 + (ANY,) * 2,
         scratch_shapes=[
             vb(4, 2, 4, 32, d),
             vb(4, 2, 2, 2, 32, d),
@@ -1674,9 +1800,14 @@
             vf(m, 256),
             vf(4, m, 256),
             vf(n, m, 256),
-            DMA((12,)),
-            DMA((12,)),
-            DMA((12,)),
+            vf(4, 256, 128),
+            vf(4, 256, 128),
+            pltpu.VMEM((4, 256, 128), jnp.int32),
+            pltpu.SemaphoreType.REGULAR((3,)),
+            pltpu.SemaphoreType.REGULAR((2,)),
+            DMA((24,)),
+            DMA((24,)),
+            DMA((24,)),
             DMA((12, 2, n)),
             DMA((12, n)),
             DMA((3,)),
@@ -1698,13 +1829,14 @@
             DMA((2, 4, 4)),
             DMA((12, 2, n)),
             DMA((12, n + 1)),
-            DMA((12,)),
-            DMA((12,)),
-            DMA((12,)),
+            DMA((24,)),
+            DMA((24,)),
+            DMA((24,)),
             DMA((n, 4)),
             DMA((n, 4)),
-            DMA((2, 3)),
-            DMA((2, 3)),
+            DMA((2, 4, 3)),
+            DMA((2, 4, 3)),
+            DMA((2, 4)),
             DMA((9 + n,)),
             DMA((9 + n,)),
             DMA((16,)),
@@ -1713,7 +1845,7 @@
             collective_id=0, has_side_effects=True, vmem_limit_bytes=63 * 2**20
         ),
         name="layer",
-    )(x_in, z_in, wq, wkv, wo, wg, wu, wd, small, cosine, sine, row_range)
+    )(x_in, z_in, wq, wk, wv, wo, wg, wu, wd, small, sizes, lengths)
 
 class Group:
     def __init__(self):
@@ -1731,15 +1863,6 @@
 
     def partners(self):
         return [(self.mate, None)] + [(self.chip(i), None) for i in (1, 2, 3)]
-
-
-def row_layout(index, buckets, lengths):
-    ends = jnp.cumsum(buckets)
-    starts = ends - buckets
-    member = (index[:, None] >= starts[None, :]) & (index[:, None] < ends[None, :])
-    position = index - jnp.sum(jnp.where(member, starts[None, :], 0), axis=1)
-    limit = jnp.sum(jnp.where(member, lengths[None, :], 0), axis=1)
-    return (None, position, limit)
 
 
 def fast_local(
@@ -1780,38 +1903,22 @@
         ],
         axis=0,
     )
-    paired = jnp.concatenate(
-        [key_matrix[:, :128], value_matrix[:, :128], key_matrix[:, 128:], value_matrix[:, 128:]],
-        axis=1,
-    )
-
-    row_index = l * span + jnp.arange(span, dtype=jnp.int32)
-    layouts = [row_layout(row_index, bucket_sizes[b], true_lengths[b]) for b in range(batches)]
-    positions = jnp.concatenate([item[1] for item in layouts])
-    row_lo = jnp.stack([row_index - item[1] for item in layouts])
-    limits = jnp.stack([item[2] for item in layouts])
-    row_hi = jnp.minimum(row_index + 1, row_lo + limits)
-    cosine, sine = rope_tables(positions, HEAD_SIZE)
-    signed = sine * jnp.where(jnp.arange(HEAD_SIZE) < HEAD_SIZE // 2, -1.0, 1.0)
     x_split = inputs.reshape(batches, 4, 32, width)
     z_split = cotangent.reshape(batches, 4, 32, width)
-    cosine = cosine.reshape(batches, span, HEAD_SIZE)
-    signed = signed.reshape(batches, span, HEAD_SIZE)
-    row_range = jnp.where(jnp.arange(128) == 0, row_lo[:, :, None], row_hi[:, :, None])
-    own_out, own_grad, dq, dkv, do, d_gate, d_up, d_down, sums, late, unused, unused = layer(
+    own_out, own_grad, dq, dk, dv, do, d_gate, d_up, d_down, sums, late, unused, unused = layer(
         n,
         x_split,
         z_split,
         query_weight,
-        paired,
+        key_matrix,
+        value_matrix,
         output_weight,
         gate_weight,
         up_weight,
         down_weight,
         own_small,
-        cosine,
-        signed,
-        row_range,
+        bucket_sizes,
+        true_lengths,
     )
     return (
         own_out.reshape(batches, rows, width),
@@ -1821,8 +1928,8 @@
         sums[0, 1, :HEAD_SIZE],
         sums[0, 1, HEAD_SIZE:],
         dq.astype(F32),
-        jnp.concatenate([dkv[:, :128], dkv[:, 256:384]], axis=1).astype(F32),
-        jnp.concatenate([dkv[:, 128:256], dkv[:, 384:]], axis=1).astype(F32),
+        dk.astype(F32),
+        dv.astype(F32),
         sums[1, :4].T,
         do.astype(F32),
         d_gate.astype(F32),

time: 487 us -> 454 us (0.932)
  Pallas kernels: 445 us -> 423 us
  other arithmetic: 17.7 us -> 8.92 us
    pallas_call x1, Pallas kernels: 445 us -> 423 us  [layer(): pl.pallas_call(functools.partial(layer_kernel, n), out_shape=(bf(4, 4, 32...]
where the time goes in v6:
time: 454 us; the launch traced here: 445 us
  Pallas kernels  423 us (93%)
  local copies, waits for them, and re-layouts  12 us (3%)
  other arithmetic  8.92 us (2%)
    pallas_call x1, Pallas kernels, layer(): pl.pallas_call(functools.partial(layer_kernel, n), out_shape=(bf(4, 4, 32...  423 us

profile of v6, /device:TPU:0, one launch (start us, length us, event | category | flops | bytes accessed | tf_op | source)
XLA Modules:
  0.0 445.3 jit_solution(16123831147210249702)
XLA Ops:
  0.6 0.7 broadcast_in_dim.12
  1.3 0.7 broadcast_in_dim.13
  2.0 0.7 fusion.2
  2.7 1.9 concatenate.3.small
  4.6 423.2 %layer.1 = (bf16[4,4,32,2048]{3,2,1,0:T(8,128)(2,1)}, bf16[4,4,32,2048]{3,2,1,0:T(8,128)(2,1)}, bf16[256,512]{1,0:T(8,128)(2,1)}, bf16[256,256]{1,0:T(8,128)(2,1...) custom-call(bf16[4,4,32,2048]{3,2,1,0:T(8,128)(2,1)} %bitcast.19, ...), custom_call_target="tpu_custom_call" | custom-call | tf_op jit(solution)/shard_map/layer/pallas_call | solution.py:1743
  427.8 0.0 copy-start.3
  427.8 1.3 constant_dynamic-slice_fusion
  429.1 1.2 slice_bitcast_fusion.1
  430.3 1.3 slice_bitcast_fusion
  431.6 1.3 slice.12
  432.9 2.5 convert_element_type.27
  435.4 0.0 copy-done.3
  435.4 1.3 convert_element_type.28
  436.7 0.0 copy-done.2
  436.7 0.0 copy-start.1
  436.8 1.3 convert_element_type.29
  438.0 0.0 copy-done.5
  438.0 0.9 convert_element_type.23
  438.9 0.8 convert_element_type.26
  439.7 0.7 convert_element_type.24
  440.4 0.7 convert_element_type.25
  441.2 1.3 copy.32
  442.5 1.0 copy-done
  443.5 1.3 copy.33
  (12 shorter events, 0.0 us)
Async XLA Ops:
  427.8 7.6 %copy-start.3 = (bf16[256,1536]{1,0:T(8,128)(2,1)S(1)}, bf16[256,1536]{1,0:T(8,128)(2,1)}, u32[]{:S(2)}) copy-start(bf16[256,1536]{1,0:T(8,128)(2,1)} %get-tuple-element.34) | copy-start | bytes 2359300
  432.9 3.9 copy-start.2
  435.4 2.6 copy-start.5
  436.7 2.1 copy-start.4
  436.7 3.0 copy-start.7
  436.7 3.7 copy-start.6
  436.7 4.4 copy-start.1
  441.2 2.3 copy-start

commit v7 on v6

--- a/solution.py
+++ b/solution.py
@@ -1660,6 +1660,7 @@
     line.rs_near(0, 2)
     line.rs_far(1, 2)
     line.rs_far(2, 1)
+    line.rs_far(0, 1)
     late_c.wait()
     late[...] = late[...] + late_core[...]
     late_s = [
@@ -1675,6 +1676,8 @@
     sums[...] = sums[...] + sum_x[...]
     small_y.start()
     each(4, lambda m: home_on(1, m))
+    line.rs_near(1, 2)
+    line.rs_far(1, 1)
     for copy in late_s:
         copy.wait()
     late[...] = late_chip[0] + late_chip[1] + late_chip[2] + late_chip[3]
@@ -1693,11 +1696,8 @@
     for d in range(1, n):
         small_line(d).start()
     sum_l[l] = sums[:, pl.ds(2 * l, 2)]
-    line.rs_near(1, 2)
-    line.rs_far(0, 1)
     line.rs_final(2)
     send_home(2)
-    line.rs_far(1, 1)
     line.rs_final(0)
     send_home(0)
     for d in range(1, n):
@@ -1865,6 +1865,73 @@
         return [(self.mate, None)] + [(self.chip(i), None) for i in (1, 2, 3)]
 
 
+def outputs_kernel(count, *refs):
+    ins, small, outs = refs[:count], refs[count : count + 2], refs[count + 2 : 2 * count + 2]
+    attention, feedforward, query, key, heads = refs[2 * count + 2 : 2 * count + 7]
+    held = refs[2 * count + 7 : 3 * count + 7]
+    wide = refs[3 * count + 7 : 4 * count + 5]
+    in_sem, out_sem = refs[-2:]
+    reads = [
+        pltpu.make_async_copy(ins[i], held[i], in_sem.at[i]) for i in range(count)
+    ]
+    writes = [
+        pltpu.make_async_copy(held[i] if i < 2 else wide[i - 2], outs[i], out_sem.at[i])
+        for i in range(count)
+    ]
+    order = list(range(2, count)) + [0, 1]
+    for i in order:
+        reads[i].start()
+    s = lax.axis_index("seq")
+    sums, late = small
+    row = lax.broadcasted_iota(jnp.int32, late.shape, 0)
+    attention[...] = jnp.sum(jnp.where(row == s, late[...], 0.0), axis=0, keepdims=True)
+    feedforward[...] = sums[0, 0:1]
+    query[...] = sums[0, 1:2, :HEAD_SIZE]
+    key[...] = sums[0, 1:2, HEAD_SIZE:]
+    heads[...] = sums[1].T[:, :4]
+    for i in order:
+        reads[i].wait()
+        if i >= 2:
+            src, dst = held[i], wide[i - 2]
+
+            def widen(part, src=src, dst=dst):
+                at = pl.ds(pl.multiple_of(part * 64, 64), 64)
+                dst[at] = src[at].astype(F32)
+
+            each(src.shape[0] // 64, widen)
+        writes[i].start()
+    for copy in writes:
+        copy.wait()
+
+
+def outputs(arrays, sums, late):
+    count = len(arrays)
+    f32 = lambda *shape: jax.ShapeDtypeStruct(shape, F32)
+    kept = [jax.ShapeDtypeStruct(a.shape, a.dtype) for a in arrays[:2]]
+    return pl.pallas_call(
+        functools.partial(outputs_kernel, count),
+        out_shape=(
+            *kept,
+            *[f32(*a.shape) for a in arrays[2:]],
+            f32(1, 256),
+            f32(1, 256),
+            f32(1, HEAD_SIZE),
+            f32(1, HEAD_SIZE),
+            f32(256, 4),
+        ),
+        in_specs=[ANY] * count + [VM] * 2,
+        out_specs=(ANY,) * count + (VM,) * 5,
+        scratch_shapes=[
+            *[pltpu.VMEM(a.shape, a.dtype) for a in arrays],
+            *[pltpu.VMEM(a.shape, F32) for a in arrays[2:]],
+            DMA((count,)),
+            DMA((count,)),
+        ],
+        compiler_params=pltpu.CompilerParams(vmem_limit_bytes=63 * 2**20),
+        name="outputs",
+    )(*arrays, sums, late)
+
+
 def fast_local(
     inputs,
     cotangent,
@@ -1920,21 +1987,36 @@
         bucket_sizes,
         true_lengths,
     )
+    res, grad, dq, dk, dv, do, dg, du, dd, attention, feedforward, query, key, heads = outputs(
+        [
+            own_out.reshape(batches, rows, width),
+            own_grad.reshape(batches, rows, width),
+            dq,
+            dk,
+            dv,
+            do,
+            d_gate,
+            d_up,
+            d_down,
+        ],
+        sums,
+        late,
+    )
     return (
-        own_out.reshape(batches, rows, width),
-        own_grad.reshape(batches, rows, width),
-        lax.dynamic_index_in_dim(late, seq, 0, keepdims=False),
-        sums[0, 0],
-        sums[0, 1, :HEAD_SIZE],
-        sums[0, 1, HEAD_SIZE:],
-        dq.astype(F32),
-        dk.astype(F32),
-        dv.astype(F32),
-        sums[1, :4].T,
-        do.astype(F32),
-        d_gate.astype(F32),
-        d_up.astype(F32),
-        d_down.astype(F32),
+        res,
+        grad,
+        attention[0],
+        feedforward[0],
+        query[0],
+        key[0],
+        dq,
+        dk,
+        dv,
+        heads,
+        do,
+        dg,
+        du,
+        dd,
     )
 
 

time: 454 us -> 441 us (0.971)
  other arithmetic: 8.92 us -> 0.68 us
  local copies, waits for them, and re-layouts: 12 us -> 4.81 us
    pallas_call x0 -> x1, Pallas kernels: none -> 9.04 us  [outputs(): pl.pallas_call(functools.partial(outputs_kernel, count), out_shape=(*kept...]
    convert_element_type x7 -> x0, other arithmetic: 8.24 us -> none  [the longest x1 2.53 us: fast_local(): d_gate.astype(F32)]
    pallas_call x1, Pallas kernels: 423 us -> 417 us  [layer(): pl.pallas_call(functools.partial(layer_kernel, n), out_shape=(bf(4, 4, 32...]
where the time goes in v7:
time: 441 us; the launch traced here: 432 us
  Pallas kernels  426 us (97%)
  local copies, waits for them, and re-layouts  4.81 us (1%)
    pallas_call x1, Pallas kernels, layer(): pl.pallas_call(functools.partial(layer_kernel, n), out_shape=(bf(4, 4, 32...  417 us
    pallas_call x1, Pallas kernels, outputs(): pl.pallas_call(functools.partial(outputs_kernel, count), out_shape=(*kept...  9.04 us

profile of v7, /device:TPU:0, one launch (start us, length us, event | category | flops | bytes accessed | tf_op | source)
XLA Modules:
  0.0 432.5 jit_solution(9994394857512968827)
XLA Ops:
  0.6 0.7 broadcast_in_dim.12
  1.3 0.7 broadcast_in_dim.13
  2.0 0.7 fusion.2
  2.7 1.9 concatenate.3.small
  4.6 416.9 %layer.1 = (bf16[4,4,32,2048]{3,2,1,0:T(8,128)(2,1)}, bf16[4,4,32,2048]{3,2,1,0:T(8,128)(2,1)}, bf16[256,512]{1,0:T(8,128)(2,1)}, bf16[256,256]{1,0:T(8,128)(2,1...) custom-call(bf16[4,4,32,2048]{3,2,1,0:T(8,128)(2,1)} %bitcast.11, ...), custom_call_target="tpu_custom_call" | custom-call | tf_op jit(solution)/shard_map/layer/pallas_call | solution.py:1743
  421.4 9.0 %outputs.1 = (bf16[4,128,2048]{2,1,0:T(8,128)(2,1)}, bf16[4,128,2048]{2,1,0:T(8,128)(2,1)}, f32[256,512]{1,0:T(8,128)}, f32[256,256]{1,0:T(8,128)}, f32[256,256]...) custom-call(bf16[4,128,2048]{2,1,0:T(8,128)(2,1)} %bitcast.13, ...), custom_call_target="tpu_custom_call" | custom-call | tf_op jit(solution)/shard_map/outputs/pallas_call | solution.py:1911
  430.5 1.6 copy.30
  (2 shorter events, 0.0 us)

commit v8 on v7

--- a/solution.py
+++ b/solution.py
@@ -629,9 +629,9 @@
             total = self.g[seat, 2 * o + h].astype(F32) + self.land[berth, 2 * slot + h].astype(F32)
             self.g[seat, 2 * o + h] = total.astype(BF)
 
-    def rs_fire(self, item):
+    def rs_fire(self, item, first=0, last=3):
         l, n = self.l, self.n
-        for o in range(n - 1, 0, -1):
+        for o in range(n - 1 - first, n - 1 - last, -1):
             pl.when(l == 0)(lambda o=o: self._rs(item, 1, o).start())
             pl.when(l == n - 1)(lambda o=o: self._rs(item, 0, n - 1 - o).start())
 
@@ -1365,7 +1365,7 @@
     free_take(1)
     line.rs_fire(10)
     free_take(2)
-    line.rs_fire(11)
+    line.rs_fire(11, 0, 2)
     gain_sum[...] = jnp.zeros_like(gain_sum)
     head_sum[...] = jnp.zeros_like(head_sum)
     each(4, lambda m: to_chips(m, 1))
@@ -1496,14 +1496,15 @@
 
     pass_on(0, 1)
     for m in range(4):
+        attend_back(m)
+        kv_fire(m)
+        if m == 0:
+            line.rs_near(10, 2)
         if m < 3:
             pass_on(m + 1, 1)
         if m == 2:
             each(4, lambda m: mate_copy(m, 2).start())
-        attend_back(m)
-        kv_fire(m)
-        if m == 0:
-            line.rs_near(10, 2)
+    line.rs_fire(11, 2, 3)
     each(4, lambda m: to_chips(m, 2))
     final_in(8)
     far(8)
@@ -1518,7 +1519,9 @@
         way, item, kind, j = backward(item)
         way.end(item, kind, j)
         line.rs_end(item)
+    kv_step(0)
     each(4, query_back)
+    kv_step(1)
     normed_back_copy.wait()
 
     def output_weights(s, unused):
@@ -1533,10 +1536,10 @@
 
     lax.fori_loop(0, blocks, output_weights, 0)
     line.rs_fire(2)
+    kv_step(2)
     lax.fori_loop(0, blocks, query_weights, 0)
     line.rs_fire(0)
-    for m in range(4):
-        kv_step(m)
+    kv_step(3)
     line.rs_near(11, 2)
     line.rs_near(2, 1)
     line.rs_near(0, 1)

time: 441 us -> 440 us (level)
  no operation moved by 1% of the time
where the time goes in v8:
time: 440 us; the launch traced here: 432 us
  Pallas kernels  425 us (97%)
  local copies, waits for them, and re-layouts  4.81 us (1%)
    pallas_call x1, Pallas kernels, layer(): pl.pallas_call(functools.partial(layer_kernel, n), out_shape=(bf(4, 4, 32...  416 us
    pallas_call x1, Pallas kernels, outputs(): pl.pallas_call(functools.partial(outputs_kernel, count), out_shape=(*kept...  9.04 us

profile of v8, /device:TPU:0, one launch (start us, length us, event | category | flops | bytes accessed | tf_op | source)
XLA Modules:
  0.0 431.5 jit_solution(13416563653874707226)
XLA Ops:
  0.6 0.7 broadcast_in_dim.12
  1.3 0.7 broadcast_in_dim.13
  2.0 0.7 fusion.2
  2.7 1.9 concatenate.3.small
  4.6 415.9 %layer.1 = (bf16[4,4,32,2048]{3,2,1,0:T(8,128)(2,1)}, bf16[4,4,32,2048]{3,2,1,0:T(8,128)(2,1)}, bf16[256,512]{1,0:T(8,128)(2,1)}, bf16[256,256]{1,0:T(8,128)(2,1...) custom-call(bf16[4,4,32,2048]{3,2,1,0:T(8,128)(2,1)} %bitcast.11, ...), custom_call_target="tpu_custom_call" | custom-call | tf_op jit(solution)/shard_map/layer/pallas_call | solution.py:1746
  420.5 9.0 %outputs.1 = (bf16[4,128,2048]{2,1,0:T(8,128)(2,1)}, bf16[4,128,2048]{2,1,0:T(8,128)(2,1)}, f32[256,512]{1,0:T(8,128)}, f32[256,256]{1,0:T(8,128)}, f32[256,256]...) custom-call(bf16[4,128,2048]{2,1,0:T(8,128)(2,1)} %bitcast.13, ...), custom_call_target="tpu_custom_call" | custom-call | tf_op jit(solution)/shard_map/outputs/pallas_call | solution.py:1914
  429.5 1.6 copy.30
  (2 shorter events, 0.0 us)
